TPU v7x, 256 devices: a whole 4x4x8 slice. The times are simulated.
256 devices in a mesh: expert: 32 (over z, y), loop: 8 (over x, core).
Axes of the slice: x: 4, y: 4, z: 8, core: 2. Of those that a mesh axis runs over, the one named last changes fastest.
Arguments:
- tokens: bfloat16 [4096, 5120], P('expert', 'loop'), may hold values from -6 to 6
- routes: int32 [4096, 6], P('expert'), may hold values from 0 to 31, all different within a row; in each aligned block of 128 rows (0 to 127, 128 to 255, ...) at most 32 rows name the same one
- route_weights: float32 [4096, 6], P('expert'), may hold values from 0.1 to 1
- gate_w: bfloat16 [32, 1536, 5120], P('expert', 'loop'), may hold values from -0.078125 to 0.078125
- up_w: bfloat16 [32, 1536, 5120], P('expert', 'loop'), may hold values from -0.078125 to 0.078125
- down_w: bfloat16 [32, 1536, 5120], P('expert', 'loop'), may hold values from -0.15625 to 0.15625
- shared_gate: bfloat16 [1536, 5120], P('loop'), may hold values from -0.078125 to 0.078125
- shared_up: bfloat16 [1536, 5120], P('loop'), may hold values from -0.078125 to 0.078125
- shared_down: bfloat16 [1536, 5120], P('loop'), may hold values from -0.15625 to 0.15625
Outputs:
- moe_out: bfloat16 [4096, 5120], P('expert', 'loop')
Inputs may be any that keep to these rules, and one draw needn't show every extreme that they name: `routes`: within the rows of one device (aligned blocks of 128 rows) no expert is named by more than 32 rows; the 6 experts of a row differ.
All inputs are finite; a program needn't handle non-finite values.
Results may differ from a plain program's by a relative error of at most 0.02.
Values may be sent and summed in bfloat16 or wider, within the bound.
No kernel may reach another device: no remote copies, remote signals or barrier semaphores. Data moves between devices by JAX's collectives and lax.ppermute only.
A program may use at most 128 MiB of HBM per device.

v0:
```python
import jax
import jax.numpy as jnp
from jax import lax
from jax.sharding import PartitionSpec as P


def project_rows(rows, weight):
    return lax.dot_general(
        rows, weight, (((1,), (1,)), ((), ())), preferred_element_type=jnp.float32
    )


def local(tokens, routes, route_weights, gate_w, up_w, down_w, shared_gate, shared_up, shared_down):
    tok_rows = tokens.shape[0]
    top_count = routes.shape[1]
    groups = lax.axis_size("expert")
    capacity = tok_rows * top_count * 4 // (3 * groups)
    slot_total = groups * capacity
    gathered = lax.all_gather(tokens, "loop", axis=1, tiled=True)
    flat_routes = routes.reshape(-1)
    onehot = (flat_routes[:, None] == jnp.arange(groups, dtype=jnp.int32)[None, :]).astype(
        jnp.int32
    )
    before = jnp.cumsum(onehot, axis=0) - onehot
    position = jnp.sum(before * onehot, axis=1)
    slot_index = (flat_routes * capacity + position).reshape(tok_rows, top_count)
    slot_ids = jnp.arange(slot_total, dtype=jnp.int32)
    matches = slot_ids[:, None, None] == slot_index[None, :, :]
    selector = jnp.sum(matches.astype(jnp.float32), axis=2).astype(jnp.bfloat16)
    combine_w = jnp.sum(jnp.where(matches, route_weights[None, :, :], 0.0), axis=2)
    combine_high = combine_w.astype(jnp.bfloat16)
    combine_low = (combine_w - combine_high.astype(jnp.float32)).astype(jnp.bfloat16)
    shared_gate_act = project_rows(gathered, shared_gate)
    shared_up_act = project_rows(gathered, shared_up)
    shared_hidden = (jax.nn.silu(shared_gate_act) * shared_up_act).astype(jnp.bfloat16)
    w_gate = gate_w[0]
    w_up = up_w[0]
    w_down = down_w[0]
    outgoing = jnp.dot(selector, gathered, preferred_element_type=jnp.float32).astype(jnp.bfloat16)
    incoming = lax.all_to_all(outgoing, "expert", split_axis=0, concat_axis=0, tiled=True)
    gate_act = project_rows(incoming, w_gate)
    up_act = project_rows(incoming, w_up)
    hidden = (jax.nn.silu(gate_act) * up_act).astype(jnp.bfloat16)
    routed_term = jnp.einsum("fc,rf->cr", w_down, hidden, preferred_element_type=jnp.float32)
    shared_term = jnp.einsum(
        "fc,rf->cr", shared_down, shared_hidden, preferred_element_type=jnp.float32
    )
    summed = lax.psum_scatter(
        jnp.concatenate([routed_term, shared_term], axis=1).astype(jnp.bfloat16),
        "loop",
        scatter_dimension=0,
        tiled=True,
    ).astype(jnp.float32)
    expert_result = summed[:, :slot_total].astype(jnp.bfloat16)
    shared_part = summed[:, slot_total:]
    returned = lax.all_to_all(expert_result, "expert", split_axis=1, concat_axis=1, tiled=True)
    routed_part = jnp.dot(returned, combine_high, preferred_element_type=jnp.float32) + jnp.dot(
        returned, combine_low, preferred_element_type=jnp.float32
    )
    return (routed_part + shared_part).T.astype(jnp.bfloat16)


def solution(mesh):
    placed = (
        P("expert", "loop"),
        P("expert", None),
        P("expert", None),
        P("expert", "loop", None),
        P("expert", "loop", None),
        P("expert", "loop", None),
        P("loop", None),
        P("loop", None),
        P("loop", None),
    )
    return jax.shard_map(
        local, mesh=mesh, in_specs=placed, out_specs=P("expert", "loop"), check_vma=False
    )
```

profile of v0, /device:TPU:1, one launch (start us, length us, event | category | flops | bytes accessed | tf_op | source)
XLA Modules:
  0.0 480.3 jit_solution(17969575525954098838)
XLA Ops:
  6.5 0.0 copy-start
  6.5 0.0 all-gather.2.cloned.1.call-start
  6.5 0.7 all-gather.2.cloned.1.call-update
  7.3 0.8 copy.38
  8.1 0.1 eq.43
  8.2 0.1 eq.39
  8.3 1.7 reduce-window.6
  10.1 0.3 slice_reduce_fusion
  10.4 0.1 fusion.30
  10.5 0.1 reduce_sum.30
  10.6 0.1 copy.41
  10.7 0.7 multiply_add_fusion
  11.4 2.2 select_reduce_fusion
  13.6 26.2 %all-gather.2.cloned.1.call-done = bf16[128,5120]{1,0:T(8,128)(2,1)} async-done(((bf16[128,640]{1,0:T(8,128)(2,1)}), bf16[128,5120]{1,0:T(8,128)(2,1)}) %all-gather.2.cloned.1.call-update) | async-done | bytes 1310736 | tf_op jit(solution)/shard_map/all_gather | solution.py:19
  39.8 6.7 %convolution_convert_fusion = bf16[1024,5120]{1,0:T(8,128)(2,1)} fusion(bf16[128,5120]{1,0:T(8,128)(2,1)} %all-gather.2.cloned.1.call-done, bf16[1024,128]{1,0:T(8,128)(2,1)S(1)} %get-tuple-element.6), kind=kOutput, calls=%fused_computation.2 | convolution fusion | flops 1347420160 | bytes 12058624 | tf_op jit(solution)/shard_map/dot_general | solution.py:39
  46.4 0.0 copy-start.2
  46.4 9.8 %all-to-all-start = ((bf16[32,32,5120]{2,1,0:T(8,128)(2,1)}), bf16[32,32,5120]{2,1,0:T(8,128)(2,1)}, u32[]{:S(2)}, u32[]{:S(2)}) async-start(bf16[32,32,5120]{2,1,0:T(8,128)(2,1)} %bitcast.57), calls=%async_computation | async-start | bytes 20971520 | tf_op jit(solution)/shard_map/all_to_all | solution.py:40
  56.2 0.2 reduce-scatter.4.cloned.1.call-start
  56.5 0.0 copy-done.2
  56.5 2.2 fusion.40
  58.7 5.1 %fusion = bf16[5120,128]{0,1:T(8,128)(2,1)} fusion(bf16[192,5120]{1,0:T(8,128)(2,1)} %param.17, bf16[128,5120]{1,0:T(8,128)(2,1)S(1)} %copy-done.2, bf16[192,5120]{1,0:T(8,128)(2,1)} %param.16, f32[128,192]{0,1:T(8,128)S(1)} %fusion.40), kind=kOutput, calls=%fused_computation.4 | convolution fusion | flops 504119296 | bytes 6651904 | tf_op jit(solution)/shard_map/fc,rf->cr/dot_general | solution.py:45
  63.8 227.0 %all-to-all-done = bf16[32,32,5120]{2,1,0:T(8,128)(2,1)} async-done(((bf16[32,32,5120]{2,1,0:T(8,128)(2,1)}), bf16[32,32,5120]{2,1,0:T(8,128)(2,1)}, u32[]{:S(2)}, u32[]{:S(2)}) %all-to-all-start) | async-done | bytes 10485792 | tf_op jit(solution)/shard_map/all_to_all | solution.py:40
  290.8 9.0 %fusion.4 = f32[1024,192]{0,1:T(8,128)} fusion(bf16[1024,5120]{1,0:T(8,128)(2,1)} %bitcast.2, bf16[1,192,5120]{2,1,0:T(8,128)(2,1)} %param.12), kind=kOutput, calls=%fused_computation.11 | convolution fusion | flops 2013265920 | bytes 13238272 | tf_op jit(solution)/shard_map/dot_general | solution.py:8
  299.8 0.0 copy-done
  299.8 0.0 copy-start.3
  299.8 17.3 %convert_bitcast_fusion = bf16[5120,1024]{0,1:T(8,128)(2,1)} fusion(bf16[1,192,5120]{2,1,0:T(8,128)(2,1)S(1)} %copy-done, bf16[1024,5120]{1,0:T(8,128)(2,1)} %bitcast.2, bf16[1,192,5120]{2,1,0:T(8,128)(2,1)} %param.13, f32[1024,192]{0,1:T(8,128)} %fusion.4), kind=kOutput, calls=%fused_computation.1 | convolution fusion | flops 4032954368 | bytes 25690112 | tf_op jit(solution)/shard_map/fc,rf->cr/dot_general | solution.py:44
  317.1 0.0 copy-done.3
  317.1 12.7 %pad_maximum_fusion = bf16[5120,1152]{0,1:T(8,128)(2,1)} fusion(bf16[5120,128]{0,1:T(8,128)(2,1)S(1)} %copy-done.3, bf16[5120,1024]{0,1:T(8,128)(2,1)} %convert_bitcast_fusion), kind=kLoop, calls=%fused_computation | loop fusion | flops 23592960 | bytes 23592960 | tf_op jit(solution)/shard_map/concatenate | solution.py:49
  329.8 15.3 %copy.44 = bf16[5120,1152]{1,0:T(8,128)(2,1)} copy(bf16[5120,1152]{0,1:T(8,128)(2,1)} %pad_maximum_fusion) | data formatting | bytes 23592960
  345.1 0.0 reduce-scatter.4.cloned.1.call-update
  345.1 81.4 %reduce-scatter.4.cloned.1.call-done = bf16[640,1152]{1,0:T(8,128)(2,1)} async-done(((bf16[5120,1152]{1,0:T(8,128)(2,1)}), bf16[640,1152]{1,0:T(8,128)(2,1)}) %reduce-scatter.4.cloned.1.call-update) | async-done | bytes 1474576 | tf_op jit(solution)/shard_map/reduce_scatter | solution.py:48
  426.6 0.0 slice-start
  426.6 1.3 slice-done
  427.9 0.7 copy.46
  428.6 0.0 copy-start.5
  428.6 0.0 copy-start.4
  428.6 43.0 %all_to_all.24 = bf16[640,32,32]{0,2,1:T(8,128)(2,1)S(1)} all-to-all(bf16[640,32,32]{0,2,1:T(8,128)(2,1)S(1)} %bitcast.60), channel_id=1, replica_groups=mesh['expert'=32,'loop'=8] {'expert'}, dimensions={1} | all-to-all | bytes 2621440 | tf_op jit(solution)/shard_map/all_to_all | solution.py:56
  471.6 0.0 copy-start.1
  471.6 0.0 copy-done.5
  471.6 0.5 fusion.26
  472.1 0.0 copy-done.4
  472.1 0.5 fusion.16
  472.7 0.8 copy.43
  473.5 0.0 copy-done.1
  (2 shorter events, 0.0 us)
Async XLA Ops:
  6.5 293.2 %copy-start = (bf16[1,192,5120]{2,1,0:T(8,128)(2,1)S(1)}, bf16[1,192,5120]{2,1,0:T(8,128)(2,1)}, u32[]{:S(2)}) copy-start(bf16[1,192,5120]{2,1,0:T(8,128)(2,1)} %param.14) | copy-start | bytes 5898244
  6.5 33.2 %all-gather.2.cloned.1.call-start = ((), (), s32[]{:S(2)}) async-start(), calls=%async_computation.3 | async-start | bytes 1474560 | tf_op jit(solution)/shard_map/all_gather | solution.py:19
  46.4 10.1 %copy-start.2 = (bf16[128,5120]{1,0:T(8,128)(2,1)S(1)}, bf16[128,5120]{1,0:T(8,128)(2,1)}, u32[]{:S(2)}) copy-start(bf16[128,5120]{1,0:T(8,128)(2,1)} %all-gather.2.cloned.1.call-done) | copy-start | bytes 3932164
  46.4 244.3 %all-to-all-start = ((bf16[32,32,5120]{2,1,0:T(8,128)(2,1)}), bf16[32,32,5120]{2,1,0:T(8,128)(2,1)}, u32[]{:S(2)}, u32[]{:S(2)}) async-start(bf16[32,32,5120]{2,1,0:T(8,128)(2,1)} %bitcast.57), calls=%async_computation | async-start | bytes 20971520 | tf_op jit(solution)/shard_map/all_to_all | solution.py:40
  56.2 370.3 %reduce-scatter.4.cloned.1.call-start = ((), (), s32[]{:S(2)}) async-start(), calls=%async_computation.4 | async-start | bytes 13271040 | tf_op jit(solution)/shard_map/reduce_scatter | solution.py:48
  299.8 17.3 %copy-start.3 = (bf16[5120,128]{0,1:T(8,128)(2,1)S(1)}, bf16[5120,128]{0,1:T(8,128)(2,1)}, u32[]{:S(2)}) copy-start(bf16[5120,128]{0,1:T(8,128)(2,1)} %fusion) | copy-start | bytes 3932164
  426.6 1.3 slice-start
  428.6 43.0 %copy-start.5 = (f32[1024,128]{1,0:T(8,128)S(1)}, f32[1024,128]{1,0:T(8,128)}, u32[]{:S(2)}) copy-start(f32[1024,128]{1,0:T(8,128)} %get-tuple-element.5) | copy-start | bytes 1572868
  428.6 43.5 %copy-start.4 = (bf16[640,1152]{1,0:T(8,128)(2,1)S(1)}, bf16[640,1152]{1,0:T(8,128)(2,1)}, u32[]{:S(2)}) copy-start(bf16[640,1152]{1,0:T(8,128)(2,1)} %reduce-scatter.4.cloned.1.call-done) | copy-start | bytes 4423684
  471.6 1.9 copy-start.1
Sparse Core Ops, SparseCore 0:
  9.2 30.5 all-gather.1
  345.3 81.2 reduce-scatter.3
where the time goes:
time: 482 us; the launch traced here: 480 us
  waiting for transfers between devices  335 us (70%)
  blocking collectives  43 us (9%)
  matrix products  41.4 us (9%)
  local copies, waits for them, and re-layouts  19.6 us (4%)
  other arithmetic  17.5 us (4%)
  between operations  13.5 us (3%)
  starting transfers between devices  10 us (2%)
    all_to_all x1, waiting for transfers between devices, local(): lax.all_to_all(outgoing, 'expert', split_axis=0, concat_axis=0, tiled=True)  227 us
    reduce_scatter x1, waiting for transfers between devices, local(): lax.psum_scatter(jnp.concatenate([routed_term, shared_term], axis=1).asty...  81.4 us
    all_to_all x1, blocking collectives, local(): lax.all_to_all(expert_result, 'expert', split_axis=1, concat_axis=1, tile...  43 us
    all_gather x1, waiting for transfers between devices, local(): gathered = lax.all_gather(tokens, 'loop', axis=1, tiled=True)  26.2 us
    dot_general x1, matrix products, local(): jnp.einsum('fc,rf->cr', w_down, hidden, preferred_element_type=jnp.float32)  17.3 us
    unnamed x15, local copies, waits for them, and re-layouts  16.8 us
    concatenate x1, other arithmetic, local(): jnp.concatenate([routed_term, shared_term], axis=1).astype(jnp.bfloat16)  12.7 us
    dot_general x2, matrix products, project_rows(): lax.dot_general(rows, weight, (((1,), (1,)), ((), ())), preferred_element...  11.2 us
  transfers between devices with their start and end apart: 3, of which 3 were waited for; matrix products, arithmetic and copies ran while one was open for 3% of the time, Pallas kernels for 0%

commit v1 on v0

v1 whole, which is shorter than its diff:
```python
import jax
import jax.numpy as jnp
from jax import lax
from jax.sharding import PartitionSpec as P

CHIPS = 4
BF16 = jnp.bfloat16
F32 = jnp.float32


def swap_cores(value):
    return lax.ppermute(value, "loop", [(i, i ^ 1) for i in range(2 * CHIPS)])


def shift_chips(value, step):
    pairs = [
        (2 * chip + core, 2 * ((chip + step) % CHIPS) + core)
        for chip in range(CHIPS)
        for core in range(2)
    ]
    return lax.ppermute(value, "loop", pairs)


def gather_chips(block):
    half = block.shape[0] // 2
    first, second = block[:half], block[half:]
    first_left, first_right = shift_chips(first, 1), shift_chips(first, -1)
    second_left, second_right = shift_chips(second, 1), shift_chips(second, -1)
    first_far, second_far = shift_chips(first_left, 1), shift_chips(second_right, -1)
    return (
        [first, first_left, first_far, first_right],
        [second, second_left, second_far, second_right],
    )


def project_rows(rows, weight):
    return lax.dot_general(rows, weight, (((1,), (1,)), ((), ())), preferred_element_type=F32)


def dot(left, right):
    return jnp.dot(left, right, preferred_element_type=F32)


def pick(chip, step, array, width):
    return lax.dynamic_slice_in_dim(array, ((chip - step) & (CHIPS - 1)) * width, width, axis=1)


def hidden_of(blocks, gates, ups, chip):
    width = blocks[0].shape[1]
    out = []
    for gate, up in zip(gates, ups):
        gate_act = sum(project_rows(b, pick(chip, k, gate, width)) for k, b in enumerate(blocks))
        up_act = sum(project_rows(b, pick(chip, k, up, width)) for k, b in enumerate(blocks))
        out.append((jax.nn.silu(gate_act) * up_act).astype(BF16))
    return jnp.concatenate(out, axis=1)


def local(tokens, routes, route_weights, gate_w, up_w, down_w, shared_gate, shared_up, shared_down):
    tok_rows, width = tokens.shape
    experts = lax.axis_size("expert")
    half_cap = tok_rows * routes.shape[1] * 4 // (3 * experts) // 2
    place = lax.axis_index("loop")
    chip, core = place >> 1, place & 1
    first_core = core == 0

    def both(own):
        other = swap_cores(own)
        return jnp.where(
            first_core,
            jnp.concatenate([own, other], axis=1),
            jnp.concatenate([other, own], axis=1),
        )

    chip_tokens = both(tokens)
    chip_width = 2 * width

    own_down = down_w[0]
    down_own = [pick(chip, 0, own_down, chip_width)] + [
        shift_chips(pick(chip, -k, own_down, chip_width), k) for k in range(1, CHIPS)
    ]
    down_other = [swap_cores(part) for part in down_own]
    down_all = jnp.concatenate([p for pair in zip(down_own, down_other) for p in pair], axis=0)
    gates = [gate_w[0], swap_cores(gate_w[0])]
    ups = [up_w[0], swap_cores(up_w[0])]
    shared_gates = [shared_gate, swap_cores(shared_gate)]
    shared_ups = [shared_up, swap_cores(shared_up)]
    shared_downs = [shared_down, swap_cores(shared_down)]

    ids = jnp.arange(experts, dtype=jnp.int32)
    equal = routes.T[:, None, :] == ids[None, :, None]
    member = jnp.any(equal, axis=0)
    weight = jnp.sum(jnp.where(equal, route_weights.T[:, None, :], 0.0), axis=0)
    row = lax.broadcasted_iota(jnp.int32, (tok_rows, tok_rows), 0)
    col = lax.broadcasted_iota(jnp.int32, (tok_rows, tok_rows), 1)
    before = dot(member.astype(BF16), (row < col).astype(BF16)).astype(jnp.int32)
    slots = jnp.arange(half_cap, dtype=jnp.int32) + core * half_cap
    hit = member[:, None, :] & (before[:, None, :] == slots[None, :, None])
    selector = hit.astype(BF16).reshape(experts * half_cap, tok_rows)
    combine = jnp.where(hit, weight[:, None, :], 0.0).reshape(experts * half_cap, tok_rows)
    combine_high = combine.astype(BF16)
    combine_low = (combine - combine_high.astype(F32)).astype(BF16)

    outgoing = dot(selector, chip_tokens).astype(BF16)
    outgoing = outgoing.reshape(experts, half_cap, chip_width)
    incoming = lax.all_to_all(outgoing, "expert", split_axis=0, concat_axis=0, tiled=True)
    rows = incoming.reshape(experts * half_cap, chip_width)

    half_tok = tok_rows // 2
    my_tokens = lax.dynamic_slice_in_dim(chip_tokens, core * half_tok, half_tok, axis=0)
    shared_blocks = [my_tokens] + [shift_chips(my_tokens, k) for k in range(1, CHIPS)]
    shared_hidden = hidden_of(shared_blocks, shared_gates, shared_ups, chip)
    unit = shared_down.shape[0]
    shared_part = (
        dot(shared_hidden[:, :unit], shared_downs[0]) + dot(shared_hidden[:, unit:], shared_downs[1])
    ).astype(BF16)
    shared_sum = pick(chip, 0, shared_part, chip_width).astype(F32)
    for k in range(1, CHIPS):
        shared_sum = shared_sum + shift_chips(
            pick(chip, -k, shared_part, chip_width), k
        ).astype(F32)

    halves = gather_chips(rows)
    results = []
    for blocks in halves:
        hidden = hidden_of(blocks, gates, ups, chip)
        hiddens = [hidden] + [shift_chips(hidden, k) for k in range(1, CHIPS)]
        results.append(dot(jnp.concatenate(hiddens, axis=1), down_all).astype(BF16))
    result = jnp.concatenate(results, axis=0).reshape(experts, half_cap, chip_width)
    returned = lax.all_to_all(result, "expert", split_axis=0, concat_axis=0, tiled=True)
    returned = returned.reshape(experts * half_cap, chip_width)
    contract = (((0,), (0,)), ((), ()))
    routed = lax.dot_general(combine_high, returned, contract, preferred_element_type=F32)
    routed = routed + lax.dot_general(combine_low, returned, contract, preferred_element_type=F32)
    zeros = jnp.zeros((half_tok, chip_width), F32)
    placed = jnp.where(
        first_core,
        jnp.concatenate([shared_sum, zeros], axis=0),
        jnp.concatenate([zeros, shared_sum], axis=0),
    )
    total = routed + placed
    mine = lax.dynamic_slice_in_dim(total, core * width, width, axis=1)
    theirs = lax.dynamic_slice_in_dim(total, (1 - core) * width, width, axis=1)
    return (mine + swap_cores(theirs)).astype(BF16)


def solution(mesh):
    placed = (
        P("expert", "loop"),
        P("expert", None),
        P("expert", None),
        P("expert", "loop", None),
        P("expert", "loop", None),
        P("expert", "loop", None),
        P("loop", None),
        P("loop", None),
        P("loop", None),
    )
    return jax.shard_map(
        local, mesh=mesh, in_specs=placed, out_specs=P("expert", "loop"), check_vma=False
    )
```

time: 482 us -> 216 us (0.45)
  waiting for transfers between devices: 335 us -> 71.8 us
  starting transfers between devices: 10 us -> 55.4 us
  blocking collectives: 43 us -> 0 us
  matrix products: 41.4 us -> 66.4 us
  other arithmetic: 17.5 us -> 3 us
  between operations: 13.5 us -> 0.56 us
    all_to_all x1, waiting for transfers between devices: 227 us -> 0.01 us  [local(): lax.all_to_all(outgoing, 'expert', split_axis=0, concat_axis=0, tiled=True)]
    reduce_scatter x1 -> x0, waiting for transfers between devices: 81.4 us -> none  [local(): lax.psum_scatter(jnp.concatenate([routed_term, shared_term], axis=1).asty...]
    ppermute x0 -> x32, waiting for transfers between devices: none -> 63.9 us  [the longest x21 62.6 us: shift_chips(): return lax.ppermute(value, 'loop', pairs)]
    dot_general x2 -> x46, matrix products: 11.2 us -> 56 us  [project_rows(): lax.dot_general(rows, weight, (((1,), (1,)), ((), ())), preferred_element...]
    all_to_all x1 -> x0, blocking collectives: 43 us -> none  [local(): lax.all_to_all(expert_result, 'expert', split_axis=1, concat_axis=1, tile...]
    ppermute x0 -> x32, starting transfers between devices: none -> 34.6 us  [the longest x21 21.5 us: shift_chips(): return lax.ppermute(value, 'loop', pairs)]
    all_gather x1 -> x0, waiting for transfers between devices: 26.2 us -> none  [local(): gathered = lax.all_gather(tokens, 'loop', axis=1, tiled=True)]
    dot_general x5 -> x8, matrix products: 30.2 us -> 10.4 us  [the longest x6 9.5 us: dot(): return jnp.dot(left, right, preferred_element_type=F32)]
  transfers between devices with their start and end apart: 3 -> 34, of which waited for: 3 -> 13; matrix products, arithmetic and copies ran while one was open for 3% -> 39% of each run, Pallas kernels for 0% -> 0%
where the time goes in v1:
time: 216 us; the launch traced here: 213 us
  waiting for transfers between devices  71.8 us (33%)
  matrix products  66.4 us (31%)
  starting transfers between devices  55.4 us (26%)
  local copies, waits for them, and re-layouts  16.2 us (8%)
  other arithmetic  3 us (1%)
    ppermute x21, waiting for transfers between devices, shift_chips(): return lax.ppermute(value, 'loop', pairs)  62.6 us
    dot_general x46, matrix products, project_rows(): lax.dot_general(rows, weight, (((1,), (1,)), ((), ())), preferred_element...  56 us
    ppermute x21, starting transfers between devices, shift_chips(): return lax.ppermute(value, 'loop', pairs)  21.5 us
    ppermute x11, starting transfers between devices, swap_cores(): return lax.ppermute(value, 'loop', [(i, i ^ 1) for i in range(2 * CHIPS)])  13.1 us
    unnamed x41, local copies, waits for them, and re-layouts  11.4 us
    all_to_all x1, starting transfers between devices, local(): lax.all_to_all(result, 'expert', split_axis=0, concat_axis=0, tiled=True)  10.8 us
    all_to_all x1, starting transfers between devices, local(): lax.all_to_all(outgoing, 'expert', split_axis=0, concat_axis=0, tiled=True)  10 us
    dot_general x6, matrix products, dot(): return jnp.dot(left, right, preferred_element_type=F32)  9.5 us
  transfers between devices with their start and end apart: 34, of which 13 were waited for; matrix products, arithmetic and copies ran while one was open for 39% of the time, Pallas kernels for 0%

profile of v1, /device:TPU:1, one launch (start us, length us, event | category | flops | bytes accessed | tf_op | source)
XLA Modules:
  0.0 213.4 jit_solution(5951553971373923943)
XLA Ops:
  0.0 3.2 %collective-permute-start = (bf16[128,640]{1,0:T(8,128)(2,1)}, bf16[128,640]{1,0:T(8,128)(2,1)S(1)}, u32[]{:S(2)}, u32[]{:S(2)}) collective-permute-start(bf16[128,640]{1,0:T(8,128)(2,1)} %param.9), channel_id=1, source_target_pairs={{0,1},{1,0},{2,3},{3,2},{4,5},{5,4},{6,7},{7,6},{8,9},{9,8},{10,11... | collective-permute-start | bytes 491528 | tf_op jit(solution)/shard_map/ppermute | solution.py:12
  3.2 2.1 constant_dynamic-update-slice_fusion.12
  5.8 2.4 %dynamic-slice_bitcast_fusion = (bf16[192,1280]{1,0:T(8,128)(2,1)}, bf16[192,1280]{1,0:T(8,128)(2,1)}, bf16[192,1280]{1,0:T(8,128)(2,1)S(1)}) fusion(bf16[1,192,5120]{2,1,0:T(8,128)(2,1)} %param.14, s32[]{:T(128)S(6)} %select_n.53, s32[]{:T(128)S(6)} %select_n.51, s32[]{:T(128)S(6)} %select_n.52), kind=kLoop, calls=%fused_computation.97 | loop fusion | bytes 2949132 | tf_op jit(solution)/shard_map/dynamic_slice | solution.py:45
  8.2 1.9 collective-permute-start.12
  12.1 1.6 convolution_convert_fusion
  13.7 10.0 %all-to-all-start = ((bf16[32,16,1280]{2,1,0:T(8,128)(2,1)}), bf16[32,16,1280]{2,1,0:T(8,128)(2,1)}, u32[]{:S(2)}, u32[]{:S(2)}) async-start(bf16[32,16,1280]{2,1,0:T(8,128)(2,1)} %bitcast.4), calls=%async_computation | async-start | bytes 2621440 | tf_op jit(solution)/shard_map/all_to_all | solution.py:105
  23.7 12.9 %collective-permute-done.22 = bf16[64,1280]{1,0:T(8,128)(2,1)S(1)} collective-permute-done((bf16[64,1280]{1,0:T(8,128)(2,1)S(1)}, bf16[64,1280]{1,0:T(8,128)(2,1)S(1)}, u32[]{:S(2)}, u32[]{:S(2)}) %collective-permute-start.22) | collective-permute-done | bytes 163872 | tf_op jit(solution)/shard_map/ppermute | solution.py:21
  37.2 4.5 %collective-permute-done.24 = bf16[64,1280]{1,0:T(8,128)(2,1)S(1)} collective-permute-done((bf16[64,1280]{1,0:T(8,128)(2,1)S(1)}, bf16[64,1280]{1,0:T(8,128)(2,1)S(1)}, u32[]{:S(2)}, u32[]{:S(2)}) %collective-permute-start.24) | collective-permute-done | bytes 163872 | tf_op jit(solution)/shard_map/ppermute | solution.py:21
  43.1 4.7 %collective-permute-done.23 = bf16[64,1280]{1,0:T(8,128)(2,1)S(1)} collective-permute-done((bf16[64,1280]{1,0:T(8,128)(2,1)S(1)}, bf16[64,1280]{1,0:T(8,128)(2,1)S(1)}, u32[]{:S(2)}, u32[]{:S(2)}) %collective-permute-start.23) | collective-permute-done | bytes 163872 | tf_op jit(solution)/shard_map/ppermute | solution.py:21
  47.8 1.6 collective-permute-start.14
  54.7 2.4 %collective-permute-start.11 = (bf16[192,1280]{1,0:T(8,128)(2,1)}, bf16[192,1280]{1,0:T(8,128)(2,1)}, u32[]{:S(2)}, u32[]{:S(2)}) collective-permute-start(bf16[192,1280]{1,0:T(8,128)(2,1)} %collective-permute-done.10), channel_id=1, source_target_pairs={{0,1},{1,0},{2,3},{3,2},{4,5},{5,4},{6,7},{7,6},{8,9},{9,8},{10,11... | collective-permute-start | bytes 1474568 | tf_op jit(solution)/shard_map/ppermute | solution.py:12
  57.1 2.6 %fusion.122 = f32[64,5120]{1,0:T(8,128)S(1)} fusion(bf16[192,5120]{1,0:T(8,128)(2,1)} %param.17, f32[64,192]{1,0:T(8,128)S(1)} %fusion.14, f32[64,192]{1,0:T(8,128)S(1)} %fusion.60, f32[64,192]{1,0:T(8,128)S(1)} %convolution_add_fusion.22, bf16[64,1280]{1,0:T(8,128)(2,1)S(1)} %collective-permute-done.23, bf16[192,5120]{1,0:T(8,128)(2,1)} %param.15, ...), kind=kOutput, calls=%fused_computation.190 | convolution fusion | flops 157384704 | bytes 4079620 | tf_op jit(solution)/shard_map/dot_general | solution.py:41
  61.2 1.9 constant_dynamic-update-slice_fusion.10
  63.6 1.9 constant_dynamic-update-slice_fusion.9
  65.5 1.9 constant_dynamic-update-slice_fusion.8
  68.3 1.8 constant_dynamic-update-slice_fusion.6
  71.4 1.9 fusion.40
  79.3 11.8 %collective-permute-done.17 = bf16[256,1280]{1,0:T(8,128)(2,1)S(1)} collective-permute-done((bf16[256,1280]{1,0:T(8,128)(2,1)S(1)}, bf16[256,1280]{1,0:T(8,128)(2,1)S(1)}, u32[]{:S(2)}, u32[]{:S(2)}) %collective-permute-start.17) | collective-permute-done | bytes 655392 | tf_op jit(solution)/shard_map/ppermute | solution.py:21
  93.0 2.6 %collective-permute-start.3 = (bf16[256,1280]{1,0:T(8,128)(2,1)S(1)}, bf16[256,1280]{1,0:T(8,128)(2,1)S(1)}, u32[]{:S(2)}, u32[]{:S(2)}) collective-permute-start(bf16[256,1280]{1,0:T(8,128)(2,1)S(1)} %bitcast.140), channel_id=1, source_target_pairs={{0,6},{1,7},{2,0},{3,1},{4,2},{5,3},{6,4},{7,5},{8,14},{9,15},{10,... | collective-permute-start | bytes 1966088 | tf_op jit(solution)/shard_map/ppermute | solution.py:21
  97.0 10.6 %collective-permute-done.16 = bf16[256,1280]{1,0:T(8,128)(2,1)S(1)} collective-permute-done((bf16[256,1280]{1,0:T(8,128)(2,1)S(1)}, bf16[256,1280]{1,0:T(8,128)(2,1)S(1)}, u32[]{:S(2)}, u32[]{:S(2)}) %collective-permute-start.16) | collective-permute-done | bytes 655392 | tf_op jit(solution)/shard_map/ppermute | solution.py:21
  109.1 2.8 %collective-permute-start.18 = (bf16[256,1280]{1,0:T(8,128)(2,1)S(1)}, bf16[256,1280]{1,0:T(8,128)(2,1)S(1)}, u32[]{:S(2)}, u32[]{:S(2)}) collective-permute-start(bf16[256,1280]{1,0:T(8,128)(2,1)S(1)} %collective-permute-done.17), channel_id=1, source_target_pairs={{0,6},{1,7},{2,0},{3,1},{4,2},{5,3},{6,4},{7,5},{8,14},{9,15},{10,... | collective-permute-start | bytes 1966088 | tf_op jit(solution)/shard_map/ppermute | solution.py:21
  113.3 1.4 fusion.84
  117.9 5.4 %collective-permute-done.1 = bf16[256,1280]{1,0:T(8,128)(2,1)S(1)} collective-permute-done((bf16[256,1280]{1,0:T(8,128)(2,1)S(1)}, bf16[256,1280]{1,0:T(8,128)(2,1)S(1)}, u32[]{:S(2)}, u32[]{:S(2)}) %collective-permute-start.1) | collective-permute-done | bytes 655392 | tf_op jit(solution)/shard_map/ppermute | solution.py:21
  128.0 1.4 convolution_add_fusion.2
  129.4 1.4 convolution_add_fusion.4
  132.6 1.4 fusion.86
  134.0 1.4 convolution_add_fusion.10
  135.4 1.4 convolution_add_fusion.12
  138.7 1.4 constant_dynamic-update-slice_fusion.17
  140.1 1.4 constant_dynamic-update-slice_fusion.16
  141.7 3.9 %collective-permute-start.20 = (bf16[256,384]{0,1:T(8,128)(2,1)S(1)}, bf16[256,384]{0,1:T(8,128)(2,1)S(1)}, u32[]{:S(2)}, u32[]{:S(2)}) collective-permute-start(bf16[256,384]{0,1:T(8,128)(2,1)S(1)} %pad_maximum_fusion.2), channel_id=1, source_target_pairs={{0,4},{1,5},{2,6},{3,7},{4,0},{5,1},{6,2},{7,3},{8,12},{9,13},{10,... | collective-permute-start | bytes 589832 | tf_op jit(solution)/shard_map/ppermute | solution.py:21
  145.9 1.4 fusion.4
  147.3 1.4 constant_dynamic-update-slice_fusion.4
  148.8 1.6 constant_dynamic-update-slice_fusion.3
  150.4 1.5 collective-permute-start.6
  152.7 2.4 %collective-permute-start.8 = (bf16[256,384]{0,1:T(8,128)(2,1)S(1)}, bf16[256,384]{0,1:T(8,128)(2,1)S(1)}, u32[]{:S(2)}, u32[]{:S(2)}) collective-permute-start(bf16[256,384]{0,1:T(8,128)(2,1)S(1)} %pad_maximum_fusion.1), channel_id=1, source_target_pairs={{0,6},{1,7},{2,0},{3,1},{4,2},{5,3},{6,4},{7,5},{8,14},{9,15},{10,... | collective-permute-start | bytes 589832 | tf_op jit(solution)/shard_map/ppermute | solution.py:21
  155.1 2.9 %collective-permute-done.6 = bf16[256,384]{0,1:T(8,128)(2,1)S(1)} collective-permute-done((bf16[256,384]{0,1:T(8,128)(2,1)S(1)}, bf16[256,384]{0,1:T(8,128)(2,1)S(1)}, u32[]{:S(2)}, u32[]{:S(2)}) %collective-permute-start.6) | collective-permute-done | bytes 196640 | tf_op jit(solution)/shard_map/ppermute | solution.py:21
  158.1 3.3 %collective-permute-done.7 = bf16[256,384]{0,1:T(8,128)(2,1)S(1)} collective-permute-done((bf16[256,384]{0,1:T(8,128)(2,1)S(1)}, bf16[256,384]{0,1:T(8,128)(2,1)S(1)}, u32[]{:S(2)}, u32[]{:S(2)}) %collective-permute-start.7) | collective-permute-done | bytes 196640 | tf_op jit(solution)/shard_map/ppermute | solution.py:21
  165.1 10.8 %all-to-all-start.1 = ((bf16[32,16,1280]{2,1,0:T(8,128)(2,1)}), bf16[32,16,1280]{2,1,0:T(8,128)(2,1)S(1)}, u32[]{:S(2)}, u32[]{:S(2)}) async-start(bf16[32,16,1280]{2,1,0:T(8,128)(2,1)} %bitcast.151), calls=%async_computation.1 | async-start | bytes 2621440 | tf_op jit(solution)/shard_map/all_to_all | solution.py:129
  179.9 2.0 fusion.49
  181.9 1.9 fusion.51
  183.8 2.0 fusion.11
  185.8 2.7 %fusion = bf16[64,5120]{1,0:T(8,128)(2,1)S(1)} fusion(f32[64,5120]{1,0:T(8,128)S(1)} %fusion.122, bf16[192,5120]{1,0:T(8,128)(2,1)} %collective-permute-done.27, f32[64,192]{1,0:T(8,128)} %fusion.11, f32[64,192]{1,0:T(8,128)S(1)} %fusion.47, f32[64,192]{1,0:T(8,128)} %fusion.49, f32[64,192]{1,0:T(8,128)} %fusion.51, ...), kind=kOutput, calls=%fused_computation.1 | convolution fusion | flops 158052352 | bytes 4833284 | tf_op jit(solution)/shard_map/dot_general | solution.py:41
  190.1 3.0 %collective-permute-done.30 = bf16[64,1280]{1,0:T(8,128)(2,1)S(1)} collective-permute-done((bf16[64,1280]{1,0:T(8,128)(2,1)S(1)}, bf16[64,1280]{1,0:T(8,128)(2,1)S(1)}, u32[]{:S(2)}, u32[]{:S(2)}) %collective-permute-start.30) | collective-permute-done | bytes 163872 | tf_op jit(solution)/shard_map/ppermute | solution.py:21
  193.1 1.6 collective-permute-done.29
  194.7 1.8 collective-permute-done.28
  197.3 7.9 %all-to-all-done.1 = bf16[32,16,1280]{2,1,0:T(8,128)(2,1)S(1)} async-done(((bf16[32,16,1280]{2,1,0:T(8,128)(2,1)}), bf16[32,16,1280]{2,1,0:T(8,128)(2,1)S(1)}, u32[]{:S(2)}, u32[]{:S(2)}) %all-to-all-start.1) | async-done | bytes 1310752 | tf_op jit(solution)/shard_map/all_to_all | solution.py:129
  206.1 5.3 %collective-permute-start.31 = (f32[128,640]{1,0:T(8,128)S(1)}, f32[128,640]{1,0:T(8,128)S(1)}, u32[]{:S(2)}, u32[]{:S(2)}) collective-permute-start(f32[128,640]{1,0:T(8,128)S(1)} %constant_dynamic-slice_fusion), channel_id=1, source_target_pairs={{0,1},{1,0},{2,3},{3,2},{4,5},{5,4},{6,7},{7,6},{8,9},{9,8},{10,11... | collective-permute-start | bytes 983048 | tf_op jit(solution)/shard_map/ppermute | solution.py:12
  (135 shorter events, 51.5 us)
Async XLA Ops:
  0.0 10.6 %collective-permute-start = (bf16[128,640]{1,0:T(8,128)(2,1)}, bf16[128,640]{1,0:T(8,128)(2,1)S(1)}, u32[]{:S(2)}, u32[]{:S(2)}) collective-permute-start(bf16[128,640]{1,0:T(8,128)(2,1)} %param.9), channel_id=1, source_target_pairs={{0,1},{1,0},{2,3},{3,2},{4,5},{5,4},{6,7},{7,6},{8,9},{9,8},{10,11... | collective-permute-start | bytes 491528 | tf_op jit(solution)/shard_map/ppermute | solution.py:12
  3.2 68.1 %collective-permute-start.26 = (bf16[192,5120]{1,0:T(8,128)(2,1)}, bf16[192,5120]{1,0:T(8,128)(2,1)}, u32[]{:S(2)}, u32[]{:S(2)}) collective-permute-start(bf16[192,5120]{1,0:T(8,128)(2,1)} %param.16), channel_id=1, source_target_pairs={{0,1},{1,0},{2,3},{3,2},{4,5},{5,4},{6,7},{7,6},{8,9},{9,8},{10,11... | collective-permute-start | bytes 5898248 | tf_op jit(solution)/shard_map/ppermute | solution.py:12
  3.2 7.0 %copy-start.13 = (s32[128,6]{0,1:T(8,128)S(1)}, s32[128,6]{0,1:T(8,128)}, u32[]{:S(2)}) copy-start(s32[128,6]{0,1:T(8,128)} %param.10) | copy-start | bytes 9220
  5.3 5.2 %copy-start.11 = (bf16[128,640]{1,0:T(8,128)(2,1)S(1)}, bf16[128,640]{1,0:T(8,128)(2,1)}, u32[]{:S(2)}) copy-start(bf16[128,640]{1,0:T(8,128)(2,1)} %param.9) | copy-start | bytes 491524
  5.3 54.4 %collective-permute-start.9 = (bf16[192,1280]{1,0:T(8,128)(2,1)}, bf16[192,1280]{1,0:T(8,128)(2,1)S(1)}, u32[]{:S(2)}, u32[]{:S(2)}) collective-permute-start(bf16[192,1280]{1,0:T(8,128)(2,1)} %get-tuple-element.6), channel_id=1, source_target_pairs={{0,1},{1,0},{2,3},{3,2},{4,5},{5,4},{6,7},{7,6},{8,9},{9,8},{10,11... | collective-permute-start | bytes 1474568 | tf_op jit(solution)/shard_map/ppermute | solution.py:12
  8.2 46.5 %collective-permute-start.10 = (bf16[192,1280]{1,0:T(8,128)(2,1)}, bf16[192,1280]{1,0:T(8,128)(2,1)}, u32[]{:S(2)}, u32[]{:S(2)}) collective-permute-start(bf16[192,1280]{1,0:T(8,128)(2,1)} %get-tuple-element.8), channel_id=1, source_target_pairs={{0,2},{1,3},{2,4},{3,5},{4,6},{5,7},{6,0},{7,1},{8,10},{9,11},{10,... | collective-permute-start | bytes 1474568 | tf_op jit(solution)/shard_map/ppermute | solution.py:21
  8.2 51.6 %collective-permute-start.12 = (bf16[192,1280]{1,0:T(8,128)(2,1)S(1)}, bf16[192,1280]{1,0:T(8,128)(2,1)}, u32[]{:S(2)}, u32[]{:S(2)}) collective-permute-start(bf16[192,1280]{1,0:T(8,128)(2,1)S(1)} %get-tuple-element.9), channel_id=1, source_target_pairs={{0,4},{1,5},{2,6},{3,7},{4,0},{5,1},{6,2},{7,3},{8,12},{9,13},{10,... | collective-permute-start | bytes 1474568 | tf_op jit(solution)/shard_map/ppermute | solution.py:21
  10.7 25.9 %copy-start.8 = (bf16[192,5120]{1,0:T(8,128)(2,1)S(1)}, bf16[192,5120]{1,0:T(8,128)(2,1)}, u32[]{:S(2)}) copy-start(bf16[192,5120]{1,0:T(8,128)(2,1)} %param.16) | copy-start | bytes 5898244
  10.7 25.9 %collective-permute-start.22 = (bf16[64,1280]{1,0:T(8,128)(2,1)S(1)}, bf16[64,1280]{1,0:T(8,128)(2,1)S(1)}, u32[]{:S(2)}, u32[]{:S(2)}) collective-permute-start(bf16[64,1280]{1,0:T(8,128)(2,1)S(1)} %constant_dynamic-slice_fusion.4), channel_id=1, source_target_pairs={{0,2},{1,3},{2,4},{3,5},{4,6},{5,7},{6,0},{7,1},{8,10},{9,11},{10,... | collective-permute-start | bytes 491528 | tf_op jit(solution)/shard_map/ppermute | solution.py:21
  13.7 59.7 %all-to-all-start = ((bf16[32,16,1280]{2,1,0:T(8,128)(2,1)}), bf16[32,16,1280]{2,1,0:T(8,128)(2,1)}, u32[]{:S(2)}, u32[]{:S(2)}) async-start(bf16[32,16,1280]{2,1,0:T(8,128)(2,1)} %bitcast.4), calls=%async_computation | async-start | bytes 2621440 | tf_op jit(solution)/shard_map/all_to_all | solution.py:105
  36.6 16.8 %copy-start.3 = (bf16[64,1280]{1,0:T(8,128)(2,1)}, bf16[64,1280]{1,0:T(8,128)(2,1)S(1)}, u32[]{:S(2)}) copy-start(bf16[64,1280]{1,0:T(8,128)(2,1)S(1)} %collective-permute-done.22) | copy-start | bytes 491524
  36.6 5.1 %collective-permute-start.24 = (bf16[64,1280]{1,0:T(8,128)(2,1)S(1)}, bf16[64,1280]{1,0:T(8,128)(2,1)S(1)}, u32[]{:S(2)}, u32[]{:S(2)}) collective-permute-start(bf16[64,1280]{1,0:T(8,128)(2,1)S(1)} %constant_dynamic-slice_fusion.4), channel_id=1, source_target_pairs={{0,6},{1,7},{2,0},{3,1},{4,2},{5,3},{6,4},{7,5},{8,14},{9,15},{10,... | collective-permute-start | bytes 491528 | tf_op jit(solution)/shard_map/ppermute | solution.py:21
  41.7 13.0 %copy-start.5 = (bf16[64,1280]{1,0:T(8,128)(2,1)}, bf16[64,1280]{1,0:T(8,128)(2,1)S(1)}, u32[]{:S(2)}) copy-start(bf16[64,1280]{1,0:T(8,128)(2,1)S(1)} %collective-permute-done.24) | copy-start | bytes 491524
  41.7 6.1 %collective-permute-start.23 = (bf16[64,1280]{1,0:T(8,128)(2,1)S(1)}, bf16[64,1280]{1,0:T(8,128)(2,1)S(1)}, u32[]{:S(2)}, u32[]{:S(2)}) collective-permute-start(bf16[64,1280]{1,0:T(8,128)(2,1)S(1)} %constant_dynamic-slice_fusion.4), channel_id=1, source_target_pairs={{0,4},{1,5},{2,6},{3,7},{4,0},{5,1},{6,2},{7,3},{8,12},{9,13},{10,... | collective-permute-start | bytes 491528 | tf_op jit(solution)/shard_map/ppermute | solution.py:21
  47.8 11.9 %copy-start.1 = (bf16[64,1280]{1,0:T(8,128)(2,1)}, bf16[64,1280]{1,0:T(8,128)(2,1)S(1)}, u32[]{:S(2)}) copy-start(bf16[64,1280]{1,0:T(8,128)(2,1)S(1)} %collective-permute-done.23) | copy-start | bytes 491524
  47.8 15.3 %collective-permute-start.14 = (bf16[192,1280]{1,0:T(8,128)(2,1)}, bf16[192,1280]{1,0:T(8,128)(2,1)}, u32[]{:S(2)}, u32[]{:S(2)}) collective-permute-start(bf16[192,1280]{1,0:T(8,128)(2,1)} %get-tuple-element.7), channel_id=1, source_target_pairs={{0,6},{1,7},{2,0},{3,1},{4,2},{5,3},{6,4},{7,5},{8,14},{9,15},{10,... | collective-permute-start | bytes 1474568 | tf_op jit(solution)/shard_map/ppermute | solution.py:21
  54.7 8.5 %collective-permute-start.11 = (bf16[192,1280]{1,0:T(8,128)(2,1)}, bf16[192,1280]{1,0:T(8,128)(2,1)}, u32[]{:S(2)}, u32[]{:S(2)}) collective-permute-start(bf16[192,1280]{1,0:T(8,128)(2,1)} %collective-permute-done.10), channel_id=1, source_target_pairs={{0,1},{1,0},{2,3},{3,2},{4,5},{5,4},{6,7},{7,6},{8,9},{9,8},{10,11... | collective-permute-start | bytes 1474568 | tf_op jit(solution)/shard_map/ppermute | solution.py:12
  59.8 126.0 %collective-permute-start.27 = (bf16[192,5120]{1,0:T(8,128)(2,1)}, bf16[192,5120]{1,0:T(8,128)(2,1)}, u32[]{:S(2)}, u32[]{:S(2)}) collective-permute-start(bf16[192,5120]{1,0:T(8,128)(2,1)} %param.17), channel_id=1, source_target_pairs={{0,1},{1,0},{2,3},{3,2},{4,5},{5,4},{6,7},{7,6},{8,9},{9,8},{10,11... | collective-permute-start | bytes 5898248 | tf_op jit(solution)/shard_map/ppermute | solution.py:12
  59.9 7.5 %collective-permute-start.13 = (bf16[192,1280]{1,0:T(8,128)(2,1)}, bf16[192,1280]{1,0:T(8,128)(2,1)S(1)}, u32[]{:S(2)}, u32[]{:S(2)}) collective-permute-start(bf16[192,1280]{1,0:T(8,128)(2,1)} %collective-permute-done.12), channel_id=1, source_target_pairs={{0,1},{1,0},{2,3},{3,2},{4,5},{5,4},{6,7},{7,6},{8,9},{9,8},{10,11... | collective-permute-start | bytes 1474568 | tf_op jit(solution)/shard_map/ppermute | solution.py:12
  63.1 7.1 %copy-start = (bf16[1,192,5120]{2,1,0:T(8,128)(2,1)S(1)}, bf16[1,192,5120]{2,1,0:T(8,128)(2,1)}, u32[]{:S(2)}) copy-start(bf16[1,192,5120]{2,1,0:T(8,128)(2,1)} %param.12) | copy-start | bytes 5898244
  63.1 115.5 %collective-permute-start.25 = (bf16[192,5120]{1,0:T(8,128)(2,1)}, bf16[192,5120]{1,0:T(8,128)(2,1)}, u32[]{:S(2)}, u32[]{:S(2)}) collective-permute-start(bf16[192,5120]{1,0:T(8,128)(2,1)} %param.15), channel_id=1, source_target_pairs={{0,1},{1,0},{2,3},{3,2},{4,5},{5,4},{6,7},{7,6},{8,9},{9,8},{10,11... | collective-permute-start | bytes 5898248 | tf_op jit(solution)/shard_map/ppermute | solution.py:12
  63.2 7.0 %collective-permute-start.15 = (bf16[192,1280]{1,0:T(8,128)(2,1)}, bf16[192,1280]{1,0:T(8,128)(2,1)S(1)}, u32[]{:S(2)}, u32[]{:S(2)}) collective-permute-start(bf16[192,1280]{1,0:T(8,128)(2,1)} %collective-permute-done.14), channel_id=1, source_target_pairs={{0,1},{1,0},{2,3},{3,2},{4,5},{5,4},{6,7},{7,6},{8,9},{9,8},{10,11... | collective-permute-start | bytes 1474568 | tf_op jit(solution)/shard_map/ppermute | solution.py:12
  65.5 5.9 %copy-start.6 = (bf16[64,1280]{1,0:T(8,128)(2,1)S(1)}, bf16[64,1280]{1,0:T(8,128)(2,1)}, u32[]{:S(2)}) copy-start(bf16[64,1280]{1,0:T(8,128)(2,1)} %copy-done.5) | copy-start | bytes 491524
  67.4 25.6 %collective-permute-start.5 = (bf16[192,5120]{1,0:T(8,128)(2,1)}, bf16[192,5120]{1,0:T(8,128)(2,1)}, u32[]{:S(2)}, u32[]{:S(2)}) collective-permute-start(bf16[192,5120]{1,0:T(8,128)(2,1)} %bitcast.15), channel_id=1, source_target_pairs={{0,1},{1,0},{2,3},{3,2},{4,5},{5,4},{6,7},{7,6},{8,9},{9,8},{10,11... | collective-permute-start | bytes 5898248 | tf_op jit(solution)/shard_map/ppermute | solution.py:12
  70.2 38.9 %collective-permute-start.4 = (bf16[192,5120]{1,0:T(8,128)(2,1)S(1)}, bf16[192,5120]{1,0:T(8,128)(2,1)}, u32[]{:S(2)}, u32[]{:S(2)}) collective-permute-start(bf16[192,5120]{1,0:T(8,128)(2,1)S(1)} %bitcast.150), channel_id=1, source_target_pairs={{0,1},{1,0},{2,3},{3,2},{4,5},{5,4},{6,7},{7,6},{8,9},{9,8},{10,11... | collective-permute-start | bytes 5898248 | tf_op jit(solution)/shard_map/ppermute | solution.py:12
  74.7 16.4 %collective-permute-start.17 = (bf16[256,1280]{1,0:T(8,128)(2,1)S(1)}, bf16[256,1280]{1,0:T(8,128)(2,1)S(1)}, u32[]{:S(2)}, u32[]{:S(2)}) collective-permute-start(bf16[256,1280]{1,0:T(8,128)(2,1)S(1)} %bitcast.144), channel_id=1, source_target_pairs={{0,6},{1,7},{2,0},{3,1},{4,2},{5,3},{6,4},{7,5},{8,14},{9,15},{10,... | collective-permute-start | bytes 1966088 | tf_op jit(solution)/shard_map/ppermute | solution.py:21
  91.1 16.6 %collective-permute-start.16 = (bf16[256,1280]{1,0:T(8,128)(2,1)S(1)}, bf16[256,1280]{1,0:T(8,128)(2,1)S(1)}, u32[]{:S(2)}, u32[]{:S(2)}) collective-permute-start(bf16[256,1280]{1,0:T(8,128)(2,1)S(1)} %bitcast.147), channel_id=1, source_target_pairs={{0,2},{1,3},{2,4},{3,5},{4,6},{5,7},{6,0},{7,1},{8,10},{9,11},{10,... | collective-permute-start | bytes 1966088 | tf_op jit(solution)/shard_map/ppermute | solution.py:21
  93.0 21.7 %collective-permute-start.3 = (bf16[256,1280]{1,0:T(8,128)(2,1)S(1)}, bf16[256,1280]{1,0:T(8,128)(2,1)S(1)}, u32[]{:S(2)}, u32[]{:S(2)}) collective-permute-start(bf16[256,1280]{1,0:T(8,128)(2,1)S(1)} %bitcast.140), channel_id=1, source_target_pairs={{0,6},{1,7},{2,0},{3,1},{4,2},{5,3},{6,4},{7,5},{8,14},{9,15},{10,... | collective-permute-start | bytes 1966088 | tf_op jit(solution)/shard_map/ppermute | solution.py:21
  107.7 15.7 %collective-permute-start.1 = (bf16[256,1280]{1,0:T(8,128)(2,1)S(1)}, bf16[256,1280]{1,0:T(8,128)(2,1)S(1)}, u32[]{:S(2)}, u32[]{:S(2)}) collective-permute-start(bf16[256,1280]{1,0:T(8,128)(2,1)S(1)} %bitcast.141), channel_id=1, source_target_pairs={{0,2},{1,3},{2,4},{3,5},{4,6},{5,7},{6,0},{7,1},{8,10},{9,11},{10,... | collective-permute-start | bytes 1966088 | tf_op jit(solution)/shard_map/ppermute | solution.py:21
  109.1 27.8 %collective-permute-start.18 = (bf16[256,1280]{1,0:T(8,128)(2,1)S(1)}, bf16[256,1280]{1,0:T(8,128)(2,1)S(1)}, u32[]{:S(2)}, u32[]{:S(2)}) collective-permute-start(bf16[256,1280]{1,0:T(8,128)(2,1)S(1)} %collective-permute-done.17), channel_id=1, source_target_pairs={{0,6},{1,7},{2,0},{3,1},{4,2},{5,3},{6,4},{7,5},{8,14},{9,15},{10,... | collective-permute-start | bytes 1966088 | tf_op jit(solution)/shard_map/ppermute | solution.py:21
  123.3 22.2 %collective-permute-start.2 = (bf16[256,1280]{1,0:T(8,128)(2,1)S(1)}, bf16[256,1280]{1,0:T(8,128)(2,1)S(1)}, u32[]{:S(2)}, u32[]{:S(2)}) collective-permute-start(bf16[256,1280]{1,0:T(8,128)(2,1)S(1)} %collective-permute-done.1), channel_id=1, source_target_pairs={{0,2},{1,3},{2,4},{3,5},{4,6},{5,7},{6,0},{7,1},{8,10},{9,11},{10,... | collective-permute-start | bytes 1966088 | tf_op jit(solution)/shard_map/ppermute | solution.py:21
  141.6 8.8 %collective-permute-start.19 = (bf16[256,384]{0,1:T(8,128)(2,1)S(1)}, bf16[256,384]{0,1:T(8,128)(2,1)S(1)}, u32[]{:S(2)}, u32[]{:S(2)}) collective-permute-start(bf16[256,384]{0,1:T(8,128)(2,1)S(1)} %pad_maximum_fusion.2), channel_id=1, source_target_pairs={{0,2},{1,3},{2,4},{3,5},{4,6},{5,7},{6,0},{7,1},{8,10},{9,11},{10,... | collective-permute-start | bytes 589832 | tf_op jit(solution)/shard_map/ppermute | solution.py:21
  141.7 10.3 %collective-permute-start.20 = (bf16[256,384]{0,1:T(8,128)(2,1)S(1)}, bf16[256,384]{0,1:T(8,128)(2,1)S(1)}, u32[]{:S(2)}, u32[]{:S(2)}) collective-permute-start(bf16[256,384]{0,1:T(8,128)(2,1)S(1)} %pad_maximum_fusion.2), channel_id=1, source_target_pairs={{0,4},{1,5},{2,6},{3,7},{4,0},{5,1},{6,2},{7,3},{8,12},{9,13},{10,... | collective-permute-start | bytes 589832 | tf_op jit(solution)/shard_map/ppermute | solution.py:21
  145.5 7.2 %collective-permute-start.21 = (bf16[256,384]{0,1:T(8,128)(2,1)S(1)}, bf16[256,384]{0,1:T(8,128)(2,1)S(1)}, u32[]{:S(2)}, u32[]{:S(2)}) collective-permute-start(bf16[256,384]{0,1:T(8,128)(2,1)S(1)} %pad_maximum_fusion.2), channel_id=1, source_target_pairs={{0,6},{1,7},{2,0},{3,1},{4,2},{5,3},{6,4},{7,5},{8,14},{9,15},{10,... | collective-permute-start | bytes 589832 | tf_op jit(solution)/shard_map/ppermute | solution.py:21
  148.8 12.6 %copy-start.12 = (bf16[1536,1280]{1,0:T(8,128)(2,1)S(1)}, bf16[1536,1280]{1,0:T(8,128)(2,1)}, u32[]{:S(2)}) copy-start(bf16[1536,1280]{1,0:T(8,128)(2,1)} %constant_dynamic-update-slice_fusion.5) | copy-start | bytes 11796484
  150.4 7.6 %collective-permute-start.6 = (bf16[256,384]{0,1:T(8,128)(2,1)S(1)}, bf16[256,384]{0,1:T(8,128)(2,1)S(1)}, u32[]{:S(2)}, u32[]{:S(2)}) collective-permute-start(bf16[256,384]{0,1:T(8,128)(2,1)S(1)} %pad_maximum_fusion.1), channel_id=1, source_target_pairs={{0,2},{1,3},{2,4},{3,5},{4,6},{5,7},{6,0},{7,1},{8,10},{9,11},{10,... | collective-permute-start | bytes 589832 | tf_op jit(solution)/shard_map/ppermute | solution.py:21
  152.0 9.4 %collective-permute-start.7 = (bf16[256,384]{0,1:T(8,128)(2,1)S(1)}, bf16[256,384]{0,1:T(8,128)(2,1)S(1)}, u32[]{:S(2)}, u32[]{:S(2)}) collective-permute-start(bf16[256,384]{0,1:T(8,128)(2,1)S(1)} %pad_maximum_fusion.1), channel_id=1, source_target_pairs={{0,4},{1,5},{2,6},{3,7},{4,0},{5,1},{6,2},{7,3},{8,12},{9,13},{10,... | collective-permute-start | bytes 589832 | tf_op jit(solution)/shard_map/ppermute | solution.py:21
  152.7 8.7 %collective-permute-start.8 = (bf16[256,384]{0,1:T(8,128)(2,1)S(1)}, bf16[256,384]{0,1:T(8,128)(2,1)S(1)}, u32[]{:S(2)}, u32[]{:S(2)}) collective-permute-start(bf16[256,384]{0,1:T(8,128)(2,1)S(1)} %pad_maximum_fusion.1), channel_id=1, source_target_pairs={{0,6},{1,7},{2,0},{3,1},{4,2},{5,3},{6,4},{7,5},{8,14},{9,15},{10,... | collective-permute-start | bytes 589832 | tf_op jit(solution)/shard_map/ppermute | solution.py:21
  165.1 10.8 %copy-start.2 = (bf16[64,1280]{1,0:T(8,128)(2,1)S(1)}, bf16[64,1280]{1,0:T(8,128)(2,1)}, u32[]{:S(2)}) copy-start(bf16[64,1280]{1,0:T(8,128)(2,1)} %copy-done.1) | copy-start | bytes 491524
  165.1 12.2 %copy-start.4 = (bf16[64,1280]{1,0:T(8,128)(2,1)S(1)}, bf16[64,1280]{1,0:T(8,128)(2,1)}, u32[]{:S(2)}) copy-start(bf16[64,1280]{1,0:T(8,128)(2,1)} %copy-done.3) | copy-start | bytes 491524
  165.1 13.5 %copy-start.7 = (bf16[64,1280]{1,0:T(8,128)(2,1)S(1)}, bf16[64,1280]{1,0:T(8,128)(2,1)}, u32[]{:S(2)}) copy-start(bf16[64,1280]{1,0:T(8,128)(2,1)} %copy-done.5) | copy-start | bytes 491524
  165.1 40.1 %all-to-all-start.1 = ((bf16[32,16,1280]{2,1,0:T(8,128)(2,1)}), bf16[32,16,1280]{2,1,0:T(8,128)(2,1)S(1)}, u32[]{:S(2)}, u32[]{:S(2)}) async-start(bf16[32,16,1280]{2,1,0:T(8,128)(2,1)} %bitcast.151), calls=%async_computation.1 | async-start | bytes 2621440 | tf_op jit(solution)/shard_map/all_to_all | solution.py:129
  175.9 7.9 %copy-start.10 = (f32[64,192]{1,0:T(8,128)S(1)}, f32[64,192]{1,0:T(8,128)}, u32[]{:S(2)}) copy-start(f32[64,192]{1,0:T(8,128)} %fusion.40) | copy-start | bytes 147460
  188.6 4.5 %collective-permute-start.30 = (bf16[64,1280]{1,0:T(8,128)(2,1)S(1)}, bf16[64,1280]{1,0:T(8,128)(2,1)S(1)}, u32[]{:S(2)}, u32[]{:S(2)}) collective-permute-start(bf16[64,1280]{1,0:T(8,128)(2,1)S(1)} %get-tuple-element.13), channel_id=1, source_target_pairs={{0,6},{1,7},{2,0},{3,1},{4,2},{5,3},{6,4},{7,5},{8,14},{9,15},{10,... | collective-permute-start | bytes 491528 | tf_op jit(solution)/shard_map/ppermute | solution.py:21
  188.7 6.0 %collective-permute-start.29 = (bf16[64,1280]{1,0:T(8,128)(2,1)S(1)}, bf16[64,1280]{1,0:T(8,128)(2,1)S(1)}, u32[]{:S(2)}, u32[]{:S(2)}) collective-permute-start(bf16[64,1280]{1,0:T(8,128)(2,1)S(1)} %get-tuple-element.14), channel_id=1, source_target_pairs={{0,4},{1,5},{2,6},{3,7},{4,0},{5,1},{6,2},{7,3},{8,12},{9,13},{10,... | collective-permute-start | bytes 491528 | tf_op jit(solution)/shard_map/ppermute | solution.py:21
  189.6 6.9 %collective-permute-start.28 = (bf16[64,1280]{1,0:T(8,128)(2,1)S(1)}, bf16[64,1280]{1,0:T(8,128)(2,1)S(1)}, u32[]{:S(2)}, u32[]{:S(2)}) collective-permute-start(bf16[64,1280]{1,0:T(8,128)(2,1)S(1)} %get-tuple-element.12), channel_id=1, source_target_pairs={{0,2},{1,3},{2,4},{3,5},{4,6},{5,7},{6,0},{7,1},{8,10},{9,11},{10,... | collective-permute-start | bytes 491528 | tf_op jit(solution)/shard_map/ppermute | solution.py:21
  197.3 8.3 %copy-start.9 = (f32[64,1280]{1,0:T(8,128)S(1)}, f32[64,1280]{1,0:T(8,128)}, u32[]{:S(2)}) copy-start(f32[64,1280]{1,0:T(8,128)} %convert_add_fusion) | copy-start | bytes 983044
  206.1 6.6 %collective-permute-start.31 = (f32[128,640]{1,0:T(8,128)S(1)}, f32[128,640]{1,0:T(8,128)S(1)}, u32[]{:S(2)}, u32[]{:S(2)}) collective-permute-start(f32[128,640]{1,0:T(8,128)S(1)} %constant_dynamic-slice_fusion), channel_id=1, source_target_pairs={{0,1},{1,0},{2,3},{3,2},{4,5},{5,4},{6,7},{7,6},{8,9},{9,8},{10,11... | collective-permute-start | bytes 983048 | tf_op jit(solution)/shard_map/ppermute | solution.py:12
  (1 other events, 4.4 us)

commit v2 on v1

v2 whole, which is shorter than its diff:
```python
import jax
import jax.numpy as jnp
from jax import lax
from jax.experimental import pallas as pl
from jax.experimental.pallas import tpu as pltpu
from jax.sharding import PartitionSpec as P

CHIPS = 4
BF16 = jnp.bfloat16
F32 = jnp.float32


def swap_cores(value):
    return lax.ppermute(value, "loop", [(i, i ^ 1) for i in range(2 * CHIPS)])


def shift_chips(value, step):
    pairs = [
        (2 * chip + core, 2 * ((chip + step) % CHIPS) + core)
        for chip in range(CHIPS)
        for core in range(2)
    ]
    return lax.ppermute(value, "loop", pairs)


def dot(left, right):
    return jnp.dot(left, right, preferred_element_type=F32)


def project_rows(rows, weight):
    return lax.dot_general(rows, weight, (((1,), (1,)), ((), ())), preferred_element_type=F32)


def pick(chip, step, array, width):
    return lax.dynamic_slice_in_dim(array, ((chip - step) & (CHIPS - 1)) * width, width, axis=1)


def hidden_of(act):
    unit = act.shape[1] // 2
    return (jax.nn.silu(act[:, :unit]) * act[:, unit:]).astype(BF16)


def roll_kernel(chip_ref, *refs):
    out = refs[-1]
    unit = refs[0].shape[0]
    for i, ref in enumerate(refs[:-1]):
        out[0, i * unit : (i + 1) * unit, :] = ref[...]


def roll_features(chip, weights, width):
    unit = weights[0].shape[0]
    rows = unit * len(weights)
    return pl.pallas_call(
        roll_kernel,
        out_shape=jax.ShapeDtypeStruct((CHIPS, rows, width), BF16),
        grid_spec=pltpu.PrefetchScalarGridSpec(
            num_scalar_prefetch=1,
            grid=(CHIPS,),
            in_specs=[pl.BlockSpec((unit, width), lambda k, c: (0, (c[0] - k) & (CHIPS - 1)))]
            * len(weights),
            out_specs=pl.BlockSpec((1, rows, width), lambda k, c: (k, 0, 0)),
        ),
        compiler_params=pltpu.CompilerParams(vmem_limit_bytes=24 << 20),
    )(chip.reshape(1), *weights)


def local(tokens, routes, route_weights, gate_w, up_w, down_w, shared_gate, shared_up, shared_down):
    tok_rows, width = tokens.shape
    experts = lax.axis_size("expert")
    half_cap = tok_rows * routes.shape[1] * 4 // (3 * experts) // 2
    place = lax.axis_index("loop")
    chip, core = place >> 1, place & 1
    first_core = core == 0
    chip_width = 2 * width
    steps = (1, 3, 2)

    other_tokens = swap_cores(tokens)
    down_own = [pick(chip, 0, down_w[0], chip_width)] + [
        shift_chips(pick(chip, -k, down_w[0], chip_width), k) for k in steps
    ]
    chip_tokens = jnp.where(
        first_core,
        jnp.concatenate([tokens, other_tokens], axis=1),
        jnp.concatenate([other_tokens, tokens], axis=1),
    )

    ids = jnp.arange(experts, dtype=jnp.int32)
    equal = routes.T[:, None, :] == ids[None, :, None]
    member = jnp.any(equal, axis=0)
    weight = jnp.sum(jnp.where(equal, route_weights.T[:, None, :], 0.0), axis=0)
    row = lax.broadcasted_iota(jnp.int32, (tok_rows, tok_rows), 0)
    col = lax.broadcasted_iota(jnp.int32, (tok_rows, tok_rows), 1)
    before = dot(member.astype(BF16), (row < col).astype(BF16)).astype(jnp.int32)
    slots = jnp.arange(half_cap, dtype=jnp.int32) + core * half_cap
    hit = member[:, None, :] & (before[:, None, :] == slots[None, :, None])
    selector = hit.astype(BF16).reshape(experts * half_cap, tok_rows)
    outgoing = dot(selector, chip_tokens).astype(BF16)

    def exchange(value):
        value = value.reshape(experts, half_cap, chip_width)
        value = lax.all_to_all(value, "expert", split_axis=0, concat_axis=0, tiled=True)
        return value.reshape(experts * half_cap, chip_width)

    rows = exchange(outgoing)

    gate_own, up_own, sent_tokens, down_own, _ = lax.optimization_barrier(
        (gate_w[0], up_w[0], chip_tokens, down_own, outgoing)
    )
    down_four = jnp.stack(down_own)
    down_all = jnp.stack([down_four, swap_cores(down_four)], axis=1).reshape(-1, chip_width)
    gate_other, up_other = swap_cores(gate_own), swap_cores(up_own)
    weights = roll_features(chip, [gate_own, gate_other, up_own, up_other], chip_width)
    token_blocks = [sent_tokens] + [shift_chips(sent_tokens, k) for k in steps]
    rows, weights, down_all, token_blocks = lax.optimization_barrier(
        (rows, weights, down_all, token_blocks)
    )

    cut = rows.shape[0] * 3 // 4
    pieces = [rows[:cut], rows[cut:]]
    gathered = []
    for piece in pieces:
        if gathered:
            gathered[-1], piece = lax.optimization_barrier((gathered[-1], piece))
        gathered.append((piece, shift_chips(piece, 1), shift_chips(piece, -1)))

    def project_in(piece, left, right):
        half = piece.shape[0] // 2
        far = [shift_chips(left[:half], 1), shift_chips(right[half:], -1)]
        act = project_rows(piece, weights[0]) + project_rows(left, weights[1])
        act = act + project_rows(right, weights[3])
        act = act + jnp.concatenate([project_rows(part, weights[2]) for part in far], axis=0)
        hidden = hidden_of(act)
        hiddens = [hidden] + [shift_chips(hidden, k) for k in steps]
        return dot(jnp.concatenate(hiddens, axis=1), down_all).astype(BF16)

    result = jnp.concatenate([project_in(*piece) for piece in gathered], axis=0)

    whole = jnp.zeros((tok_rows, CHIPS * chip_width), BF16)
    for block, k in zip(token_blocks, (0,) + steps):
        at = ((chip - k) & (CHIPS - 1)) * chip_width
        whole = lax.dynamic_update_slice_in_dim(whole, block, at, axis=1)
    shared_hidden = (
        jax.nn.silu(project_rows(whole, shared_gate)) * project_rows(whole, shared_up)
    ).astype(BF16)
    shared_part = dot(shared_hidden, shared_down).astype(BF16)
    result, shared_part = lax.optimization_barrier((result, shared_part))
    returned = exchange(result)

    shared = pick(chip, 0, shared_part, chip_width).astype(F32)
    for k in steps:
        shared = shared + shift_chips(pick(chip, -k, shared_part, chip_width), k).astype(F32)
    combine = jnp.where(hit, weight[:, None, :], 0.0).reshape(experts * half_cap, tok_rows)
    high = combine.astype(BF16)
    low = (combine - high.astype(F32)).astype(BF16)
    contract = (((0,), (0,)), ((), ()))
    total = shared + lax.dot_general(high, returned, contract, preferred_element_type=F32)
    total = total + lax.dot_general(low, returned, contract, preferred_element_type=F32)
    mine = lax.dynamic_slice_in_dim(total, core * width, width, axis=1)
    theirs = lax.dynamic_slice_in_dim(total, (1 - core) * width, width, axis=1)
    return (mine + swap_cores(theirs)).astype(BF16)


def solution(mesh):
    placed = (
        P("expert", "loop"),
        P("expert", None),
        P("expert", None),
        P("expert", "loop", None),
        P("expert", "loop", None),
        P("expert", "loop", None),
        P("loop", None),
        P("loop", None),
        P("loop", None),
    )
    return jax.shard_map(
        local, mesh=mesh, in_specs=placed, out_specs=P("expert", "loop"), check_vma=False
    )
```

time: 216 us -> 177 us (0.82); the launches traced: 213 us -> 177 us
  matrix products: 66.4 us -> 26.4 us
  waiting for transfers between devices: 71.8 us -> 54.5 us
  other arithmetic: 3 us -> 10.8 us
  starting transfers between devices: 55.4 us -> 60.2 us
  local copies, waits for them, and re-layouts: 16.2 us -> 20.9 us
  Pallas kernels: 0 us -> 3.25 us
    dot_general x46 -> x11, matrix products: 56 us -> 15.6 us  [project_rows(): lax.dot_general(rows, weight, (((1,), (1,)), ((), ())), preferred_element...]
    ppermute x21 -> x23, waiting for transfers between devices: 62.6 us -> 26.5 us  [shift_chips(): return lax.ppermute(value, 'loop', pairs)]
    all_to_all x2, waiting for transfers between devices: 7.87 us -> 26.2 us  [exchange(): lax.all_to_all(value, 'expert', split_axis=0, concat_axis=0, tiled=True)]
    another operation x0 -> x2, other arithmetic: none -> 7.48 us  [local(): jnp.stack([down_four, swap_cores(down_four)], axis=1)]
    ppermute x21 -> x23, starting transfers between devices: 21.5 us -> 28.9 us  [shift_chips(): return lax.ppermute(value, 'loop', pairs)]
    slice x1 -> x6, local copies, waits for them, and re-layouts: 1.37 us -> 5.13 us  [the longest x2 2.83 us: local(): pieces = [rows[:cut], rows[cut:]]]
    pallas_call x0 -> x1, Pallas kernels: none -> 3.25 us  [roll_features(): pl.pallas_call(roll_kernel, out_shape=jax.ShapeDtypeStruct((CHIPS, rows,...]
    dynamic_slice x2, local copies, waits for them, and re-layouts: 2.43 us -> 5.12 us  [pick(): lax.dynamic_slice_in_dim(array, (chip - step & CHIPS - 1) * width, width,...]
  transfers between devices with their start and end apart: 34 -> 30, of which waited for: 13 -> 10; matrix products, arithmetic and copies ran while one was open for 39% -> 21% of each run, Pallas kernels for 0% -> 2%
where the time goes in v2:
time: 177 us
  starting transfers between devices  60.2 us (34%)
  waiting for transfers between devices  54.5 us (31%)
  matrix products  26.4 us (15%)
  local copies, waits for them, and re-layouts  20.9 us (12%)
  other arithmetic  10.8 us (6%)
  Pallas kernels  3.25 us (2%)
    ppermute x23, starting transfers between devices, shift_chips(): return lax.ppermute(value, 'loop', pairs)  28.9 us
    ppermute x23, waiting for transfers between devices, shift_chips(): return lax.ppermute(value, 'loop', pairs)  26.5 us
    all_to_all x2, waiting for transfers between devices, exchange(): lax.all_to_all(value, 'expert', split_axis=0, concat_axis=0, tiled=True)  26.2 us
    all_to_all x2, starting transfers between devices, exchange(): lax.all_to_all(value, 'expert', split_axis=0, concat_axis=0, tiled=True)  20.6 us
    dot_general x11, matrix products, project_rows(): lax.dot_general(rows, weight, (((1,), (1,)), ((), ())), preferred_element...  15.6 us
    ppermute x5, starting transfers between devices, swap_cores(): return lax.ppermute(value, 'loop', [(i, i ^ 1) for i in range(2 * CHIPS)])  10.7 us
    unnamed x42, local copies, waits for them, and re-layouts  9.36 us
    dot_general x5, matrix products, dot(): return jnp.dot(left, right, preferred_element_type=F32)  8.58 us
  transfers between devices with their start and end apart: 30, of which 10 were waited for; matrix products, arithmetic and copies ran while one was open for 21% of the time, Pallas kernels for 2%

profile of v2, /device:TPU:1, one launch (start us, length us, event | category | flops | bytes accessed | tf_op | source)
XLA Modules:
  0.0 176.7 jit_solution(12311848454340545350)
XLA Ops:
  0.0 3.0 %dynamic-slice_bitcast_fusion = (bf16[192,1280]{1,0:T(8,128)(2,1)}, bf16[192,1280]{1,0:T(8,128)(2,1)}, bf16[192,1280]{1,0:T(8,128)(2,1)}, bf16[192,1280]{1,0:T(8,128)(2,1)}) fusion(bf16[1,192,5120]{2,1,0:T(8,128)(2,1)} %param.14, s32[]{:T(128)S(6)} %select_n.56, s32[]{:T(128)S(6)} %select_n.54, s32[]{:T(128)S(6)} %select_n.53, s32[]{:T(128)S(6)} %select_n.55), kind=kLoop, calls=%fused_computation.58 | loop fusion | bytes 3932176 | tf_op jit(solution)/shard_map/dynamic_slice | solution.py:35
  3.0 2.0 %collective-permute-start.1 = (bf16[192,1280]{1,0:T(8,128)(2,1)}, bf16[192,1280]{1,0:T(8,128)(2,1)}, u32[]{:S(2)}, u32[]{:S(2)}) collective-permute-start(bf16[192,1280]{1,0:T(8,128)(2,1)} %get-tuple-element.48), channel_id=1, source_target_pairs={{0,2},{1,3},{2,4},{3,5},{4,6},{5,7},{6,0},{7,1},{8,10},{9,11},{10,... | collective-permute-start | bytes 1474568 | tf_op jit(solution)/shard_map/ppermute | solution.py:23
  5.0 1.3 collective-permute-start.2
  6.3 1.7 collective-permute-start.3
  8.0 1.5 collective-permute-start
  11.4 1.6 convolution_convert_fusion.1
  12.9 11.2 %all-to-all-start = ((bf16[32,16,1280]{2,1,0:T(8,128)(2,1)}), bf16[32,16,1280]{2,1,0:T(8,128)(2,1)S(1)}, u32[]{:S(2)}, u32[]{:S(2)}) async-start(bf16[32,16,1280]{2,1,0:T(8,128)(2,1)} %bitcast.104), calls=%async_computation | async-start | bytes 2621440 | tf_op jit(solution)/shard_map/all_to_all | solution.py:101
  24.2 4.8 %collective-permute-done.3 = bf16[192,1280]{1,0:T(8,128)(2,1)} collective-permute-done((bf16[192,1280]{1,0:T(8,128)(2,1)}, bf16[192,1280]{1,0:T(8,128)(2,1)}, u32[]{:S(2)}, u32[]{:S(2)}) %collective-permute-start.3) | collective-permute-done | bytes 491552 | tf_op jit(solution)/shard_map/ppermute | solution.py:23
  28.9 1.5 collective-permute-start.4
  30.5 3.7 %fusion.90 = (bf16[4,1,192,1280]{3,2,1,0:T(8,128)(2,1)}, bf16[4,192,1280]{2,1,0:T(8,128)(2,1)}) fusion(bf16[1,192,1280]{2,1,0:T(8,128)(2,1)} %bitcast.15, bf16[1,192,1280]{2,1,0:T(8,128)(2,1)} %bitcast.14, bf16[1,192,1280]{2,1,0:T(8,128)(2,1)} %bitcast.13, bf16[1,192,1280]{2,1,0:T(8,128)(2,1)} %bitcast.108), kind=kLoop, calls=%fused_computation.113 | loop fusion | flops 2949120 | bytes 5898240 | tf_op jit(solution)/shard_map/stack | solution.py:110
  35.6 1.8 %collective-permute-start.8 = (bf16[128,1280]{1,0:T(8,128)(2,1)}, bf16[128,1280]{1,0:T(8,128)(2,1)S(1)}, u32[]{:S(2)}, u32[]{:S(2)}) collective-permute-start(bf16[128,1280]{1,0:T(8,128)(2,1)} %copy-done.7), channel_id=1, source_target_pairs={{0,6},{1,7},{2,0},{3,1},{4,2},{5,3},{6,4},{7,5},{8,14},{9,15},{10,... | collective-permute-start | bytes 983048 | tf_op jit(solution)/shard_map/ppermute | solution.py:23
  37.4 1.5 copy-done.2
  38.9 1.5 copy-done.3
  40.5 3.3 %shard_map.91 = bf16[4,768,1280]{2,1,0:T(8,128)(2,1)S(1)} custom-call(s32[1]{0:T(128)} %bitcast.5.chip_ref, bf16[192,5120]{1,0:T(8,128)(2,1)S(1)} %bitcast.99, bf16[192,5120]{1,0:T(8,128)(2,1)} %collective-permute-done.4.refs_1_, bf16[192,5120]{1,0:T(8,128)(2,1)S(1)} %bitcast.101, bf16[192,5120]{1,0:T(8,128)(2,1)} %collective-permute-done.5.refs_3_), custom_call_target="tpu_custom_call" | custom-call | tf_op jit(solution)/shard_map/pallas_call | solution.py:53
  43.8 3.1 %copy-done.1 = bf16[4,768,1280]{2,1,0:T(8,128)(2,1)} copy-done((bf16[4,768,1280]{2,1,0:T(8,128)(2,1)}, bf16[4,768,1280]{2,1,0:T(8,128)(2,1)S(1)}, u32[]{:S(2)}) %copy-start.1) | copy-done | bytes 7864344
  46.8 3.8 %pad_maximum_fusion = bf16[4,2,192,1280]{3,2,1,0:T(8,128)(2,1)} fusion(bf16[4,1,192,1280]{3,2,1,0:T(8,128)(2,1)} %bitcast.18, bf16[4,1,192,1280]{3,2,1,0:T(8,128)(2,1)S(1)} %copy-done.4), kind=kLoop, calls=%fused_computation.1 | loop fusion | flops 1966080 | bytes 7864320 | tf_op jit(solution)/shard_map/stack | solution.py:110
  52.6 3.9 %all-to-all-done = bf16[32,16,1280]{2,1,0:T(8,128)(2,1)S(1)} async-done(((bf16[32,16,1280]{2,1,0:T(8,128)(2,1)}), bf16[32,16,1280]{2,1,0:T(8,128)(2,1)S(1)}, u32[]{:S(2)}, u32[]{:S(2)}) %all-to-all-start) | async-done | bytes 1310752 | tf_op jit(solution)/shard_map/all_to_all | solution.py:101
  56.5 1.0 slice.48
  57.9 2.3 %collective-permute-start.11 = (bf16[384,1280]{1,0:T(8,128)(2,1)}, bf16[384,1280]{1,0:T(8,128)(2,1)}, u32[]{:S(2)}, u32[]{:S(2)}) collective-permute-start(bf16[384,1280]{1,0:T(8,128)(2,1)} %slice.48), channel_id=1, source_target_pairs={{0,6},{1,7},{2,0},{3,1},{4,2},{5,3},{6,4},{7,5},{8,14},{9,15},{10,... | collective-permute-start | bytes 2949128 | tf_op jit(solution)/shard_map/ppermute | solution.py:23
  60.5 1.8 %slice.49 = bf16[128,1280]{1,0:T(8,128)(2,1)} slice(bf16[512,1280]{1,0:T(8,128)(2,1)} %bitcast.103), slice={[384:512], [0:1280]} | slice | bytes 655360 | tf_op jit(solution)/shard_map/slice | solution.py:119
  62.3 1.0 constant_dynamic-update-slice_fusion
  64.0 4.5 %convolution_convert_fusion = bf16[128,5120]{1,0:T(8,128)(2,1)} fusion(bf16[192,5120]{1,0:T(8,128)(2,1)S(1)} %copy-done, bf16[128,5120]{1,0:T(8,128)(2,1)S(1)} %constant_dynamic-update-slice_fusion, bf16[192,5120]{1,0:T(8,128)(2,1)} %param.16, f32[128,192]{0,1:T(8,128)S(1)} %fusion.91), kind=kOutput, calls=%fused_computation | convolution fusion | flops 504119296 | bytes 6651904 | tf_op jit(solution)/shard_map/dot_general | solution.py:27
  68.5 11.6 %collective-permute-done.10 = bf16[384,1280]{1,0:T(8,128)(2,1)} collective-permute-done((bf16[384,1280]{1,0:T(8,128)(2,1)}, bf16[384,1280]{1,0:T(8,128)(2,1)}, u32[]{:S(2)}, u32[]{:S(2)}) %collective-permute-start.10) | collective-permute-done | bytes 983072 | tf_op jit(solution)/shard_map/ppermute | solution.py:23
  80.1 2.7 %collective-permute-start.18 = (bf16[128,1280]{1,0:T(8,128)(2,1)}, bf16[128,1280]{1,0:T(8,128)(2,1)S(1)}, u32[]{:S(2)}, u32[]{:S(2)}) collective-permute-start(bf16[128,1280]{1,0:T(8,128)(2,1)} %slice.49), channel_id=1, source_target_pairs={{0,6},{1,7},{2,0},{3,1},{4,2},{5,3},{6,4},{7,5},{8,14},{9,15},{10,... | collective-permute-start | bytes 983048 | tf_op jit(solution)/shard_map/ppermute | solution.py:23
  82.8 1.1 slice.53
  84.0 1.2 slice.55
  85.2 2.7 %collective-permute-start.13 = (bf16[192,1280]{1,0:T(8,128)(2,1)S(1)}, bf16[192,1280]{1,0:T(8,128)(2,1)S(1)}, u32[]{:S(2)}, u32[]{:S(2)}) collective-permute-start(bf16[192,1280]{1,0:T(8,128)(2,1)S(1)} %slice.55), channel_id=1, source_target_pairs={{0,6},{1,7},{2,0},{3,1},{4,2},{5,3},{6,4},{7,5},{8,14},{9,15},{10,... | collective-permute-start | bytes 1474568 | tf_op jit(solution)/shard_map/ppermute | solution.py:23
  87.9 2.8 %fusion.14 = f32[384,768]{1,0:T(8,128)S(1)} fusion(bf16[384,1280]{1,0:T(8,128)(2,1)} %collective-permute-done.10, bf16[4,768,1280]{2,1,0:T(8,128)(2,1)} %copy-done.1), kind=kOutput, calls=%fused_computation.22 | convolution fusion | flops 754974720 | bytes 4128768 | tf_op jit(solution)/shard_map/dot_general | solution.py:31
  90.7 3.0 %fusion.10 = f32[384,768]{1,0:T(8,128)S(1)} fusion(bf16[384,1280]{1,0:T(8,128)(2,1)} %collective-permute-done.11, bf16[4,768,1280]{2,1,0:T(8,128)(2,1)} %copy-done.1), kind=kOutput, calls=%fused_computation.18 | convolution fusion | flops 754974720 | bytes 4128768 | tf_op jit(solution)/shard_map/dot_general | solution.py:31
  93.9 2.7 %collective-permute-start.20 = (bf16[64,1280]{1,0:T(8,128)(2,1)S(1)}, bf16[64,1280]{1,0:T(8,128)(2,1)S(1)}, u32[]{:S(2)}, u32[]{:S(2)}) collective-permute-start(bf16[64,1280]{1,0:T(8,128)(2,1)S(1)} %slice.65), channel_id=1, source_target_pairs={{0,6},{1,7},{2,0},{3,1},{4,2},{5,3},{6,4},{7,5},{8,14},{9,15},{10,... | collective-permute-start | bytes 491528 | tf_op jit(solution)/shard_map/ppermute | solution.py:23
  96.6 2.3 %fusion.12 = f32[128,768]{1,0:T(8,128)S(1)} fusion(bf16[128,1280]{1,0:T(8,128)(2,1)S(1)} %collective-permute-done.17, bf16[4,768,1280]{2,1,0:T(8,128)(2,1)} %copy-done.1), kind=kOutput, calls=%fused_computation.20 | convolution fusion | flops 251658240 | bytes 2686976 | tf_op jit(solution)/shard_map/dot_general | solution.py:31
  101.4 2.2 %fusion.32 = f32[384,768]{1,0:T(8,128)S(1)} fusion(f32[384,768]{1,0:T(8,128)S(1)} %fusion.10, f32[384,768]{1,0:T(8,128)S(1)} %fusion.14, bf16[384,1280]{1,0:T(8,128)(2,1)} %slice.48, bf16[4,768,1280]{2,1,0:T(8,128)(2,1)S(1)} %bitcast.97, f32[192,768]{1,0:T(8,128)S(1)} %fusion.4, f32[192,768]{1,0:T(8,128)S(1)} %fusion.6), kind=kOutput, calls=%fused_computation.36 | convolution fusion | flops 756154368 | bytes 7667712 | tf_op jit(solution)/shard_map/dot_general | solution.py:31
  106.1 2.7 %collective-permute-start.22 = (bf16[128,384]{1,0:T(8,128)(2,1)S(1)}, bf16[128,384]{1,0:T(8,128)(2,1)S(1)}, u32[]{:S(2)}, u32[]{:S(2)}) collective-permute-start(bf16[128,384]{1,0:T(8,128)(2,1)S(1)} %fusion.66), channel_id=1, source_target_pairs={{0,6},{1,7},{2,0},{3,1},{4,2},{5,3},{6,4},{7,5},{8,14},{9,15},{10,... | collective-permute-start | bytes 294920 | tf_op jit(solution)/shard_map/ppermute | solution.py:23
  109.2 0.9 collective-permute-start.14
  110.1 1.8 %collective-permute-start.15 = (bf16[384,384]{1,0:T(8,128)(2,1)S(1)}, bf16[384,384]{1,0:T(8,128)(2,1)S(1)}, u32[]{:S(2)}, u32[]{:S(2)}) collective-permute-start(bf16[384,384]{1,0:T(8,128)(2,1)S(1)} %fusion.56), channel_id=1, source_target_pairs={{0,6},{1,7},{2,0},{3,1},{4,2},{5,3},{6,4},{7,5},{8,14},{9,15},{10,... | collective-permute-start | bytes 884744 | tf_op jit(solution)/shard_map/ppermute | solution.py:23
  112.0 1.5 collective-permute-start.16
  114.5 3.4 %collective-permute-done.14 = bf16[384,384]{1,0:T(8,128)(2,1)S(1)} collective-permute-done((bf16[384,384]{1,0:T(8,128)(2,1)S(1)}, bf16[384,384]{1,0:T(8,128)(2,1)S(1)}, u32[]{:S(2)}, u32[]{:S(2)}) %collective-permute-start.14) | collective-permute-done | bytes 294944 | tf_op jit(solution)/shard_map/ppermute | solution.py:23
  117.9 5.8 %collective-permute-done.16 = bf16[384,384]{1,0:T(8,128)(2,1)S(1)} collective-permute-done((bf16[384,384]{1,0:T(8,128)(2,1)S(1)}, bf16[384,384]{1,0:T(8,128)(2,1)S(1)}, u32[]{:S(2)}, u32[]{:S(2)}) %collective-permute-start.16) | collective-permute-done | bytes 294944 | tf_op jit(solution)/shard_map/ppermute | solution.py:23
  123.7 1.7 convolution_convert_fusion.2
  125.3 1.2 pad_maximum_fusion.2
  126.5 9.4 %all-to-all-start.1 = ((bf16[32,16,1280]{2,1,0:T(8,128)(2,1)}), bf16[32,16,1280]{2,1,0:T(8,128)(2,1)S(1)}, u32[]{:S(2)}, u32[]{:S(2)}) async-start(bf16[32,16,1280]{2,1,0:T(8,128)(2,1)} %bitcast.105), calls=%async_computation.1 | async-start | bytes 2621440 | tf_op jit(solution)/shard_map/all_to_all | solution.py:101
  136.0 2.2 %constant_dynamic-slice_fusion.3 = (bf16[128,1280]{1,0:T(8,128)(2,1)}, bf16[128,1280]{1,0:T(8,128)(2,1)}, bf16[128,1280]{1,0:T(8,128)(2,1)}) fusion(bf16[128,5120]{1,0:T(8,128)(2,1)} %convolution_convert_fusion, s32[]{:T(128)S(6)} %select_n.54, s32[]{:T(128)S(6)} %select_n.56, s32[]{:T(128)S(6)} %select_n.55), kind=kLoop, calls=%fused_computation.102 | loop fusion | bytes 1966092 | tf_op jit(solution)/shard_map/dynamic_slice | solution.py:35
  138.4 2.4 %collective-permute-start.25 = (bf16[128,1280]{1,0:T(8,128)(2,1)}, bf16[128,1280]{1,0:T(8,128)(2,1)}, u32[]{:S(2)}, u32[]{:S(2)}) collective-permute-start(bf16[128,1280]{1,0:T(8,128)(2,1)} %get-tuple-element.53), channel_id=1, source_target_pairs={{0,6},{1,7},{2,0},{3,1},{4,2},{5,3},{6,4},{7,5},{8,14},{9,15},{10,... | collective-permute-start | bytes 983048 | tf_op jit(solution)/shard_map/ppermute | solution.py:23
  141.2 22.3 %all-to-all-done.1 = bf16[32,16,1280]{2,1,0:T(8,128)(2,1)S(1)} async-done(((bf16[32,16,1280]{2,1,0:T(8,128)(2,1)}), bf16[32,16,1280]{2,1,0:T(8,128)(2,1)S(1)}, u32[]{:S(2)}, u32[]{:S(2)}) %all-to-all-start.1) | async-done | bytes 1310752 | tf_op jit(solution)/shard_map/all_to_all | solution.py:101
  163.9 1.8 add_add_fusion
  166.6 7.1 %collective-permute-start.27 = (f32[128,640]{1,0:T(8,128)S(1)}, f32[128,640]{1,0:T(8,128)S(1)}, u32[]{:S(2)}, u32[]{:S(2)}) collective-permute-start(f32[128,640]{1,0:T(8,128)S(1)} %constant_dynamic-slice_fusion), channel_id=1, source_target_pairs={{0,1},{1,0},{2,3},{3,2},{4,5},{5,4},{6,7},{7,6},{8,9},{9,8},{10,11... | collective-permute-start | bytes 983048 | tf_op jit(solution)/shard_map/ppermute | solution.py:14
  173.7 1.3 collective-permute-done.27
  175.0 1.7 add_convert_fusion
  (101 shorter events, 15.0 us)
Async XLA Ops:
  0.0 64.0 %copy-start = (bf16[192,5120]{1,0:T(8,128)(2,1)S(1)}, bf16[192,5120]{1,0:T(8,128)(2,1)}, u32[]{:S(2)}) copy-start(bf16[192,5120]{1,0:T(8,128)(2,1)} %param.17) | copy-start | bytes 5898244
  0.0 8.0 %copy-start.16 = (bf16[128,640]{1,0:T(8,128)(2,1)S(1)}, bf16[128,640]{1,0:T(8,128)(2,1)}, u32[]{:S(2)}) copy-start(bf16[128,640]{1,0:T(8,128)(2,1)} %param.9) | copy-start | bytes 491524
  0.0 9.6 %copy-start.17 = (s32[128,6]{0,1:T(8,128)S(1)}, s32[128,6]{0,1:T(8,128)}, u32[]{:S(2)}) copy-start(s32[128,6]{0,1:T(8,128)} %param.10) | copy-start | bytes 9220
  3.0 21.2 %collective-permute-start.1 = (bf16[192,1280]{1,0:T(8,128)(2,1)}, bf16[192,1280]{1,0:T(8,128)(2,1)}, u32[]{:S(2)}, u32[]{:S(2)}) collective-permute-start(bf16[192,1280]{1,0:T(8,128)(2,1)} %get-tuple-element.48), channel_id=1, source_target_pairs={{0,2},{1,3},{2,4},{3,5},{4,6},{5,7},{6,0},{7,1},{8,10},{9,11},{10,... | collective-permute-start | bytes 1474568 | tf_op jit(solution)/shard_map/ppermute | solution.py:23
  5.0 19.2 %collective-permute-start.2 = (bf16[192,1280]{1,0:T(8,128)(2,1)}, bf16[192,1280]{1,0:T(8,128)(2,1)}, u32[]{:S(2)}, u32[]{:S(2)}) collective-permute-start(bf16[192,1280]{1,0:T(8,128)(2,1)} %get-tuple-element.50), channel_id=1, source_target_pairs={{0,6},{1,7},{2,0},{3,1},{4,2},{5,3},{6,4},{7,5},{8,14},{9,15},{10,... | collective-permute-start | bytes 1474568 | tf_op jit(solution)/shard_map/ppermute | solution.py:23
  6.3 22.7 %collective-permute-start.3 = (bf16[192,1280]{1,0:T(8,128)(2,1)}, bf16[192,1280]{1,0:T(8,128)(2,1)}, u32[]{:S(2)}, u32[]{:S(2)}) collective-permute-start(bf16[192,1280]{1,0:T(8,128)(2,1)} %get-tuple-element.47), channel_id=1, source_target_pairs={{0,4},{1,5},{2,6},{3,7},{4,0},{5,1},{6,2},{7,3},{8,12},{9,13},{10,... | collective-permute-start | bytes 1474568 | tf_op jit(solution)/shard_map/ppermute | solution.py:23
  8.0 2.5 %collective-permute-start = (bf16[128,640]{1,0:T(8,128)(2,1)S(1)}, bf16[128,640]{1,0:T(8,128)(2,1)S(1)}, u32[]{:S(2)}, u32[]{:S(2)}) collective-permute-start(bf16[128,640]{1,0:T(8,128)(2,1)S(1)} %copy-done.16), channel_id=1, source_target_pairs={{0,1},{1,0},{2,3},{3,2},{4,5},{5,4},{6,7},{7,6},{8,9},{9,8},{10,11... | collective-permute-start | bytes 491528 | tf_op jit(solution)/shard_map/ppermute | solution.py:14
  12.9 43.6 %all-to-all-start = ((bf16[32,16,1280]{2,1,0:T(8,128)(2,1)}), bf16[32,16,1280]{2,1,0:T(8,128)(2,1)S(1)}, u32[]{:S(2)}, u32[]{:S(2)}) async-start(bf16[32,16,1280]{2,1,0:T(8,128)(2,1)} %bitcast.104), calls=%async_computation | async-start | bytes 2621440 | tf_op jit(solution)/shard_map/all_to_all | solution.py:101
  28.9 8.4 %collective-permute-start.4 = (bf16[192,5120]{1,0:T(8,128)(2,1)}, bf16[192,5120]{1,0:T(8,128)(2,1)}, u32[]{:S(2)}, u32[]{:S(2)}) collective-permute-start(bf16[192,5120]{1,0:T(8,128)(2,1)} %bitcast.98), channel_id=1, source_target_pairs={{0,1},{1,0},{2,3},{3,2},{4,5},{5,4},{6,7},{7,6},{8,9},{9,8},{10,11... | collective-permute-start | bytes 5898248 | tf_op jit(solution)/shard_map/ppermute | solution.py:14
  30.5 6.9 %collective-permute-start.5 = (bf16[192,5120]{1,0:T(8,128)(2,1)}, bf16[192,5120]{1,0:T(8,128)(2,1)}, u32[]{:S(2)}, u32[]{:S(2)}) collective-permute-start(bf16[192,5120]{1,0:T(8,128)(2,1)} %bitcast.100), channel_id=1, source_target_pairs={{0,1},{1,0},{2,3},{3,2},{4,5},{5,4},{6,7},{7,6},{8,9},{9,8},{10,11... | collective-permute-start | bytes 5898248 | tf_op jit(solution)/shard_map/ppermute | solution.py:14
  34.2 12.6 %collective-permute-start.6 = (bf16[4,192,1280]{2,1,0:T(8,128)(2,1)}, bf16[4,192,1280]{2,1,0:T(8,128)(2,1)}, u32[]{:S(2)}, u32[]{:S(2)}) collective-permute-start(bf16[4,192,1280]{2,1,0:T(8,128)(2,1)} %get-tuple-element.46), channel_id=1, source_target_pairs={{0,1},{1,0},{2,3},{3,2},{4,5},{5,4},{6,7},{7,6},{8,9},{9,8},{10,11... | collective-permute-start | bytes 5898248 | tf_op jit(solution)/shard_map/ppermute | solution.py:14
  34.7 15.9 %collective-permute-start.7 = (bf16[128,1280]{1,0:T(8,128)(2,1)}, bf16[128,1280]{1,0:T(8,128)(2,1)S(1)}, u32[]{:S(2)}, u32[]{:S(2)}) collective-permute-start(bf16[128,1280]{1,0:T(8,128)(2,1)} %copy-done.7), channel_id=1, source_target_pairs={{0,2},{1,3},{2,4},{3,5},{4,6},{5,7},{6,0},{7,1},{8,10},{9,11},{10,... | collective-permute-start | bytes 983048 | tf_op jit(solution)/shard_map/ppermute | solution.py:23
  35.6 15.0 %collective-permute-start.8 = (bf16[128,1280]{1,0:T(8,128)(2,1)}, bf16[128,1280]{1,0:T(8,128)(2,1)S(1)}, u32[]{:S(2)}, u32[]{:S(2)}) collective-permute-start(bf16[128,1280]{1,0:T(8,128)(2,1)} %copy-done.7), channel_id=1, source_target_pairs={{0,6},{1,7},{2,0},{3,1},{4,2},{5,3},{6,4},{7,5},{8,14},{9,15},{10,... | collective-permute-start | bytes 983048 | tf_op jit(solution)/shard_map/ppermute | solution.py:23
  37.4 15.2 %collective-permute-start.9 = (bf16[128,1280]{1,0:T(8,128)(2,1)}, bf16[128,1280]{1,0:T(8,128)(2,1)}, u32[]{:S(2)}, u32[]{:S(2)}) collective-permute-start(bf16[128,1280]{1,0:T(8,128)(2,1)} %copy-done.7), channel_id=1, source_target_pairs={{0,4},{1,5},{2,6},{3,7},{4,0},{5,1},{6,2},{7,3},{8,12},{9,13},{10,... | collective-permute-start | bytes 983048 | tf_op jit(solution)/shard_map/ppermute | solution.py:23
  37.4 1.5 copy-start.2
  38.9 1.5 copy-start.3
  40.5 6.3 %copy-start.4 = (bf16[4,1,192,1280]{3,2,1,0:T(8,128)(2,1)S(1)}, bf16[4,1,192,1280]{3,2,1,0:T(8,128)(2,1)}, u32[]{:S(2)}) copy-start(bf16[4,1,192,1280]{3,2,1,0:T(8,128)(2,1)} %get-tuple-element.45) | copy-start | bytes 5898244
  43.7 3.1 %copy-start.1 = (bf16[4,768,1280]{2,1,0:T(8,128)(2,1)}, bf16[4,768,1280]{2,1,0:T(8,128)(2,1)S(1)}, u32[]{:S(2)}) copy-start(bf16[4,768,1280]{2,1,0:T(8,128)(2,1)S(1)} %shard_map.91) | copy-start | bytes 23592964
  56.5 1.4 copy-start.5
  56.5 3.8 %copy-start.8 = (bf16[128,1280]{1,0:T(8,128)(2,1)S(1)}, bf16[128,1280]{1,0:T(8,128)(2,1)}, u32[]{:S(2)}) copy-start(bf16[128,1280]{1,0:T(8,128)(2,1)} %copy-done.7) | copy-start | bytes 983044
  56.5 3.9 %copy-start.13 = (bf16[128,1280]{1,0:T(8,128)(2,1)S(1)}, bf16[128,1280]{1,0:T(8,128)(2,1)}, u32[]{:S(2)}) copy-start(bf16[128,1280]{1,0:T(8,128)(2,1)} %copy-done.12) | copy-start | bytes 983044
  56.5 3.9 %copy-start.15 = (bf16[128,1280]{1,0:T(8,128)(2,1)S(1)}, bf16[128,1280]{1,0:T(8,128)(2,1)}, u32[]{:S(2)}) copy-start(bf16[128,1280]{1,0:T(8,128)(2,1)} %copy-done.14) | copy-start | bytes 983044
  57.5 22.6 %collective-permute-start.10 = (bf16[384,1280]{1,0:T(8,128)(2,1)}, bf16[384,1280]{1,0:T(8,128)(2,1)}, u32[]{:S(2)}, u32[]{:S(2)}) collective-permute-start(bf16[384,1280]{1,0:T(8,128)(2,1)} %slice.48), channel_id=1, source_target_pairs={{0,2},{1,3},{2,4},{3,5},{4,6},{5,7},{6,0},{7,1},{8,10},{9,11},{10,... | collective-permute-start | bytes 2949128 | tf_op jit(solution)/shard_map/ppermute | solution.py:23
  57.9 22.2 %collective-permute-start.11 = (bf16[384,1280]{1,0:T(8,128)(2,1)}, bf16[384,1280]{1,0:T(8,128)(2,1)}, u32[]{:S(2)}, u32[]{:S(2)}) collective-permute-start(bf16[384,1280]{1,0:T(8,128)(2,1)} %slice.48), channel_id=1, source_target_pairs={{0,6},{1,7},{2,0},{3,1},{4,2},{5,3},{6,4},{7,5},{8,14},{9,15},{10,... | collective-permute-start | bytes 2949128 | tf_op jit(solution)/shard_map/ppermute | solution.py:23
  60.3 3.0 %copy-start.10 = (bf16[192,5120]{1,0:T(8,128)(2,1)S(1)}, bf16[192,5120]{1,0:T(8,128)(2,1)}, u32[]{:S(2)}) copy-start(bf16[192,5120]{1,0:T(8,128)(2,1)} %param.15) | copy-start | bytes 5898244
  80.1 13.6 %collective-permute-start.17 = (bf16[128,1280]{1,0:T(8,128)(2,1)}, bf16[128,1280]{1,0:T(8,128)(2,1)S(1)}, u32[]{:S(2)}, u32[]{:S(2)}) collective-permute-start(bf16[128,1280]{1,0:T(8,128)(2,1)} %slice.49), channel_id=1, source_target_pairs={{0,2},{1,3},{2,4},{3,5},{4,6},{5,7},{6,0},{7,1},{8,10},{9,11},{10,... | collective-permute-start | bytes 983048 | tf_op jit(solution)/shard_map/ppermute | solution.py:23
  80.1 13.7 %collective-permute-start.18 = (bf16[128,1280]{1,0:T(8,128)(2,1)}, bf16[128,1280]{1,0:T(8,128)(2,1)S(1)}, u32[]{:S(2)}, u32[]{:S(2)}) collective-permute-start(bf16[128,1280]{1,0:T(8,128)(2,1)} %slice.49), channel_id=1, source_target_pairs={{0,6},{1,7},{2,0},{3,1},{4,2},{5,3},{6,4},{7,5},{8,14},{9,15},{10,... | collective-permute-start | bytes 983048 | tf_op jit(solution)/shard_map/ppermute | solution.py:23
  83.8 15.9 %collective-permute-start.12 = (bf16[192,1280]{1,0:T(8,128)(2,1)S(1)}, bf16[192,1280]{1,0:T(8,128)(2,1)S(1)}, u32[]{:S(2)}, u32[]{:S(2)}) collective-permute-start(bf16[192,1280]{1,0:T(8,128)(2,1)S(1)} %slice.53), channel_id=1, source_target_pairs={{0,2},{1,3},{2,4},{3,5},{4,6},{5,7},{6,0},{7,1},{8,10},{9,11},{10,... | collective-permute-start | bytes 1474568 | tf_op jit(solution)/shard_map/ppermute | solution.py:23
  83.9 15.0 %slice-start = ((s8[7864320]{0:T(1024)(128)(4,1)}), s8[4194304]{0:T(1024)(128)(4,1)S(1)}, s32[]{:S(2)}) async-start(s8[7864320]{0:T(1024)(128)(4,1)} %bitcast.96), calls=%async_computation.2 | async-start | bytes 8388608
  85.2 15.4 %collective-permute-start.13 = (bf16[192,1280]{1,0:T(8,128)(2,1)S(1)}, bf16[192,1280]{1,0:T(8,128)(2,1)S(1)}, u32[]{:S(2)}, u32[]{:S(2)}) collective-permute-start(bf16[192,1280]{1,0:T(8,128)(2,1)S(1)} %slice.55), channel_id=1, source_target_pairs={{0,6},{1,7},{2,0},{3,1},{4,2},{5,3},{6,4},{7,5},{8,14},{9,15},{10,... | collective-permute-start | bytes 1474568 | tf_op jit(solution)/shard_map/ppermute | solution.py:23
  90.7 8.2 %slice-start.1 = ((s8[7864320]{0:T(1024)(128)(4,1)}), s8[3670016]{0:T(1024)(128)(4,1)S(1)}, s32[]{:S(2)}) async-start(s8[7864320]{0:T(1024)(128)(4,1)} %bitcast.96), calls=%async_computation.3 | async-start | bytes 7340032
  93.7 9.8 %collective-permute-start.19 = (bf16[64,1280]{1,0:T(8,128)(2,1)S(1)}, bf16[64,1280]{1,0:T(8,128)(2,1)S(1)}, u32[]{:S(2)}, u32[]{:S(2)}) collective-permute-start(bf16[64,1280]{1,0:T(8,128)(2,1)S(1)} %slice.64), channel_id=1, source_target_pairs={{0,2},{1,3},{2,4},{3,5},{4,6},{5,7},{6,0},{7,1},{8,10},{9,11},{10,... | collective-permute-start | bytes 491528 | tf_op jit(solution)/shard_map/ppermute | solution.py:23
  93.9 10.5 %collective-permute-start.20 = (bf16[64,1280]{1,0:T(8,128)(2,1)S(1)}, bf16[64,1280]{1,0:T(8,128)(2,1)S(1)}, u32[]{:S(2)}, u32[]{:S(2)}) collective-permute-start(bf16[64,1280]{1,0:T(8,128)(2,1)S(1)} %slice.65), channel_id=1, source_target_pairs={{0,6},{1,7},{2,0},{3,1},{4,2},{5,3},{6,4},{7,5},{8,14},{9,15},{10,... | collective-permute-start | bytes 491528 | tf_op jit(solution)/shard_map/ppermute | solution.py:23
  103.6 1.5 copy-start.11
  105.1 8.7 %copy-start.6 = (bf16[4,2,192,1280]{3,2,1,0:T(8,128)(2,1)S(1)}, bf16[4,2,192,1280]{3,2,1,0:T(8,128)(2,1)}, u32[]{:S(2)}) copy-start(bf16[4,2,192,1280]{3,2,1,0:T(8,128)(2,1)} %pad_maximum_fusion) | copy-start | bytes 11796484
  106.0 6.0 %collective-permute-start.21 = (bf16[128,384]{1,0:T(8,128)(2,1)S(1)}, bf16[128,384]{1,0:T(8,128)(2,1)S(1)}, u32[]{:S(2)}, u32[]{:S(2)}) collective-permute-start(bf16[128,384]{1,0:T(8,128)(2,1)S(1)} %fusion.66), channel_id=1, source_target_pairs={{0,2},{1,3},{2,4},{3,5},{4,6},{5,7},{6,0},{7,1},{8,10},{9,11},{10,... | collective-permute-start | bytes 294920 | tf_op jit(solution)/shard_map/ppermute | solution.py:23
  106.1 7.4 %collective-permute-start.22 = (bf16[128,384]{1,0:T(8,128)(2,1)S(1)}, bf16[128,384]{1,0:T(8,128)(2,1)S(1)}, u32[]{:S(2)}, u32[]{:S(2)}) collective-permute-start(bf16[128,384]{1,0:T(8,128)(2,1)S(1)} %fusion.66), channel_id=1, source_target_pairs={{0,6},{1,7},{2,0},{3,1},{4,2},{5,3},{6,4},{7,5},{8,14},{9,15},{10,... | collective-permute-start | bytes 294920 | tf_op jit(solution)/shard_map/ppermute | solution.py:23
  108.7 5.1 %collective-permute-start.23 = (bf16[128,384]{1,0:T(8,128)(2,1)S(1)}, bf16[128,384]{1,0:T(8,128)(2,1)S(1)}, u32[]{:S(2)}, u32[]{:S(2)}) collective-permute-start(bf16[128,384]{1,0:T(8,128)(2,1)S(1)} %fusion.66), channel_id=1, source_target_pairs={{0,4},{1,5},{2,6},{3,7},{4,0},{5,1},{6,2},{7,3},{8,12},{9,13},{10,... | collective-permute-start | bytes 294920 | tf_op jit(solution)/shard_map/ppermute | solution.py:23
  109.2 8.7 %collective-permute-start.14 = (bf16[384,384]{1,0:T(8,128)(2,1)S(1)}, bf16[384,384]{1,0:T(8,128)(2,1)S(1)}, u32[]{:S(2)}, u32[]{:S(2)}) collective-permute-start(bf16[384,384]{1,0:T(8,128)(2,1)S(1)} %fusion.56), channel_id=1, source_target_pairs={{0,2},{1,3},{2,4},{3,5},{4,6},{5,7},{6,0},{7,1},{8,10},{9,11},{10,... | collective-permute-start | bytes 884744 | tf_op jit(solution)/shard_map/ppermute | solution.py:23
  110.1 7.8 %collective-permute-start.15 = (bf16[384,384]{1,0:T(8,128)(2,1)S(1)}, bf16[384,384]{1,0:T(8,128)(2,1)S(1)}, u32[]{:S(2)}, u32[]{:S(2)}) collective-permute-start(bf16[384,384]{1,0:T(8,128)(2,1)S(1)} %fusion.56), channel_id=1, source_target_pairs={{0,6},{1,7},{2,0},{3,1},{4,2},{5,3},{6,4},{7,5},{8,14},{9,15},{10,... | collective-permute-start | bytes 884744 | tf_op jit(solution)/shard_map/ppermute | solution.py:23
  112.0 11.7 %collective-permute-start.16 = (bf16[384,384]{1,0:T(8,128)(2,1)S(1)}, bf16[384,384]{1,0:T(8,128)(2,1)S(1)}, u32[]{:S(2)}, u32[]{:S(2)}) collective-permute-start(bf16[384,384]{1,0:T(8,128)(2,1)S(1)} %fusion.56), channel_id=1, source_target_pairs={{0,4},{1,5},{2,6},{3,7},{4,0},{5,1},{6,2},{7,3},{8,12},{9,13},{10,... | collective-permute-start | bytes 884744 | tf_op jit(solution)/shard_map/ppermute | solution.py:23
  126.5 14.6 %copy-start.18 = (f32[128,6]{0,1:T(8,128)S(1)}, f32[128,6]{0,1:T(8,128)}, u32[]{:S(2)}) copy-start(f32[128,6]{0,1:T(8,128)} %param.11) | copy-start | bytes 9220
  126.5 36.9 %all-to-all-start.1 = ((bf16[32,16,1280]{2,1,0:T(8,128)(2,1)}), bf16[32,16,1280]{2,1,0:T(8,128)(2,1)S(1)}, u32[]{:S(2)}, u32[]{:S(2)}) async-start(bf16[32,16,1280]{2,1,0:T(8,128)(2,1)} %bitcast.105), calls=%async_computation.1 | async-start | bytes 2621440 | tf_op jit(solution)/shard_map/all_to_all | solution.py:101
  138.1 25.8 %collective-permute-start.24 = (bf16[128,1280]{1,0:T(8,128)(2,1)}, bf16[128,1280]{1,0:T(8,128)(2,1)}, u32[]{:S(2)}, u32[]{:S(2)}) collective-permute-start(bf16[128,1280]{1,0:T(8,128)(2,1)} %get-tuple-element.51), channel_id=1, source_target_pairs={{0,2},{1,3},{2,4},{3,5},{4,6},{5,7},{6,0},{7,1},{8,10},{9,11},{10,... | collective-permute-start | bytes 983048 | tf_op jit(solution)/shard_map/ppermute | solution.py:23
  138.4 25.5 %collective-permute-start.25 = (bf16[128,1280]{1,0:T(8,128)(2,1)}, bf16[128,1280]{1,0:T(8,128)(2,1)}, u32[]{:S(2)}, u32[]{:S(2)}) collective-permute-start(bf16[128,1280]{1,0:T(8,128)(2,1)} %get-tuple-element.53), channel_id=1, source_target_pairs={{0,6},{1,7},{2,0},{3,1},{4,2},{5,3},{6,4},{7,5},{8,14},{9,15},{10,... | collective-permute-start | bytes 983048 | tf_op jit(solution)/shard_map/ppermute | solution.py:23
  140.8 23.1 %collective-permute-start.26 = (bf16[128,1280]{1,0:T(8,128)(2,1)}, bf16[128,1280]{1,0:T(8,128)(2,1)}, u32[]{:S(2)}, u32[]{:S(2)}) collective-permute-start(bf16[128,1280]{1,0:T(8,128)(2,1)} %get-tuple-element.52), channel_id=1, source_target_pairs={{0,4},{1,5},{2,6},{3,7},{4,0},{5,1},{6,2},{7,3},{8,12},{9,13},{10,... | collective-permute-start | bytes 983048 | tf_op jit(solution)/shard_map/ppermute | solution.py:23
  165.7 0.9 copy-start.9
  166.6 8.4 %collective-permute-start.27 = (f32[128,640]{1,0:T(8,128)S(1)}, f32[128,640]{1,0:T(8,128)S(1)}, u32[]{:S(2)}, u32[]{:S(2)}) collective-permute-start(f32[128,640]{1,0:T(8,128)S(1)} %constant_dynamic-slice_fusion), channel_id=1, source_target_pairs={{0,1},{1,0},{2,3},{3,2},{4,5},{5,4},{6,7},{7,6},{8,9},{9,8},{10,11... | collective-permute-start | bytes 983048 | tf_op jit(solution)/shard_map/ppermute | solution.py:14
  (3 other events, 2.2 us)

commit v3 on v2

v3 whole, which is shorter than its diff:
```python
import jax
import jax.numpy as jnp
from jax import lax
from jax.experimental import pallas as pl
from jax.experimental.pallas import tpu as pltpu
from jax.sharding import PartitionSpec as P

CHIPS = 4
BF16 = jnp.bfloat16
F32 = jnp.float32


def swap_cores(value):
    return lax.ppermute(value, "loop", [(i, i ^ 1) for i in range(2 * CHIPS)])


def shift_chips(value, step):
    pairs = [
        (2 * chip + core, 2 * ((chip + step) % CHIPS) + core)
        for chip in range(CHIPS)
        for core in range(2)
    ]
    return lax.ppermute(value, "loop", pairs)


def dot(left, right):
    return jnp.dot(left, right, preferred_element_type=F32)


def project_rows(rows, weight):
    return lax.dot_general(rows, weight, (((1,), (1,)), ((), ())), preferred_element_type=F32)


def pick(chip, step, array, width):
    return lax.dynamic_slice_in_dim(array, ((chip - step) & (CHIPS - 1)) * width, width, axis=1)


def hidden_of(act):
    unit = act.shape[1] // 2
    return (jax.nn.silu(act[:, :unit]) * act[:, unit:]).astype(BF16)


def select_kernel(core_ref, tokens, other, chosen, out, half):
    first = core_ref[0] == 0
    whole = jnp.where(
        first,
        jnp.concatenate([tokens[...], other[...]], axis=1),
        jnp.concatenate([other[...], tokens[...]], axis=1),
    )
    out[...] = dot(chosen[...], whole).astype(BF16)
    rows = half.shape[0]
    half[...] = jnp.where(first, whole[:rows], whole[rows:])


def select_rows(core, tokens, other, chosen):
    rows, width = tokens.shape
    arrays = (tokens, other, chosen)
    shapes = [(chosen.shape[0], 2 * width), (rows // 2, 2 * width)]
    return pl.pallas_call(
        select_kernel,
        out_shape=[jax.ShapeDtypeStruct(shape, BF16) for shape in shapes],
        grid_spec=pltpu.PrefetchScalarGridSpec(
            num_scalar_prefetch=1,
            grid=(1,),
            in_specs=[pl.BlockSpec(array.shape, lambda k, c: (0, 0)) for array in arrays],
            out_specs=[pl.BlockSpec(shape, lambda k, c: (0, 0)) for shape in shapes],
        ),
        compiler_params=pltpu.CompilerParams(vmem_limit_bytes=24 << 20),
    )(core.reshape(1), *arrays)


def roll_kernel(chip_ref, *refs):
    out = refs[-1]
    unit = refs[0].shape[0]
    for i, ref in enumerate(refs[:-1]):
        out[0, i * unit : (i + 1) * unit, :] = ref[...]


def roll_features(chip, weights, width):
    unit = weights[0].shape[0]
    rows = unit * len(weights)
    return pl.pallas_call(
        roll_kernel,
        out_shape=jax.ShapeDtypeStruct((CHIPS, rows, width), BF16),
        grid_spec=pltpu.PrefetchScalarGridSpec(
            num_scalar_prefetch=1,
            grid=(CHIPS,),
            in_specs=[pl.BlockSpec((unit, width), lambda k, c: (0, (c[0] - k) & (CHIPS - 1)))]
            * len(weights),
            out_specs=pl.BlockSpec((1, rows, width), lambda k, c: (k, 0, 0)),
        ),
        compiler_params=pltpu.CompilerParams(vmem_limit_bytes=24 << 20),
    )(chip.reshape(1), *weights)


def join_kernel(*refs):
    out = refs[-1]
    unit = refs[0].shape[0]
    for i, ref in enumerate(refs[:-1]):
        out[i * unit : (i + 1) * unit, :] = ref[...]


def join_rows(pieces):
    unit, width = pieces[0].shape
    tile = width // 2
    return pl.pallas_call(
        join_kernel,
        out_shape=jax.ShapeDtypeStruct((unit * len(pieces), width), BF16),
        grid=(2,),
        in_specs=[pl.BlockSpec((unit, tile), lambda n: (0, n))] * len(pieces),
        out_specs=pl.BlockSpec((unit * len(pieces), tile), lambda n: (0, n)),
        compiler_params=pltpu.CompilerParams(vmem_limit_bytes=24 << 20),
    )(*pieces)


def act_of(gate, up):
    return (gate / (1.0 + jnp.exp(-gate)) * up).astype(BF16)


def shared_kernel(where_ref, mine, other, gate, up, down, *refs):
    keep, give, gate_acc, up_acc, hidden = refs
    step = pl.program_id(0)
    rows = mine.shape[0] // CHIPS

    @pl.when(step < CHIPS)
    def _():
        at = pl.ds(pl.multiple_of(step * rows, rows), rows)
        block = jnp.concatenate([mine[at, :], other[at, :]], axis=0)
        first = step == 0
        gate_term, up_term = project_rows(block, gate[...]), project_rows(block, up[...])
        gate_acc[...] = jnp.where(first, gate_term, gate_acc[...] + gate_term)
        up_acc[...] = jnp.where(first, up_term, up_acc[...] + up_term)

    @pl.when(step == CHIPS - 1)
    def _():
        hidden[...] = act_of(gate_acc[...], up_acc[...])

    @pl.when(step >= CHIPS)
    def _():
        at = pl.ds(pl.multiple_of((step - CHIPS) * rows, rows), rows)
        term = dot(hidden[...], down[...]).astype(BF16)
        keep[at, :] = term[:rows]
        give[at, :] = term[rows:]


def shared_terms(where, mine, other, gate, up, down):
    unit = gate.shape[0]
    rows, width = mine.shape[0] // CHIPS * 2, mine.shape[1]

    def near(k):
        return k ^ (k >> 1)

    whole = pl.BlockSpec(mine.shape, lambda k, w: (0, 0))
    into = pl.BlockSpec(
        (unit, width), lambda k, w: (0, (w[0] - near(jnp.minimum(k, CHIPS - 1))) & (CHIPS - 1))
    )
    out_of = pl.BlockSpec(
        (unit, width), lambda k, w: (0, (w[0] + near(jnp.maximum(k - CHIPS, 0))) & (CHIPS - 1))
    )
    return pl.pallas_call(
        shared_kernel,
        out_shape=[jax.ShapeDtypeStruct(mine.shape, BF16)] * 2,
        grid_spec=pltpu.PrefetchScalarGridSpec(
            num_scalar_prefetch=1,
            grid=(2 * CHIPS,),
            in_specs=[whole, whole, into, into, out_of],
            out_specs=[whole] * 2,
            scratch_shapes=[
                pltpu.VMEM((rows, unit), F32),
                pltpu.VMEM((rows, unit), F32),
                pltpu.VMEM((rows, unit), BF16),
            ],
        ),
        compiler_params=pltpu.CompilerParams(vmem_limit_bytes=24 << 20),
    )(where, mine, other, gate, up, down)


def combine_kernel(where_ref, high, low, returned, *refs):
    shared, (mine, theirs) = refs[:CHIPS], refs[CHIPS:]
    contract = (((0,), (0,)), ((), ()))
    part = sum(ref[...].astype(F32) for ref in shared)
    none = jnp.zeros_like(part)
    total = jnp.where(
        where_ref[1] == 0,
        jnp.concatenate([part, none], axis=0),
        jnp.concatenate([none, part], axis=0),
    )
    for weight in (high, low):
        total = total + lax.dot_general(
            weight[...], returned[...], contract, preferred_element_type=F32
        )
    width = mine.shape[1]
    first = where_ref[1] == 0
    mine[...] = jnp.where(first, total[:, :width], total[:, width:])
    theirs[...] = jnp.where(first, total[:, width:], total[:, :width])


def combine(where, high, low, returned, shared):
    rows, width = high.shape[1], returned.shape[1]
    half = jax.ShapeDtypeStruct((rows, width // 2), F32)
    arrays = (high, low, returned, *shared)
    return pl.pallas_call(
        combine_kernel,
        out_shape=[half, half],
        grid_spec=pltpu.PrefetchScalarGridSpec(
            num_scalar_prefetch=1,
            grid=(1,),
            in_specs=[pl.BlockSpec(array.shape, lambda k, w: (0, 0)) for array in arrays],
            out_specs=[pl.BlockSpec(half.shape, lambda k, w: (0, 0))] * 2,
        ),
        compiler_params=pltpu.CompilerParams(vmem_limit_bytes=24 << 20),
    )(where, *arrays)


def local(tokens, routes, route_weights, gate_w, up_w, down_w, shared_gate, shared_up, shared_down):
    tok_rows, width = tokens.shape
    experts = lax.axis_size("expert")
    half_cap = tok_rows * routes.shape[1] * 4 // (3 * experts) // 2
    place = lax.axis_index("loop")
    chip, core = place >> 1, place & 1
    chip_width = 2 * width
    steps = (1, 3, 2)

    other_tokens = swap_cores(tokens)
    ids = jnp.arange(experts, dtype=jnp.int32)
    equal = routes.T[:, None, :] == ids[None, :, None]
    member = jnp.any(equal, axis=0)
    weight = jnp.sum(jnp.where(equal, route_weights.T[:, None, :], 0.0), axis=0)
    row = lax.broadcasted_iota(jnp.int32, (tok_rows, tok_rows), 0)
    col = lax.broadcasted_iota(jnp.int32, (tok_rows, tok_rows), 1)
    before = dot(member.astype(BF16), (row < col).astype(BF16)).astype(jnp.int32)
    slots = jnp.arange(half_cap, dtype=jnp.int32) + core * half_cap
    hit = member[:, None, :] & (before[:, None, :] == slots[None, :, None])
    selector = hit.astype(BF16).reshape(experts * half_cap, tok_rows)
    outgoing, sent_tokens = select_rows(core, tokens, other_tokens, selector)

    def exchange(value):
        value = value.reshape(experts, half_cap, chip_width)
        value = lax.all_to_all(value, "expert", split_axis=0, concat_axis=0, tiled=True)
        return value.reshape(experts * half_cap, chip_width)

    rows = exchange(outgoing)

    gate_own, up_own, down_mine, sent_tokens, _ = lax.optimization_barrier(
        (gate_w[0], up_w[0], down_w[0], sent_tokens, outgoing)
    )
    down_own = [pick(chip, 0, down_mine, chip_width)] + [
        shift_chips(pick(chip, -k, down_mine, chip_width), k) for k in steps
    ]
    gate_other, up_other = swap_cores(gate_own), swap_cores(up_own)
    sent_tokens, gate_other, up_other = lax.optimization_barrier(
        (sent_tokens, gate_other, up_other)
    )
    weights = roll_features(chip, [gate_own, gate_other, up_own, up_other], chip_width)
    token_blocks = [sent_tokens] + [shift_chips(sent_tokens, k) for k in steps]
    down_own, token_blocks[1:3], weights = lax.optimization_barrier(
        (down_own, token_blocks[1:3], weights)
    )
    down_four = join_rows(down_own)
    down_other = swap_cores(down_four)
    rows, weights, down_own, down_other, token_blocks = lax.optimization_barrier(
        (rows, weights, down_own, down_other, token_blocks)
    )
    down_other = jnp.split(down_other, CHIPS)
    down_all = join_rows([part for pair in zip(down_own, down_other) for part in pair])

    cut = rows.shape[0] // 2
    pieces = [rows[:cut], rows[cut:]]
    sides = [(shift_chips(piece, 1), shift_chips(piece, -1)) for piece in pieces]
    acts = [project_rows(piece, weights[0]) for piece in pieces]
    sides[0], acts, down_all = lax.optimization_barrier((sides[0], acts, down_all))
    fars = [
        [
            shift_chips(left[: left.shape[0] // 2], 1),
            shift_chips(right[right.shape[0] // 2 :], -1),
        ]
        for left, right in sides
    ]
    result = []
    for act, (left, right), far in zip(acts, sides, fars):
        act = act + project_rows(left, weights[1]) + project_rows(right, weights[3])
        act = act + jnp.concatenate([project_rows(part, weights[2]) for part in far], axis=0)
        hidden = hidden_of(act)
        hiddens = [hidden] + [shift_chips(hidden, k) for k in steps]
        result.append(dot(jnp.concatenate(hiddens, axis=1), down_all).astype(BF16))
    result = jnp.concatenate(result, axis=0)

    result, token_blocks = lax.optimization_barrier((result, token_blocks))
    returned = exchange(result)

    where = jnp.stack([chip, core]).astype(jnp.int32)
    mine = join_rows(token_blocks)
    keep, give = shared_terms(where, mine, swap_cores(mine), shared_gate, shared_up, shared_down)
    both = keep.astype(F32) + swap_cores(give).astype(F32)
    terms = jnp.split(both.astype(BF16), CHIPS)
    terms = [terms[0]] + [shift_chips(term, k) for term, k in zip(terms[1:], steps)]
    spread = jnp.where(hit, weight[:, None, :], 0.0).reshape(experts * half_cap, tok_rows)
    high = spread.astype(BF16)
    low = (spread - high.astype(F32)).astype(BF16)
    mine, theirs = combine(where, high, low, returned, terms)
    return (mine + swap_cores(theirs)).astype(BF16)


def solution(mesh):
    placed = (
        P("expert", "loop"),
        P("expert", None),
        P("expert", None),
        P("expert", "loop", None),
        P("expert", "loop", None),
        P("expert", "loop", None),
        P("loop", None),
        P("loop", None),
        P("loop", None),
    )
    return jax.shard_map(
        local, mesh=mesh, in_specs=placed, out_specs=P("expert", "loop"), check_vma=False
    )
```

time: 177 us -> 171 us (0.966)
  matrix products: 26.4 us -> 13.1 us
  waiting for transfers between devices: 54.5 us -> 64.2 us
  Pallas kernels: 3.25 us -> 11.8 us
  other arithmetic: 10.8 us -> 3.5 us
  local copies, waits for them, and re-layouts: 20.9 us -> 16.5 us
    ppermute x23, waiting for transfers between devices: 26.5 us -> 56.2 us  [shift_chips(): return lax.ppermute(value, 'loop', pairs)]
    all_to_all x2, waiting for transfers between devices: 26.2 us -> 3.26 us  [exchange(): lax.all_to_all(value, 'expert', split_axis=0, concat_axis=0, tiled=True)]
    pallas_call x0 -> x6, Pallas kernels: none -> 8.85 us  [the longest x1 4.24 us: shared_terms(): pl.pallas_call(shared_kernel, out_shape=[jax.ShapeDtypeStruct(mine.shape,...]
    another operation x2 -> x1, other arithmetic: 7.48 us -> 0.07 us  [local(): where = jnp.stack([chip, core]).astype(jnp.int32)]
    dot_general x5 -> x3, matrix products: 8.58 us -> 2.53 us  [dot(): return jnp.dot(left, right, preferred_element_type=F32)]
    dot_general x11 -> x10, matrix products: 15.6 us -> 10.6 us  [project_rows(): lax.dot_general(rows, weight, (((1,), (1,)), ((), ())), preferred_element...]
    dynamic_slice x2 -> x1, local copies, waits for them, and re-layouts: 5.12 us -> 1.77 us  [pick(): lax.dynamic_slice_in_dim(array, (chip - step & CHIPS - 1) * width, width,...]
    ppermute x5 -> x7, waiting for transfers between devices: 1.89 us -> 4.78 us  [swap_cores(): return lax.ppermute(value, 'loop', [(i, i ^ 1) for i in range(2 * CHIPS)])]
  transfers between devices with their start and end apart: 30 -> 32, of which waited for: 10 -> 19; matrix products, arithmetic and copies ran while one was open for 21% -> 10% of each run, Pallas kernels for 2% -> 5%
where the time goes in v3:
time: 171 us; the launch traced here: 170 us
  waiting for transfers between devices  64.2 us (38%)
  starting transfers between devices  60.8 us (36%)
  local copies, waits for them, and re-layouts  16.5 us (10%)
  matrix products  13.1 us (8%)
  Pallas kernels  11.8 us (7%)
  other arithmetic  3.5 us (2%)
    ppermute x23, waiting for transfers between devices, shift_chips(): return lax.ppermute(value, 'loop', pairs)  56.2 us
    ppermute x23, starting transfers between devices, shift_chips(): return lax.ppermute(value, 'loop', pairs)  29.7 us
    all_to_all x2, starting transfers between devices, exchange(): lax.all_to_all(value, 'expert', split_axis=0, concat_axis=0, tiled=True)  18.9 us
    ppermute x7, starting transfers between devices, swap_cores(): return lax.ppermute(value, 'loop', [(i, i ^ 1) for i in range(2 * CHIPS)])  12.3 us
    unnamed x44, local copies, waits for them, and re-layouts  11.3 us
    dot_general x10, matrix products, project_rows(): lax.dot_general(rows, weight, (((1,), (1,)), ((), ())), preferred_element...  10.6 us
    ppermute x7, waiting for transfers between devices, swap_cores(): return lax.ppermute(value, 'loop', [(i, i ^ 1) for i in range(2 * CHIPS)])  4.78 us
    pallas_call x1, Pallas kernels, shared_terms(): pl.pallas_call(shared_kernel, out_shape=[jax.ShapeDtypeStruct(mine.shape,...  4.24 us
  transfers between devices with their start and end apart: 32, of which 19 were waited for; matrix products, arithmetic and copies ran while one was open for 10% of the time, Pallas kernels for 5%

profile of v3, /device:TPU:1, one launch (start us, length us, event | category | flops | bytes accessed | tf_op | source)
XLA Modules:
  0.0 170.2 jit_solution(2509601786929874697)
XLA Ops:
  0.0 3.2 %collective-permute-start = (bf16[128,640]{1,0:T(8,128)(2,1)}, bf16[128,640]{1,0:T(8,128)(2,1)S(1)}, u32[]{:S(2)}, u32[]{:S(2)}) collective-permute-start(bf16[128,640]{1,0:T(8,128)(2,1)} %tokens.1), channel_id=1, source_target_pairs={{0,1},{1,0},{2,3},{3,2},{4,5},{5,4},{6,7},{7,6},{8,9},{9,8},{10,11... | collective-permute-start | bytes 491528 | tf_op jit(solution)/shard_map/ppermute | solution.py:14
  5.4 1.6 shard_map.91
  8.2 9.6 %all-to-all-start = ((bf16[32,16,1280]{2,1,0:T(8,128)(2,1)}), bf16[32,16,1280]{2,1,0:T(8,128)(2,1)}, u32[]{:S(2)}, u32[]{:S(2)}) async-start(bf16[32,16,1280]{2,1,0:T(8,128)(2,1)} %bitcast.7), calls=%async_computation | async-start | bytes 2621440 | tf_op jit(solution)/shard_map/all_to_all | solution.py:239
  17.8 1.8 %constant_dynamic-slice_fusion = (bf16[192,1280]{1,0:T(8,128)(2,1)S(1)}, bf16[192,1280]{1,0:T(8,128)(2,1)S(1)}, bf16[192,1280]{1,0:T(8,128)(2,1)S(1)}, bf16[192,1280]{1,0:T(8,128)(2,1)S(1)}) fusion(bf16[192,5120]{1,0:T(8,128)(2,1)} %bitcast.90, s32[]{:T(128)S(6)} %select_n.26, s32[]{:T(128)S(6)} %select_n.25, s32[]{:T(128)S(6)} %select_n.24, s32[]{:T(128)S(6)} %select_n.23), kind=kLoop, calls=%fused_computation.67 | loop fusion | bytes 3932176 | tf_op jit(solution)/shard_map/dynamic_slice | solution.py:35
  19.6 1.3 collective-permute-start.1
  20.9 1.5 collective-permute-start.2
  22.3 1.5 collective-permute-start.3
  24.2 2.4 %collective-permute-start.7 = (bf16[64,1280]{1,0:T(8,128)(2,1)}, bf16[64,1280]{1,0:T(8,128)(2,1)S(1)}, u32[]{:S(2)}, u32[]{:S(2)}) collective-permute-start(bf16[64,1280]{1,0:T(8,128)(2,1)} %copy-done.8), channel_id=1, source_target_pairs={{0,6},{1,7},{2,0},{3,1},{4,2},{5,3},{6,4},{7,5},{8,14},{9,15},{10,... | collective-permute-start | bytes 491528 | tf_op jit(solution)/shard_map/ppermute | solution.py:23
  26.6 2.9 %shard_map.92 = bf16[4,768,1280]{2,1,0:T(8,128)(2,1)S(1)} custom-call(s32[1]{0:T(128)} %bitcast.chip_ref, bf16[192,5120]{1,0:T(8,128)(2,1)S(1)} %bitcast.86, bf16[192,5120]{1,0:T(8,128)(2,1)S(1)} %collective-permute-done.4.refs_1_, bf16[192,5120]{1,0:T(8,128)(2,1)S(1)} %bitcast.88, bf16[192,5120]{1,0:T(8,128)(2,1)} %collective-permute-done.5.refs_3_), custom_call_target="tpu_custom_call" | custom-call | tf_op jit(solution)/shard_map/pallas_call | solution.py:82
  29.5 3.1 %copy-done = bf16[4,768,1280]{2,1,0:T(8,128)(2,1)} copy-done((bf16[4,768,1280]{2,1,0:T(8,128)(2,1)}, bf16[4,768,1280]{2,1,0:T(8,128)(2,1)S(1)}, u32[]{:S(2)}) %copy-start) | copy-done | bytes 7864344
  33.1 11.6 %collective-permute-done.3.refs_3_.refs_6_ = bf16[192,1280]{1,0:T(8,128)(2,1)S(1)} collective-permute-done((bf16[192,1280]{1,0:T(8,128)(2,1)S(1)}, bf16[192,1280]{1,0:T(8,128)(2,1)S(1)}, u32[]{:S(2)}, u32[]{:S(2)}) %collective-permute-start.3) | collective-permute-done | bytes 491552 | tf_op jit(solution)/shard_map/ppermute | solution.py:23
  44.7 2.5 %collective-permute-done.6.refs_1_ = bf16[64,1280]{1,0:T(8,128)(2,1)S(1)} collective-permute-done((bf16[64,1280]{1,0:T(8,128)(2,1)}, bf16[64,1280]{1,0:T(8,128)(2,1)S(1)}, u32[]{:S(2)}, u32[]{:S(2)}) %collective-permute-start.6) | collective-permute-done | bytes 163872 | tf_op jit(solution)/shard_map/ppermute | solution.py:23
  47.9 1.4 collective-permute-start.8
  49.3 2.5 %collective-permute-start.9 = (bf16[64,1280]{1,0:T(8,128)(2,1)S(1)}, bf16[64,1280]{1,0:T(8,128)(2,1)S(1)}, u32[]{:S(2)}, u32[]{:S(2)}) collective-permute-start(bf16[64,1280]{1,0:T(8,128)(2,1)S(1)} %copy-done.9), channel_id=1, source_target_pairs={{0,4},{1,5},{2,6},{3,7},{4,0},{5,1},{6,2},{7,3},{8,12},{9,13},{10,... | collective-permute-start | bytes 491528 | tf_op jit(solution)/shard_map/ppermute | solution.py:23
  51.8 4.5 %collective-permute-done.9.refs_3_ = bf16[64,1280]{1,0:T(8,128)(2,1)S(1)} collective-permute-done((bf16[64,1280]{1,0:T(8,128)(2,1)S(1)}, bf16[64,1280]{1,0:T(8,128)(2,1)S(1)}, u32[]{:S(2)}, u32[]{:S(2)}) %collective-permute-start.9) | collective-permute-done | bytes 163872 | tf_op jit(solution)/shard_map/ppermute | solution.py:23
  57.0 1.4 fusion.57
  58.3 1.3 collective-permute-start.10
  59.6 1.6 collective-permute-start.11
  61.2 2.7 %collective-permute-start.18 = (bf16[256,1280]{1,0:T(8,128)(2,1)S(1)}, bf16[256,1280]{1,0:T(8,128)(2,1)S(1)}, u32[]{:S(2)}, u32[]{:S(2)}) collective-permute-start(bf16[256,1280]{1,0:T(8,128)(2,1)S(1)} %get-tuple-element.95), channel_id=1, source_target_pairs={{0,6},{1,7},{2,0},{3,1},{4,2},{5,3},{6,4},{7,5},{8,14},{9,15},{10,... | collective-permute-start | bytes 1966088 | tf_op jit(solution)/shard_map/ppermute | solution.py:23
  63.8 1.8 %fusion.56 = (bf16[192,1280]{1,0:T(8,128)(2,1)S(1)}, bf16[192,1280]{1,0:T(8,128)(2,1)S(1)}, bf16[192,1280]{1,0:T(8,128)(2,1)S(1)}, bf16[192,1280]{1,0:T(8,128)(2,1)S(1)}) fusion(bf16[768,1280]{1,0:T(8,128)(2,1)} %collective-permute-done.8), kind=kLoop, calls=%fused_computation.77 | loop fusion | bytes 3932160 | tf_op jit(solution)/shard_map/split | solution.py:264
  65.6 2.7 %fusion.16 = f32[256,768]{1,0:T(8,128)S(1)} fusion(bf16[4,768,1280]{2,1,0:T(8,128)(2,1)} %copy-done, bf16[512,1280]{1,0:T(8,128)(2,1)} %bitcast.8), kind=kOutput, calls=%fused_computation.18 | convolution fusion | flops 503316480 | bytes 3407872 | tf_op jit(solution)/shard_map/dot_general | solution.py:31
  69.4 1.8 %fusion.18 = f32[256,768]{1,0:T(8,128)S(1)} fusion(bf16[4,768,1280]{2,1,0:T(8,128)(2,1)S(1)} %bitcast.83, bf16[512,1280]{1,0:T(8,128)(2,1)} %bitcast.8), kind=kOutput, calls=%fused_computation.20 | convolution fusion | flops 503316480 | bytes 3407872 | tf_op jit(solution)/shard_map/dot_general | solution.py:31
  71.2 3.5 %collective-permute-done.10 = bf16[256,1280]{1,0:T(8,128)(2,1)S(1)} collective-permute-done((bf16[256,1280]{1,0:T(8,128)(2,1)S(1)}, bf16[256,1280]{1,0:T(8,128)(2,1)S(1)}, u32[]{:S(2)}, u32[]{:S(2)}) %collective-permute-start.10) | collective-permute-done | bytes 655392 | tf_op jit(solution)/shard_map/ppermute | solution.py:23
  76.3 2.1 %collective-permute-start.13 = (bf16[128,1280]{1,0:T(8,128)(2,1)S(1)}, bf16[128,1280]{1,0:T(8,128)(2,1)S(1)}, u32[]{:S(2)}, u32[]{:S(2)}) collective-permute-start(bf16[128,1280]{1,0:T(8,128)(2,1)S(1)} %slice.55), channel_id=1, source_target_pairs={{0,6},{1,7},{2,0},{3,1},{4,2},{5,3},{6,4},{7,5},{8,14},{9,15},{10,... | collective-permute-start | bytes 983048 | tf_op jit(solution)/shard_map/ppermute | solution.py:23
  78.4 10.4 %collective-permute-done.17 = bf16[256,1280]{1,0:T(8,128)(2,1)S(1)} collective-permute-done((bf16[256,1280]{1,0:T(8,128)(2,1)S(1)}, bf16[256,1280]{1,0:T(8,128)(2,1)S(1)}, u32[]{:S(2)}, u32[]{:S(2)}) %collective-permute-start.17) | collective-permute-done | bytes 655392 | tf_op jit(solution)/shard_map/ppermute | solution.py:23
  88.9 2.7 %collective-permute-start.20 = (bf16[128,1280]{1,0:T(8,128)(2,1)S(1)}, bf16[128,1280]{1,0:T(8,128)(2,1)S(1)}, u32[]{:S(2)}, u32[]{:S(2)}) collective-permute-start(bf16[128,1280]{1,0:T(8,128)(2,1)S(1)} %slice.65), channel_id=1, source_target_pairs={{0,6},{1,7},{2,0},{3,1},{4,2},{5,3},{6,4},{7,5},{8,14},{9,15},{10,... | collective-permute-start | bytes 983048 | tf_op jit(solution)/shard_map/ppermute | solution.py:23
  92.3 3.4 %collective-permute-done.12 = bf16[128,1280]{1,0:T(8,128)(2,1)S(1)} collective-permute-done((bf16[128,1280]{1,0:T(8,128)(2,1)S(1)}, bf16[128,1280]{1,0:T(8,128)(2,1)S(1)}, u32[]{:S(2)}, u32[]{:S(2)}) %collective-permute-start.12) | collective-permute-done | bytes 327712 | tf_op jit(solution)/shard_map/ppermute | solution.py:23
  98.3 2.7 %collective-permute-start.15 = (bf16[256,384]{1,0:T(8,128)(2,1)S(1)}, bf16[256,384]{1,0:T(8,128)(2,1)S(1)}, u32[]{:S(2)}, u32[]{:S(2)}) collective-permute-start(bf16[256,384]{1,0:T(8,128)(2,1)S(1)} %fusion.45), channel_id=1, source_target_pairs={{0,6},{1,7},{2,0},{3,1},{4,2},{5,3},{6,4},{7,5},{8,14},{9,15},{10,... | collective-permute-start | bytes 589832 | tf_op jit(solution)/shard_map/ppermute | solution.py:23
  101.4 1.4 collective-permute-done.19
  105.3 2.7 %collective-permute-start.22 = (bf16[256,384]{1,0:T(8,128)(2,1)S(1)}, bf16[256,384]{1,0:T(8,128)(2,1)S(1)}, u32[]{:S(2)}, u32[]{:S(2)}) collective-permute-start(bf16[256,384]{1,0:T(8,128)(2,1)S(1)} %fusion.44), channel_id=1, source_target_pairs={{0,6},{1,7},{2,0},{3,1},{4,2},{5,3},{6,4},{7,5},{8,14},{9,15},{10,... | collective-permute-start | bytes 589832 | tf_op jit(solution)/shard_map/ppermute | solution.py:23
  108.4 4.0 %collective-permute-done.16 = bf16[256,384]{1,0:T(8,128)(2,1)S(1)} collective-permute-done((bf16[256,384]{1,0:T(8,128)(2,1)S(1)}, bf16[256,384]{1,0:T(8,128)(2,1)S(1)}, u32[]{:S(2)}, u32[]{:S(2)}) %collective-permute-start.16) | collective-permute-done | bytes 196640 | tf_op jit(solution)/shard_map/ppermute | solution.py:23
  112.4 1.2 convolution_convert_fusion.1
  113.6 1.6 collective-permute-done.21
  115.8 5.1 %collective-permute-done.23 = bf16[256,384]{1,0:T(8,128)(2,1)S(1)} collective-permute-done((bf16[256,384]{1,0:T(8,128)(2,1)S(1)}, bf16[256,384]{1,0:T(8,128)(2,1)S(1)}, u32[]{:S(2)}, u32[]{:S(2)}) %collective-permute-start.23) | collective-permute-done | bytes 196640 | tf_op jit(solution)/shard_map/ppermute | solution.py:23
  120.9 1.2 convolution_convert_fusion
  123.3 9.3 %all-to-all-start.1 = ((bf16[32,16,1280]{2,1,0:T(8,128)(2,1)}), bf16[32,16,1280]{2,1,0:T(8,128)(2,1)S(1)}, u32[]{:S(2)}, u32[]{:S(2)}) async-start(bf16[32,16,1280]{2,1,0:T(8,128)(2,1)} %bitcast.89), calls=%async_computation.1 | async-start | bytes 2621440 | tf_op jit(solution)/shard_map/all_to_all | solution.py:239
  135.6 2.4 %collective-permute-start.24 = (bf16[256,1280]{1,0:T(8,128)(2,1)S(1)}, bf16[256,1280]{1,0:T(8,128)(2,1)S(1)}, u32[]{:S(2)}, u32[]{:S(2)}) collective-permute-start(bf16[256,1280]{1,0:T(8,128)(2,1)S(1)} %shard_map.95.mine), channel_id=1, source_target_pairs={{0,1},{1,0},{2,3},{3,2},{4,5},{5,4},{6,7},{7,6},{8,9},{9,8},{10,11... | collective-permute-start | bytes 1966088 | tf_op jit(solution)/shard_map/ppermute | solution.py:14
  138.0 1.6 collective-permute-done.24.other
  139.7 1.5 copy-done.2
  141.2 1.5 copy-done.3
  142.8 4.2 %shard_map.96 = (bf16[256,1280]{1,0:T(8,128)(2,1)S(1)}, bf16[256,1280]{1,0:T(8,128)(2,1)S(1)}) custom-call(s32[2]{0:T(128)S(1)} %pad_add_fusion.where_ref, bf16[256,1280]{1,0:T(8,128)(2,1)S(1)} %shard_map.95.mine, bf16[256,1280]{1,0:T(8,128)(2,1)S(1)} %collective-permute-done.24.other, bf16[192,5120]{1,0:T(8,128)(2,1)S(1)} %copy-done.1, ...), custom_call_target="tpu_custom_call" | custom-call | tf_op jit(solution)/shard_map/pallas_call | solution.py:160
  147.5 1.7 %collective-permute-done.25 = bf16[256,1280]{1,0:T(8,128)(2,1)S(1)} collective-permute-done((bf16[256,1280]{1,0:T(8,128)(2,1)S(1)}, bf16[256,1280]{1,0:T(8,128)(2,1)S(1)}, u32[]{:S(2)}, u32[]{:S(2)}) %collective-permute-start.25) | collective-permute-done | bytes 655392 | tf_op jit(solution)/shard_map/ppermute | solution.py:14
  150.3 1.9 %collective-permute-start.27 = (bf16[64,1280]{1,0:T(8,128)(2,1)S(1)}, bf16[64,1280]{1,0:T(8,128)(2,1)S(1)}, u32[]{:S(2)}, u32[]{:S(2)}) collective-permute-start(bf16[64,1280]{1,0:T(8,128)(2,1)S(1)} %get-tuple-element.98), channel_id=1, source_target_pairs={{0,6},{1,7},{2,0},{3,1},{4,2},{5,3},{6,4},{7,5},{8,14},{9,15},{10,... | collective-permute-start | bytes 491528 | tf_op jit(solution)/shard_map/ppermute | solution.py:23
  152.6 3.6 %collective-permute-done.26.refs_1_ = bf16[64,1280]{1,0:T(8,128)(2,1)S(1)} collective-permute-done((bf16[64,1280]{1,0:T(8,128)(2,1)S(1)}, bf16[64,1280]{1,0:T(8,128)(2,1)S(1)}, u32[]{:S(2)}, u32[]{:S(2)}) %collective-permute-start.26) | collective-permute-done | bytes 163872 | tf_op jit(solution)/shard_map/ppermute | solution.py:23
  156.2 3.5 %collective-permute-done.28.refs_3_ = bf16[64,1280]{1,0:T(8,128)(2,1)S(1)} collective-permute-done((bf16[64,1280]{1,0:T(8,128)(2,1)S(1)}, bf16[64,1280]{1,0:T(8,128)(2,1)S(1)}, u32[]{:S(2)}, u32[]{:S(2)}) %collective-permute-start.28) | collective-permute-done | bytes 163872 | tf_op jit(solution)/shard_map/ppermute | solution.py:23
  159.7 3.3 %all-to-all-done.1 = bf16[32,16,1280]{2,1,0:T(8,128)(2,1)S(1)} async-done(((bf16[32,16,1280]{2,1,0:T(8,128)(2,1)}), bf16[32,16,1280]{2,1,0:T(8,128)(2,1)S(1)}, u32[]{:S(2)}, u32[]{:S(2)}) %all-to-all-start.1) | async-done | bytes 1310752 | tf_op jit(solution)/shard_map/all_to_all | solution.py:239
  164.0 4.3 %collective-permute-start.29 = (f32[128,640]{1,0:T(8,128)S(1)}, f32[128,640]{1,0:T(8,128)S(1)}, u32[]{:S(2)}, u32[]{:S(2)}) collective-permute-start(f32[128,640]{1,0:T(8,128)S(1)} %get-tuple-element.86), channel_id=1, source_target_pairs={{0,1},{1,0},{2,3},{3,2},{4,5},{5,4},{6,7},{7,6},{8,9},{9,8},{10,11... | collective-permute-start | bytes 983048 | tf_op jit(solution)/shard_map/ppermute | solution.py:14
  168.3 1.3 collective-permute-done.29
  (103 shorter events, 23.5 us)
Async XLA Ops:
  0.0 4.5 %collective-permute-start = (bf16[128,640]{1,0:T(8,128)(2,1)}, bf16[128,640]{1,0:T(8,128)(2,1)S(1)}, u32[]{:S(2)}, u32[]{:S(2)}) collective-permute-start(bf16[128,640]{1,0:T(8,128)(2,1)} %tokens.1), channel_id=1, source_target_pairs={{0,1},{1,0},{2,3},{3,2},{4,5},{5,4},{6,7},{7,6},{8,9},{9,8},{10,11... | collective-permute-start | bytes 491528 | tf_op jit(solution)/shard_map/ppermute | solution.py:14
  4.5 0.9 copy-start.17
  7.7 16.2 %collective-permute-start.4 = (bf16[192,5120]{1,0:T(8,128)(2,1)}, bf16[192,5120]{1,0:T(8,128)(2,1)S(1)}, u32[]{:S(2)}, u32[]{:S(2)}) collective-permute-start(bf16[192,5120]{1,0:T(8,128)(2,1)} %bitcast.85), channel_id=1, source_target_pairs={{0,1},{1,0},{2,3},{3,2},{4,5},{5,4},{6,7},{7,6},{8,9},{9,8},{10,11... | collective-permute-start | bytes 5898248 | tf_op jit(solution)/shard_map/ppermute | solution.py:14
  8.0 15.8 %collective-permute-start.5 = (bf16[192,5120]{1,0:T(8,128)(2,1)}, bf16[192,5120]{1,0:T(8,128)(2,1)}, u32[]{:S(2)}, u32[]{:S(2)}) collective-permute-start(bf16[192,5120]{1,0:T(8,128)(2,1)} %bitcast.87), channel_id=1, source_target_pairs={{0,1},{1,0},{2,3},{3,2},{4,5},{5,4},{6,7},{7,6},{8,9},{9,8},{10,11... | collective-permute-start | bytes 5898248 | tf_op jit(solution)/shard_map/ppermute | solution.py:14
  8.2 48.8 %all-to-all-start = ((bf16[32,16,1280]{2,1,0:T(8,128)(2,1)}), bf16[32,16,1280]{2,1,0:T(8,128)(2,1)}, u32[]{:S(2)}, u32[]{:S(2)}) async-start(bf16[32,16,1280]{2,1,0:T(8,128)(2,1)} %bitcast.7), calls=%async_computation | async-start | bytes 2621440 | tf_op jit(solution)/shard_map/all_to_all | solution.py:239
  17.8 8.8 %copy-start.4 = (bf16[1,192,5120]{2,1,0:T(8,128)(2,1)S(1)}, bf16[1,192,5120]{2,1,0:T(8,128)(2,1)}, u32[]{:S(2)}) copy-start(bf16[1,192,5120]{2,1,0:T(8,128)(2,1)} %param.12) | copy-start | bytes 5898244
  17.8 8.8 %copy-start.5 = (bf16[1,192,5120]{2,1,0:T(8,128)(2,1)S(1)}, bf16[1,192,5120]{2,1,0:T(8,128)(2,1)}, u32[]{:S(2)}) copy-start(bf16[1,192,5120]{2,1,0:T(8,128)(2,1)} %param.13) | copy-start | bytes 5898244
  19.6 13.5 %collective-permute-start.1 = (bf16[192,1280]{1,0:T(8,128)(2,1)S(1)}, bf16[192,1280]{1,0:T(8,128)(2,1)S(1)}, u32[]{:S(2)}, u32[]{:S(2)}) collective-permute-start(bf16[192,1280]{1,0:T(8,128)(2,1)S(1)} %get-tuple-element.93), channel_id=1, source_target_pairs={{0,2},{1,3},{2,4},{3,5},{4,6},{5,7},{6,0},{7,1},{8,10},{9,11},{10,... | collective-permute-start | bytes 1474568 | tf_op jit(solution)/shard_map/ppermute | solution.py:23
  20.9 12.2 %collective-permute-start.2 = (bf16[192,1280]{1,0:T(8,128)(2,1)S(1)}, bf16[192,1280]{1,0:T(8,128)(2,1)S(1)}, u32[]{:S(2)}, u32[]{:S(2)}) collective-permute-start(bf16[192,1280]{1,0:T(8,128)(2,1)S(1)} %get-tuple-element.92), channel_id=1, source_target_pairs={{0,6},{1,7},{2,0},{3,1},{4,2},{5,3},{6,4},{7,5},{8,14},{9,15},{10,... | collective-permute-start | bytes 1474568 | tf_op jit(solution)/shard_map/ppermute | solution.py:23
  22.3 22.3 %collective-permute-start.3 = (bf16[192,1280]{1,0:T(8,128)(2,1)S(1)}, bf16[192,1280]{1,0:T(8,128)(2,1)S(1)}, u32[]{:S(2)}, u32[]{:S(2)}) collective-permute-start(bf16[192,1280]{1,0:T(8,128)(2,1)S(1)} %get-tuple-element.91), channel_id=1, source_target_pairs={{0,4},{1,5},{2,6},{3,7},{4,0},{5,1},{6,2},{7,3},{8,12},{9,13},{10,... | collective-permute-start | bytes 1474568 | tf_op jit(solution)/shard_map/ppermute | solution.py:23
  23.9 23.3 %collective-permute-start.6 = (bf16[64,1280]{1,0:T(8,128)(2,1)}, bf16[64,1280]{1,0:T(8,128)(2,1)S(1)}, u32[]{:S(2)}, u32[]{:S(2)}) collective-permute-start(bf16[64,1280]{1,0:T(8,128)(2,1)} %copy-done.8), channel_id=1, source_target_pairs={{0,2},{1,3},{2,4},{3,5},{4,6},{5,7},{6,0},{7,1},{8,10},{9,11},{10,... | collective-permute-start | bytes 491528 | tf_op jit(solution)/shard_map/ppermute | solution.py:23
  24.2 23.0 %collective-permute-start.7 = (bf16[64,1280]{1,0:T(8,128)(2,1)}, bf16[64,1280]{1,0:T(8,128)(2,1)S(1)}, u32[]{:S(2)}, u32[]{:S(2)}) collective-permute-start(bf16[64,1280]{1,0:T(8,128)(2,1)} %copy-done.8), channel_id=1, source_target_pairs={{0,6},{1,7},{2,0},{3,1},{4,2},{5,3},{6,4},{7,5},{8,14},{9,15},{10,... | collective-permute-start | bytes 491528 | tf_op jit(solution)/shard_map/ppermute | solution.py:23
  29.5 3.1 %copy-start = (bf16[4,768,1280]{2,1,0:T(8,128)(2,1)}, bf16[4,768,1280]{2,1,0:T(8,128)(2,1)S(1)}, u32[]{:S(2)}) copy-start(bf16[4,768,1280]{2,1,0:T(8,128)(2,1)S(1)} %shard_map.92) | copy-start | bytes 23592964
  44.7 3.1 %copy-start.6 = (bf16[192,1280]{1,0:T(8,128)(2,1)}, bf16[192,1280]{1,0:T(8,128)(2,1)S(1)}, u32[]{:S(2)}) copy-start(bf16[192,1280]{1,0:T(8,128)(2,1)S(1)} %collective-permute-done.3.refs_3_.refs_6_) | copy-start | bytes 1474564
  47.2 2.1 %copy-start.9 = (bf16[64,1280]{1,0:T(8,128)(2,1)S(1)}, bf16[64,1280]{1,0:T(8,128)(2,1)}, u32[]{:S(2)}) copy-start(bf16[64,1280]{1,0:T(8,128)(2,1)} %copy-done.8) | copy-start | bytes 491524
  47.9 9.1 %collective-permute-start.8 = (bf16[768,1280]{1,0:T(8,128)(2,1)S(1)}, bf16[768,1280]{1,0:T(8,128)(2,1)}, u32[]{:S(2)}, u32[]{:S(2)}) collective-permute-start(bf16[768,1280]{1,0:T(8,128)(2,1)S(1)} %shard_map.93), channel_id=1, source_target_pairs={{0,1},{1,0},{2,3},{3,2},{4,5},{5,4},{6,7},{7,6},{8,9},{9,8},{10,11... | collective-permute-start | bytes 5898248 | tf_op jit(solution)/shard_map/ppermute | solution.py:14
  49.3 7.0 %collective-permute-start.9 = (bf16[64,1280]{1,0:T(8,128)(2,1)S(1)}, bf16[64,1280]{1,0:T(8,128)(2,1)S(1)}, u32[]{:S(2)}, u32[]{:S(2)}) collective-permute-start(bf16[64,1280]{1,0:T(8,128)(2,1)S(1)} %copy-done.9), channel_id=1, source_target_pairs={{0,4},{1,5},{2,6},{3,7},{4,0},{5,1},{6,2},{7,3},{8,12},{9,13},{10,... | collective-permute-start | bytes 491528 | tf_op jit(solution)/shard_map/ppermute | solution.py:23
  58.3 16.4 %collective-permute-start.10 = (bf16[256,1280]{1,0:T(8,128)(2,1)S(1)}, bf16[256,1280]{1,0:T(8,128)(2,1)S(1)}, u32[]{:S(2)}, u32[]{:S(2)}) collective-permute-start(bf16[256,1280]{1,0:T(8,128)(2,1)S(1)} %get-tuple-element.96), channel_id=1, source_target_pairs={{0,2},{1,3},{2,4},{3,5},{4,6},{5,7},{6,0},{7,1},{8,10},{9,11},{10,... | collective-permute-start | bytes 1966088 | tf_op jit(solution)/shard_map/ppermute | solution.py:23
  59.6 15.1 %collective-permute-start.11 = (bf16[256,1280]{1,0:T(8,128)(2,1)S(1)}, bf16[256,1280]{1,0:T(8,128)(2,1)S(1)}, u32[]{:S(2)}, u32[]{:S(2)}) collective-permute-start(bf16[256,1280]{1,0:T(8,128)(2,1)S(1)} %get-tuple-element.96), channel_id=1, source_target_pairs={{0,6},{1,7},{2,0},{3,1},{4,2},{5,3},{6,4},{7,5},{8,14},{9,15},{10,... | collective-permute-start | bytes 1966088 | tf_op jit(solution)/shard_map/ppermute | solution.py:23
  61.2 27.6 %collective-permute-start.17 = (bf16[256,1280]{1,0:T(8,128)(2,1)S(1)}, bf16[256,1280]{1,0:T(8,128)(2,1)S(1)}, u32[]{:S(2)}, u32[]{:S(2)}) collective-permute-start(bf16[256,1280]{1,0:T(8,128)(2,1)S(1)} %get-tuple-element.95), channel_id=1, source_target_pairs={{0,2},{1,3},{2,4},{3,5},{4,6},{5,7},{6,0},{7,1},{8,10},{9,11},{10,... | collective-permute-start | bytes 1966088 | tf_op jit(solution)/shard_map/ppermute | solution.py:23
  61.2 27.7 %collective-permute-start.18 = (bf16[256,1280]{1,0:T(8,128)(2,1)S(1)}, bf16[256,1280]{1,0:T(8,128)(2,1)S(1)}, u32[]{:S(2)}, u32[]{:S(2)}) collective-permute-start(bf16[256,1280]{1,0:T(8,128)(2,1)S(1)} %get-tuple-element.95), channel_id=1, source_target_pairs={{0,6},{1,7},{2,0},{3,1},{4,2},{5,3},{6,4},{7,5},{8,14},{9,15},{10,... | collective-permute-start | bytes 1966088 | tf_op jit(solution)/shard_map/ppermute | solution.py:23
  63.8 4.5 %copy-start.7 = (bf16[192,1280]{1,0:T(8,128)(2,1)S(1)}, bf16[192,1280]{1,0:T(8,128)(2,1)}, u32[]{:S(2)}) copy-start(bf16[192,1280]{1,0:T(8,128)(2,1)} %copy-done.6) | copy-start | bytes 1474564
  63.8 5.6 %slice-start = ((s8[7864320]{0:T(1024)(128)(4,1)}), s8[4194304]{0:T(1024)(128)(4,1)S(1)}, s32[]{:S(2)}) async-start(s8[7864320]{0:T(1024)(128)(4,1)} %bitcast.82), calls=%async_computation.2 | async-start | bytes 8388608
  65.6 3.8 %slice-start.1 = ((s8[7864320]{0:T(1024)(128)(4,1)}), s8[3670016]{0:T(1024)(128)(4,1)S(1)}, s32[]{:S(2)}) async-start(s8[7864320]{0:T(1024)(128)(4,1)} %bitcast.82), calls=%async_computation.3 | async-start | bytes 7340032
  74.7 21.0 %collective-permute-start.12 = (bf16[128,1280]{1,0:T(8,128)(2,1)S(1)}, bf16[128,1280]{1,0:T(8,128)(2,1)S(1)}, u32[]{:S(2)}, u32[]{:S(2)}) collective-permute-start(bf16[128,1280]{1,0:T(8,128)(2,1)S(1)} %slice.53), channel_id=1, source_target_pairs={{0,2},{1,3},{2,4},{3,5},{4,6},{5,7},{6,0},{7,1},{8,10},{9,11},{10,... | collective-permute-start | bytes 983048 | tf_op jit(solution)/shard_map/ppermute | solution.py:23
  76.3 20.3 %collective-permute-start.13 = (bf16[128,1280]{1,0:T(8,128)(2,1)S(1)}, bf16[128,1280]{1,0:T(8,128)(2,1)S(1)}, u32[]{:S(2)}, u32[]{:S(2)}) collective-permute-start(bf16[128,1280]{1,0:T(8,128)(2,1)S(1)} %slice.55), channel_id=1, source_target_pairs={{0,6},{1,7},{2,0},{3,1},{4,2},{5,3},{6,4},{7,5},{8,14},{9,15},{10,... | collective-permute-start | bytes 983048 | tf_op jit(solution)/shard_map/ppermute | solution.py:23
  88.8 14.0 %collective-permute-start.19 = (bf16[128,1280]{1,0:T(8,128)(2,1)S(1)}, bf16[128,1280]{1,0:T(8,128)(2,1)S(1)}, u32[]{:S(2)}, u32[]{:S(2)}) collective-permute-start(bf16[128,1280]{1,0:T(8,128)(2,1)S(1)} %slice.64), channel_id=1, source_target_pairs={{0,2},{1,3},{2,4},{3,5},{4,6},{5,7},{6,0},{7,1},{8,10},{9,11},{10,... | collective-permute-start | bytes 983048 | tf_op jit(solution)/shard_map/ppermute | solution.py:23
  88.9 14.7 %collective-permute-start.20 = (bf16[128,1280]{1,0:T(8,128)(2,1)S(1)}, bf16[128,1280]{1,0:T(8,128)(2,1)S(1)}, u32[]{:S(2)}, u32[]{:S(2)}) collective-permute-start(bf16[128,1280]{1,0:T(8,128)(2,1)S(1)} %slice.65), channel_id=1, source_target_pairs={{0,6},{1,7},{2,0},{3,1},{4,2},{5,3},{6,4},{7,5},{8,14},{9,15},{10,... | collective-permute-start | bytes 983048 | tf_op jit(solution)/shard_map/ppermute | solution.py:23
  98.2 9.8 %collective-permute-start.14 = (bf16[256,384]{1,0:T(8,128)(2,1)S(1)}, bf16[256,384]{1,0:T(8,128)(2,1)S(1)}, u32[]{:S(2)}, u32[]{:S(2)}) collective-permute-start(bf16[256,384]{1,0:T(8,128)(2,1)S(1)} %fusion.45), channel_id=1, source_target_pairs={{0,2},{1,3},{2,4},{3,5},{4,6},{5,7},{6,0},{7,1},{8,10},{9,11},{10,... | collective-permute-start | bytes 589832 | tf_op jit(solution)/shard_map/ppermute | solution.py:23
  98.3 10.0 %collective-permute-start.15 = (bf16[256,384]{1,0:T(8,128)(2,1)S(1)}, bf16[256,384]{1,0:T(8,128)(2,1)S(1)}, u32[]{:S(2)}, u32[]{:S(2)}) collective-permute-start(bf16[256,384]{1,0:T(8,128)(2,1)S(1)} %fusion.45), channel_id=1, source_target_pairs={{0,6},{1,7},{2,0},{3,1},{4,2},{5,3},{6,4},{7,5},{8,14},{9,15},{10,... | collective-permute-start | bytes 589832 | tf_op jit(solution)/shard_map/ppermute | solution.py:23
  101.0 11.4 %collective-permute-start.16 = (bf16[256,384]{1,0:T(8,128)(2,1)S(1)}, bf16[256,384]{1,0:T(8,128)(2,1)S(1)}, u32[]{:S(2)}, u32[]{:S(2)}) collective-permute-start(bf16[256,384]{1,0:T(8,128)(2,1)S(1)} %fusion.45), channel_id=1, source_target_pairs={{0,4},{1,5},{2,6},{3,7},{4,0},{5,1},{6,2},{7,3},{8,12},{9,13},{10,... | collective-permute-start | bytes 589832 | tf_op jit(solution)/shard_map/ppermute | solution.py:23
  105.2 10.0 %collective-permute-start.21 = (bf16[256,384]{1,0:T(8,128)(2,1)S(1)}, bf16[256,384]{1,0:T(8,128)(2,1)S(1)}, u32[]{:S(2)}, u32[]{:S(2)}) collective-permute-start(bf16[256,384]{1,0:T(8,128)(2,1)S(1)} %fusion.44), channel_id=1, source_target_pairs={{0,2},{1,3},{2,4},{3,5},{4,6},{5,7},{6,0},{7,1},{8,10},{9,11},{10,... | collective-permute-start | bytes 589832 | tf_op jit(solution)/shard_map/ppermute | solution.py:23
  105.3 10.5 %collective-permute-start.22 = (bf16[256,384]{1,0:T(8,128)(2,1)S(1)}, bf16[256,384]{1,0:T(8,128)(2,1)S(1)}, u32[]{:S(2)}, u32[]{:S(2)}) collective-permute-start(bf16[256,384]{1,0:T(8,128)(2,1)S(1)} %fusion.44), channel_id=1, source_target_pairs={{0,6},{1,7},{2,0},{3,1},{4,2},{5,3},{6,4},{7,5},{8,14},{9,15},{10,... | collective-permute-start | bytes 589832 | tf_op jit(solution)/shard_map/ppermute | solution.py:23
  108.0 12.9 %collective-permute-start.23 = (bf16[256,384]{1,0:T(8,128)(2,1)S(1)}, bf16[256,384]{1,0:T(8,128)(2,1)S(1)}, u32[]{:S(2)}, u32[]{:S(2)}) collective-permute-start(bf16[256,384]{1,0:T(8,128)(2,1)S(1)} %fusion.44), channel_id=1, source_target_pairs={{0,4},{1,5},{2,6},{3,7},{4,0},{5,1},{6,2},{7,3},{8,12},{9,13},{10,... | collective-permute-start | bytes 589832 | tf_op jit(solution)/shard_map/ppermute | solution.py:23
  123.3 9.3 %copy-start.10 = (bf16[64,1280]{1,0:T(8,128)(2,1)S(1)}, bf16[64,1280]{1,0:T(8,128)(2,1)}, u32[]{:S(2)}) copy-start(bf16[64,1280]{1,0:T(8,128)(2,1)} %copy-done.8) | copy-start | bytes 491524
  123.3 16.4 %copy-start.1 = (bf16[192,5120]{1,0:T(8,128)(2,1)S(1)}, bf16[192,5120]{1,0:T(8,128)(2,1)}, u32[]{:S(2)}) copy-start(bf16[192,5120]{1,0:T(8,128)(2,1)} %gate.1) | copy-start | bytes 5898244
  123.3 39.6 %all-to-all-start.1 = ((bf16[32,16,1280]{2,1,0:T(8,128)(2,1)}), bf16[32,16,1280]{2,1,0:T(8,128)(2,1)S(1)}, u32[]{:S(2)}, u32[]{:S(2)}) async-start(bf16[32,16,1280]{2,1,0:T(8,128)(2,1)} %bitcast.89), calls=%async_computation.1 | async-start | bytes 2621440 | tf_op jit(solution)/shard_map/all_to_all | solution.py:239
  132.6 0.9 copy-start.12
  135.6 4.1 %collective-permute-start.24 = (bf16[256,1280]{1,0:T(8,128)(2,1)S(1)}, bf16[256,1280]{1,0:T(8,128)(2,1)S(1)}, u32[]{:S(2)}, u32[]{:S(2)}) collective-permute-start(bf16[256,1280]{1,0:T(8,128)(2,1)S(1)} %shard_map.95.mine), channel_id=1, source_target_pairs={{0,1},{1,0},{2,3},{3,2},{4,5},{5,4},{6,7},{7,6},{8,9},{9,8},{10,11... | collective-permute-start | bytes 1966088 | tf_op jit(solution)/shard_map/ppermute | solution.py:14
  139.7 1.5 copy-start.2
  141.2 1.5 copy-start.3
  147.0 5.2 %copy-start.18 = (s32[128,6]{0,1:T(8,128)S(1)}, s32[128,6]{0,1:T(8,128)}, u32[]{:S(2)}) copy-start(s32[128,6]{0,1:T(8,128)} %param.10) | copy-start | bytes 9220
  147.0 5.2 %copy-start.19 = (f32[128,6]{0,1:T(8,128)S(1)}, f32[128,6]{0,1:T(8,128)}, u32[]{:S(2)}) copy-start(f32[128,6]{0,1:T(8,128)} %param.11) | copy-start | bytes 9220
  147.1 2.2 %collective-permute-start.25 = (bf16[256,1280]{1,0:T(8,128)(2,1)S(1)}, bf16[256,1280]{1,0:T(8,128)(2,1)S(1)}, u32[]{:S(2)}, u32[]{:S(2)}) collective-permute-start(bf16[256,1280]{1,0:T(8,128)(2,1)S(1)} %get-tuple-element.84), channel_id=1, source_target_pairs={{0,1},{1,0},{2,3},{3,2},{4,5},{5,4},{6,7},{7,6},{8,9},{9,8},{10,11... | collective-permute-start | bytes 1966088 | tf_op jit(solution)/shard_map/ppermute | solution.py:14
  149.4 6.7 %collective-permute-start.26 = (bf16[64,1280]{1,0:T(8,128)(2,1)S(1)}, bf16[64,1280]{1,0:T(8,128)(2,1)S(1)}, u32[]{:S(2)}, u32[]{:S(2)}) collective-permute-start(bf16[64,1280]{1,0:T(8,128)(2,1)S(1)} %get-tuple-element.99), channel_id=1, source_target_pairs={{0,2},{1,3},{2,4},{3,5},{4,6},{5,7},{6,0},{7,1},{8,10},{9,11},{10,... | collective-permute-start | bytes 491528 | tf_op jit(solution)/shard_map/ppermute | solution.py:23
  150.3 5.8 %collective-permute-start.27 = (bf16[64,1280]{1,0:T(8,128)(2,1)S(1)}, bf16[64,1280]{1,0:T(8,128)(2,1)S(1)}, u32[]{:S(2)}, u32[]{:S(2)}) collective-permute-start(bf16[64,1280]{1,0:T(8,128)(2,1)S(1)} %get-tuple-element.98), channel_id=1, source_target_pairs={{0,6},{1,7},{2,0},{3,1},{4,2},{5,3},{6,4},{7,5},{8,14},{9,15},{10,... | collective-permute-start | bytes 491528 | tf_op jit(solution)/shard_map/ppermute | solution.py:23
  152.2 7.5 %collective-permute-start.28 = (bf16[64,1280]{1,0:T(8,128)(2,1)S(1)}, bf16[64,1280]{1,0:T(8,128)(2,1)S(1)}, u32[]{:S(2)}, u32[]{:S(2)}) collective-permute-start(bf16[64,1280]{1,0:T(8,128)(2,1)S(1)} %get-tuple-element.97), channel_id=1, source_target_pairs={{0,4},{1,5},{2,6},{3,7},{4,0},{5,1},{6,2},{7,3},{8,12},{9,13},{10,... | collective-permute-start | bytes 491528 | tf_op jit(solution)/shard_map/ppermute | solution.py:23
  164.0 5.5 %collective-permute-start.29 = (f32[128,640]{1,0:T(8,128)S(1)}, f32[128,640]{1,0:T(8,128)S(1)}, u32[]{:S(2)}, u32[]{:S(2)}) collective-permute-start(f32[128,640]{1,0:T(8,128)S(1)} %get-tuple-element.86), channel_id=1, source_target_pairs={{0,1},{1,0},{2,3},{3,2},{4,5},{5,4},{6,7},{7,6},{8,9},{9,8},{10,11... | collective-permute-start | bytes 983048 | tf_op jit(solution)/shard_map/ppermute | solution.py:14
  (6 other events, 4.5 us)

commit v4 on v3

--- a/solution.py
+++ b/solution.py
@@ -93,39 +93,78 @@
     )(chip.reshape(1), *weights)
 
 
-def join_kernel(*refs):
+def near(k):
+    return k ^ (k >> 1)
+
+
+def pack_kernel(chip_ref, down, tokens, *outs):
+    unit = down.shape[0]
+    for index, out in enumerate(outs):
+
+        @pl.when(pl.program_id(0) == index)
+        def _(out=out):
+            out[:unit, :] = down[...]
+            out[unit:, :] = tokens[...]
+
+
+def pack(chip, down, tokens):
+    unit, (rows, width) = down.shape[0], tokens.shape
+    shape = (unit + rows, width)
+    return pl.pallas_call(
+        pack_kernel,
+        out_shape=[jax.ShapeDtypeStruct(shape, BF16)] * CHIPS,
+        grid_spec=pltpu.PrefetchScalarGridSpec(
+            num_scalar_prefetch=1,
+            grid=(CHIPS,),
+            in_specs=[
+                pl.BlockSpec((unit, width), lambda k, c: (0, (c[0] + near(k)) & (CHIPS - 1))),
+                pl.BlockSpec((rows, width), lambda k, c: (0, 0)),
+            ],
+            out_specs=[pl.BlockSpec(shape, lambda k, c: (0, 0))] * CHIPS,
+        ),
+        compiler_params=pltpu.CompilerParams(vmem_limit_bytes=24 << 20),
+    )(chip.reshape(1), down, tokens)
+
+
+def down_kernel(*refs):
     out = refs[-1]
-    unit = refs[0].shape[0]
-    for i, ref in enumerate(refs[:-1]):
-        out[i * unit : (i + 1) * unit, :] = ref[...]
-
-
-def join_rows(pieces):
-    unit, width = pieces[0].shape
+    unit = out.shape[0] // (2 * CHIPS)
+    for k, ref in enumerate(refs[:-1]):
+        out[k * unit : (k + 1) * unit, :] = ref[:unit, :]
+
+
+def join_down(unit, own, other):
+    rows, width = own[0].shape
     tile = width // 2
     return pl.pallas_call(
-        join_kernel,
-        out_shape=jax.ShapeDtypeStruct((unit * len(pieces), width), BF16),
+        down_kernel,
+        out_shape=jax.ShapeDtypeStruct((2 * CHIPS * unit, width), BF16),
         grid=(2,),
-        in_specs=[pl.BlockSpec((unit, tile), lambda n: (0, n))] * len(pieces),
-        out_specs=pl.BlockSpec((unit * len(pieces), tile), lambda n: (0, n)),
-        compiler_params=pltpu.CompilerParams(vmem_limit_bytes=24 << 20),
-    )(*pieces)
+        in_specs=[pl.BlockSpec((rows, tile), lambda n: (0, n))] * (2 * CHIPS),
+        out_specs=pl.BlockSpec((2 * CHIPS * unit, tile), lambda n: (0, n)),
+        compiler_params=pltpu.CompilerParams(vmem_limit_bytes=24 << 20),
+    )(*[part for pair in zip(own, other) for part in pair])
 
 
 def act_of(gate, up):
     return (gate / (1.0 + jnp.exp(-gate)) * up).astype(BF16)
 
 
-def shared_kernel(where_ref, mine, other, gate, up, down, *refs):
-    keep, give, gate_acc, up_acc, hidden = refs
+def shared_kernel(where_ref, *refs):
+    mine, other, refs = refs[:CHIPS], refs[CHIPS : 2 * CHIPS], refs[2 * CHIPS :]
+    gate, up, down, keep, give, gate_acc, up_acc, hidden = refs
     step = pl.program_id(0)
-    rows = mine.shape[0] // CHIPS
+    rows = mine[0].shape[0]
+
+    def pick_block(parts):
+        block = parts[0][...]
+        for k in range(1, CHIPS):
+            block = jnp.where(step == k, parts[k][...], block)
+        return block
 
     @pl.when(step < CHIPS)
     def _():
-        at = pl.ds(pl.multiple_of(step * rows, rows), rows)
-        block = jnp.concatenate([mine[at, :], other[at, :]], axis=0)
+        block = jnp.concatenate([pick_block(mine), pick_block(other)], axis=0)
         first = step == 0
         gate_term, up_term = project_rows(block, gate[...]), project_rows(block, up[...])
         gate_acc[...] = jnp.where(first, gate_term, gate_acc[...] + gate_term)
@@ -145,12 +184,12 @@
 
 def shared_terms(where, mine, other, gate, up, down):
     unit = gate.shape[0]
-    rows, width = mine.shape[0] // CHIPS * 2, mine.shape[1]
-
-    def near(k):
-        return k ^ (k >> 1)
-
-    whole = pl.BlockSpec(mine.shape, lambda k, w: (0, 0))
+    pack_rows, width = mine[0].shape
+    half = pack_rows - unit
+    rows = 2 * half
+    shape = (CHIPS * half, width)
+    whole = pl.BlockSpec(shape, lambda k, w: (0, 0))
+    block = pl.BlockSpec((half, width), lambda k, w: (unit // half, 0))
     into = pl.BlockSpec(
         (unit, width), lambda k, w: (0, (w[0] - near(jnp.minimum(k, CHIPS - 1))) & (CHIPS - 1))
     )
@@ -159,11 +198,11 @@
     )
     return pl.pallas_call(
         shared_kernel,
-        out_shape=[jax.ShapeDtypeStruct(mine.shape, BF16)] * 2,
+        out_shape=[jax.ShapeDtypeStruct(shape, BF16)] * 2,
         grid_spec=pltpu.PrefetchScalarGridSpec(
             num_scalar_prefetch=1,
             grid=(2 * CHIPS,),
-            in_specs=[whole, whole, into, into, out_of],
+            in_specs=[block] * (2 * CHIPS) + [into, into, out_of],
             out_specs=[whole] * 2,
             scratch_shapes=[
                 pltpu.VMEM((rows, unit), F32),
@@ -172,7 +211,7 @@
             ],
         ),
         compiler_params=pltpu.CompilerParams(vmem_limit_bytes=24 << 20),
-    )(where, mine, other, gate, up, down)
+    )(where, *mine, *other, gate, up, down)
 
 
 def combine_kernel(where_ref, high, low, returned, *refs):
@@ -244,25 +283,16 @@
     gate_own, up_own, down_mine, sent_tokens, _ = lax.optimization_barrier(
         (gate_w[0], up_w[0], down_w[0], sent_tokens, outgoing)
     )
-    down_own = [pick(chip, 0, down_mine, chip_width)] + [
-        shift_chips(pick(chip, -k, down_mine, chip_width), k) for k in steps
-    ]
     gate_other, up_other = swap_cores(gate_own), swap_cores(up_own)
-    sent_tokens, gate_other, up_other = lax.optimization_barrier(
-        (sent_tokens, gate_other, up_other)
-    )
+    packs = pack(chip, down_mine, sent_tokens)
+    packs = [packs[0]] + [shift_chips(part, k) for part, k in zip(packs[1:], steps)]
     weights = roll_features(chip, [gate_own, gate_other, up_own, up_other], chip_width)
-    token_blocks = [sent_tokens] + [shift_chips(sent_tokens, k) for k in steps]
-    down_own, token_blocks[1:3], weights = lax.optimization_barrier(
-        (down_own, token_blocks[1:3], weights)
-    )
-    down_four = join_rows(down_own)
-    down_other = swap_cores(down_four)
-    rows, weights, down_own, down_other, token_blocks = lax.optimization_barrier(
-        (rows, weights, down_own, down_other, token_blocks)
-    )
-    down_other = jnp.split(down_other, CHIPS)
-    down_all = join_rows([part for pair in zip(down_own, down_other) for part in pair])
+    packs[1:3], weights = lax.optimization_barrier((packs[1:3], weights))
+    own_pack, other_pack = packs, [swap_cores(part) for part in packs]
+    rows, weights, own_pack, other_pack = lax.optimization_barrier(
+        (rows, weights, own_pack, other_pack)
+    )
+    down_all = join_down(down_mine.shape[0], own_pack, other_pack)
 
     cut = rows.shape[0] // 2
     pieces = [rows[:cut], rows[cut:]]
@@ -281,16 +311,21 @@
         act = act + project_rows(left, weights[1]) + project_rows(right, weights[3])
         act = act + jnp.concatenate([project_rows(part, weights[2]) for part in far], axis=0)
         hidden = hidden_of(act)
-        hiddens = [hidden] + [shift_chips(hidden, k) for k in steps]
+        if len(result) in (0, 1):
+            left, right = shift_chips(hidden, 1), shift_chips(hidden, -1)
+            middle = hidden.shape[0] // 2
+            far = [shift_chips(left[:middle], 1), shift_chips(right[middle:], -1)]
+            hiddens = [hidden, left, right, jnp.concatenate(far, axis=0)]
+        else:
+            hiddens = [hidden] + [shift_chips(hidden, k) for k in steps]
         result.append(dot(jnp.concatenate(hiddens, axis=1), down_all).astype(BF16))
     result = jnp.concatenate(result, axis=0)
 
-    result, token_blocks = lax.optimization_barrier((result, token_blocks))
+    result, own_pack, other_pack = lax.optimization_barrier((result, own_pack, other_pack))
     returned = exchange(result)
 
     where = jnp.stack([chip, core]).astype(jnp.int32)
-    mine = join_rows(token_blocks)
-    keep, give = shared_terms(where, mine, swap_cores(mine), shared_gate, shared_up, shared_down)
+    keep, give = shared_terms(where, own_pack, other_pack, shared_gate, shared_up, shared_down)
     both = keep.astype(F32) + swap_cores(give).astype(F32)
     terms = jnp.split(both.astype(BF16), CHIPS)
     terms = [terms[0]] + [shift_chips(term, k) for term, k in zip(terms[1:], steps)]

time: 171 us -> 166 us (0.971)
  waiting for transfers between devices: 64.2 us -> 49.7 us
  starting transfers between devices: 60.8 us -> 65.5 us
  local copies, waits for them, and re-layouts: 16.5 us -> 19.6 us
  Pallas kernels: 11.8 us -> 13.6 us
    ppermute x23 -> x22, waiting for transfers between devices: 56.2 us -> 44.6 us  [shift_chips(): return lax.ppermute(value, 'loop', pairs)]
    unnamed x44 -> x38, local copies, waits for them, and re-layouts: 11.3 us -> 17.8 us
    all_to_all x2, waiting for transfers between devices: 3.26 us -> 0.01 us  [exchange(): lax.all_to_all(value, 'expert', split_axis=0, concat_axis=0, tiled=True)]
    ppermute x23 -> x22, starting transfers between devices: 29.7 us -> 32.2 us  [shift_chips(): return lax.ppermute(value, 'loop', pairs)]
    ppermute x7 -> x9, starting transfers between devices: 12.3 us -> 14.5 us  [swap_cores(): return lax.ppermute(value, 'loop', [(i, i ^ 1) for i in range(2 * CHIPS)])]
    dynamic_slice x1 -> x0, local copies, waits for them, and re-layouts: 1.77 us -> none  [pick(): lax.dynamic_slice_in_dim(array, (chip - step & CHIPS - 1) * width, width,...]
    split x1 -> x0, local copies, waits for them, and re-layouts: 1.75 us -> none  [local(): down_other = jnp.split(down_other, CHIPS)]
    pallas_call x4 -> x3, Pallas kernels: 6.14 us -> 7.78 us  [the longest x1 5.3 us: shared_terms(): pl.pallas_call(shared_kernel, out_shape=[jax.ShapeDtypeStruct(shape, BF16...]
  transfers between devices with their start and end apart: 32 -> 33, of which waited for: 19 -> 16; matrix products, arithmetic and copies ran while one was open for 10% -> 8% of each run, Pallas kernels for 5% -> 7%
where the time goes in v4:
time: 166 us; the launch traced here: 165 us
  starting transfers between devices  65.5 us (39%)
  waiting for transfers between devices  49.7 us (30%)
  local copies, waits for them, and re-layouts  19.6 us (12%)
  Pallas kernels  13.6 us (8%)
  matrix products  12.9 us (8%)
  other arithmetic  3.51 us (2%)
    ppermute x22, waiting for transfers between devices, shift_chips(): return lax.ppermute(value, 'loop', pairs)  44.6 us
    ppermute x22, starting transfers between devices, shift_chips(): return lax.ppermute(value, 'loop', pairs)  32.2 us
    all_to_all x2, starting transfers between devices, exchange(): lax.all_to_all(value, 'expert', split_axis=0, concat_axis=0, tiled=True)  18.7 us
    unnamed x38, local copies, waits for them, and re-layouts  17.8 us
    ppermute x9, starting transfers between devices, swap_cores(): return lax.ppermute(value, 'loop', [(i, i ^ 1) for i in range(2 * CHIPS)])  14.5 us
    dot_general x10, matrix products, project_rows(): lax.dot_general(rows, weight, (((1,), (1,)), ((), ())), preferred_element...  10.3 us
    pallas_call x1, Pallas kernels, shared_terms(): pl.pallas_call(shared_kernel, out_shape=[jax.ShapeDtypeStruct(shape, BF16...  5.3 us
    ppermute x9, waiting for transfers between devices, swap_cores(): return lax.ppermute(value, 'loop', [(i, i ^ 1) for i in range(2 * CHIPS)])  5.03 us
  transfers between devices with their start and end apart: 33, of which 16 were waited for; matrix products, arithmetic and copies ran while one was open for 8% of the time, Pallas kernels for 7%

profile of v4, /device:TPU:1, one launch (start us, length us, event | category | flops | bytes accessed | tf_op | source)
XLA Modules:
  0.0 165.2 jit_solution(9908504199896505246)
XLA Ops:
  0.0 3.2 %collective-permute-start = (bf16[128,640]{1,0:T(8,128)(2,1)}, bf16[128,640]{1,0:T(8,128)(2,1)S(1)}, u32[]{:S(2)}, u32[]{:S(2)}) collective-permute-start(bf16[128,640]{1,0:T(8,128)(2,1)} %tokens.1), channel_id=1, source_target_pairs={{0,1},{1,0},{2,3},{3,2},{4,5},{5,4},{6,7},{7,6},{8,9},{9,8},{10,11... | collective-permute-start | bytes 491528 | tf_op jit(solution)/shard_map/ppermute | solution.py:14
  5.4 1.6 shard_map.91
  7.5 9.6 %all-to-all-start = ((bf16[32,16,1280]{2,1,0:T(8,128)(2,1)}), bf16[32,16,1280]{2,1,0:T(8,128)(2,1)}, u32[]{:S(2)}, u32[]{:S(2)}) async-start(bf16[32,16,1280]{2,1,0:T(8,128)(2,1)} %bitcast.7), calls=%async_computation | async-start | bytes 2621440 | tf_op jit(solution)/shard_map/all_to_all | solution.py:278
  17.1 1.5 copy-done.8
  19.1 2.8 %collective-permute-start.5 = (bf16[256,1280]{1,0:T(8,128)(2,1)S(1)}, bf16[256,1280]{1,0:T(8,128)(2,1)S(1)}, u32[]{:S(2)}, u32[]{:S(2)}) collective-permute-start(bf16[256,1280]{1,0:T(8,128)(2,1)S(1)} %get-tuple-element.58), channel_id=1, source_target_pairs={{0,4},{1,5},{2,6},{3,7},{4,0},{5,1},{6,2},{7,3},{8,12},{9,13},{10,... | collective-permute-start | bytes 1966088 | tf_op jit(solution)/shard_map/ppermute | solution.py:23
  22.3 2.4 %collective-permute-start.2 = (bf16[256,1280]{1,0:T(8,128)(2,1)S(1)}, bf16[256,1280]{1,0:T(8,128)(2,1)S(1)}, u32[]{:S(2)}, u32[]{:S(2)}) collective-permute-start(bf16[256,1280]{1,0:T(8,128)(2,1)S(1)} %get-tuple-element.51), channel_id=1, source_target_pairs={{0,6},{1,7},{2,0},{3,1},{4,2},{5,3},{6,4},{7,5},{8,14},{9,15},{10,... | collective-permute-start | bytes 1966088 | tf_op jit(solution)/shard_map/ppermute | solution.py:23
  24.6 11.9 %collective-permute-done.5.refs_6_.refs_3_ = bf16[256,1280]{1,0:T(8,128)(2,1)S(1)} collective-permute-done((bf16[256,1280]{1,0:T(8,128)(2,1)S(1)}, bf16[256,1280]{1,0:T(8,128)(2,1)S(1)}, u32[]{:S(2)}, u32[]{:S(2)}) %collective-permute-start.5) | collective-permute-done | bytes 655392 | tf_op jit(solution)/shard_map/ppermute | solution.py:23
  36.5 2.5 %collective-permute-start.6 = (bf16[256,1280]{1,0:T(8,128)(2,1)S(1)}, bf16[256,1280]{1,0:T(8,128)(2,1)S(1)}, u32[]{:S(2)}, u32[]{:S(2)}) collective-permute-start(bf16[256,1280]{1,0:T(8,128)(2,1)S(1)} %get-tuple-element.75.refs_0_), channel_id=1, source_target_pairs={{0,1},{1,0},{2,3},{3,2},{4,5},{5,4},{6,7},{7,6},{8,9},{9,8},{10,11... | collective-permute-start | bytes 1966088 | tf_op jit(solution)/shard_map/ppermute | solution.py:14
  39.1 1.5 copy-done.9
  40.6 1.5 copy-done.10
  42.1 3.2 %shard_map.93 = bf16[4,768,1280]{2,1,0:T(8,128)(2,1)S(1)} custom-call(s32[1]{0:T(128)} %bitcast.chip_ref, bf16[192,5120]{1,0:T(8,128)(2,1)S(1)} %bitcast.91, bf16[192,5120]{1,0:T(8,128)(2,1)} %collective-permute-done.3.refs_1_, bf16[192,5120]{1,0:T(8,128)(2,1)S(1)} %bitcast.93, bf16[192,5120]{1,0:T(8,128)(2,1)} %collective-permute-done.4.refs_3_), custom_call_target="tpu_custom_call" | custom-call | tf_op jit(solution)/shard_map/pallas_call | solution.py:82
  45.3 3.1 %copy-done = bf16[4,768,1280]{2,1,0:T(8,128)(2,1)} copy-done((bf16[4,768,1280]{2,1,0:T(8,128)(2,1)}, bf16[4,768,1280]{2,1,0:T(8,128)(2,1)S(1)}, u32[]{:S(2)}) %copy-start) | copy-done | bytes 7864344
  48.4 3.0 %collective-permute-done.1.refs_2_.refs_1_ = bf16[256,1280]{1,0:T(8,128)(2,1)S(1)} collective-permute-done((bf16[256,1280]{1,0:T(8,128)(2,1)S(1)}, bf16[256,1280]{1,0:T(8,128)(2,1)S(1)}, u32[]{:S(2)}, u32[]{:S(2)}) %collective-permute-start.1) | collective-permute-done | bytes 655392 | tf_op jit(solution)/shard_map/ppermute | solution.py:23
  54.9 1.5 fusion.69
  56.4 1.2 collective-permute-start.10
  57.6 1.5 collective-permute-start.11
  59.1 2.7 %collective-permute-start.19 = (bf16[256,1280]{1,0:T(8,128)(2,1)S(1)}, bf16[256,1280]{1,0:T(8,128)(2,1)S(1)}, u32[]{:S(2)}, u32[]{:S(2)}) collective-permute-start(bf16[256,1280]{1,0:T(8,128)(2,1)S(1)} %get-tuple-element.87), channel_id=1, source_target_pairs={{0,6},{1,7},{2,0},{3,1},{4,2},{5,3},{6,4},{7,5},{8,14},{9,15},{10,... | collective-permute-start | bytes 1966088 | tf_op jit(solution)/shard_map/ppermute | solution.py:23
  61.8 2.5 %fusion.16 = f32[256,768]{1,0:T(8,128)S(1)} fusion(bf16[4,768,1280]{2,1,0:T(8,128)(2,1)} %copy-done, bf16[512,1280]{1,0:T(8,128)(2,1)} %bitcast.8), kind=kOutput, calls=%fused_computation.18 | convolution fusion | flops 503316480 | bytes 3407872 | tf_op jit(solution)/shard_map/dot_general | solution.py:31
  64.3 2.0 %shard_map.94 = bf16[1536,1280]{1,0:T(8,128)(2,1)S(1)} custom-call(bf16[256,1280]{1,0:T(8,128)(2,1)S(1)} %get-tuple-element.75.refs_0_, bf16[256,1280]{1,0:T(8,128)(2,1)S(1)} %collective-permute-done.6.refs_1_.refs_4_, bf16[256,1280]{1,0:T(8,128)(2,1)S(1)} %collective-permute-done.1.refs_2_.refs_1_, ...), custom_call_target="tpu_custom_call" | custom-call | tf_op jit(solution)/shard_map/pallas_call | solution.py:139
  66.7 1.8 %fusion.18 = f32[256,768]{1,0:T(8,128)S(1)} fusion(bf16[4,768,1280]{2,1,0:T(8,128)(2,1)S(1)} %bitcast.87, bf16[512,1280]{1,0:T(8,128)(2,1)} %bitcast.8), kind=kOutput, calls=%fused_computation.20 | convolution fusion | flops 503316480 | bytes 3407872 | tf_op jit(solution)/shard_map/dot_general | solution.py:31
  68.6 5.1 %collective-permute-done.10 = bf16[256,1280]{1,0:T(8,128)(2,1)S(1)} collective-permute-done((bf16[256,1280]{1,0:T(8,128)(2,1)S(1)}, bf16[256,1280]{1,0:T(8,128)(2,1)S(1)}, u32[]{:S(2)}, u32[]{:S(2)}) %collective-permute-start.10) | collective-permute-done | bytes 655392 | tf_op jit(solution)/shard_map/ppermute | solution.py:23
  75.0 2.2 %collective-permute-start.13 = (bf16[128,1280]{1,0:T(8,128)(2,1)S(1)}, bf16[128,1280]{1,0:T(8,128)(2,1)S(1)}, u32[]{:S(2)}, u32[]{:S(2)}) collective-permute-start(bf16[128,1280]{1,0:T(8,128)(2,1)S(1)} %slice.67), channel_id=1, source_target_pairs={{0,6},{1,7},{2,0},{3,1},{4,2},{5,3},{6,4},{7,5},{8,14},{9,15},{10,... | collective-permute-start | bytes 983048 | tf_op jit(solution)/shard_map/ppermute | solution.py:23
  77.2 10.4 %collective-permute-done.18 = bf16[256,1280]{1,0:T(8,128)(2,1)S(1)} collective-permute-done((bf16[256,1280]{1,0:T(8,128)(2,1)S(1)}, bf16[256,1280]{1,0:T(8,128)(2,1)S(1)}, u32[]{:S(2)}, u32[]{:S(2)}) %collective-permute-start.18) | collective-permute-done | bytes 655392 | tf_op jit(solution)/shard_map/ppermute | solution.py:23
  87.8 2.7 %collective-permute-start.21 = (bf16[128,1280]{1,0:T(8,128)(2,1)S(1)}, bf16[128,1280]{1,0:T(8,128)(2,1)S(1)}, u32[]{:S(2)}, u32[]{:S(2)}) collective-permute-start(bf16[128,1280]{1,0:T(8,128)(2,1)S(1)} %slice.83), channel_id=1, source_target_pairs={{0,6},{1,7},{2,0},{3,1},{4,2},{5,3},{6,4},{7,5},{8,14},{9,15},{10,... | collective-permute-start | bytes 983048 | tf_op jit(solution)/shard_map/ppermute | solution.py:23
  91.3 3.4 %collective-permute-done.12 = bf16[128,1280]{1,0:T(8,128)(2,1)S(1)} collective-permute-done((bf16[128,1280]{1,0:T(8,128)(2,1)S(1)}, bf16[128,1280]{1,0:T(8,128)(2,1)S(1)}, u32[]{:S(2)}, u32[]{:S(2)}) %collective-permute-start.12) | collective-permute-done | bytes 327712 | tf_op jit(solution)/shard_map/ppermute | solution.py:23
  97.3 2.7 %collective-permute-start.15 = (bf16[256,384]{1,0:T(8,128)(2,1)S(1)}, bf16[256,384]{1,0:T(8,128)(2,1)S(1)}, u32[]{:S(2)}, u32[]{:S(2)}) collective-permute-start(bf16[256,384]{1,0:T(8,128)(2,1)S(1)} %fusion.58), channel_id=1, source_target_pairs={{0,6},{1,7},{2,0},{3,1},{4,2},{5,3},{6,4},{7,5},{8,14},{9,15},{10,... | collective-permute-start | bytes 589832 | tf_op jit(solution)/shard_map/ppermute | solution.py:23
  99.9 1.8 %collective-permute-done.20 = bf16[128,1280]{1,0:T(8,128)(2,1)S(1)} collective-permute-done((bf16[128,1280]{1,0:T(8,128)(2,1)S(1)}, bf16[128,1280]{1,0:T(8,128)(2,1)S(1)}, u32[]{:S(2)}, u32[]{:S(2)}) %collective-permute-start.20) | collective-permute-done | bytes 327712 | tf_op jit(solution)/shard_map/ppermute | solution.py:23
  104.2 2.7 %collective-permute-start.23 = (bf16[256,384]{1,0:T(8,128)(2,1)S(1)}, bf16[256,384]{1,0:T(8,128)(2,1)S(1)}, u32[]{:S(2)}, u32[]{:S(2)}) collective-permute-start(bf16[256,384]{1,0:T(8,128)(2,1)S(1)} %fusion.57), channel_id=1, source_target_pairs={{0,6},{1,7},{2,0},{3,1},{4,2},{5,3},{6,4},{7,5},{8,14},{9,15},{10,... | collective-permute-start | bytes 589832 | tf_op jit(solution)/shard_map/ppermute | solution.py:23
  107.0 2.9 %collective-permute-start.17 = (bf16[128,384]{1,0:T(8,128)(2,1)S(1)}, bf16[128,384]{1,0:T(8,128)(2,1)S(1)}, u32[]{:S(2)}, u32[]{:S(2)}) collective-permute-start(bf16[128,384]{1,0:T(8,128)(2,1)S(1)} %slice.81), channel_id=1, source_target_pairs={{0,6},{1,7},{2,0},{3,1},{4,2},{5,3},{6,4},{7,5},{8,14},{9,15},{10,... | collective-permute-start | bytes 294920 | tf_op jit(solution)/shard_map/ppermute | solution.py:23
  110.1 2.7 %collective-permute-start.25 = (bf16[128,384]{1,0:T(8,128)(2,1)S(1)}, bf16[128,384]{1,0:T(8,128)(2,1)S(1)}, u32[]{:S(2)}, u32[]{:S(2)}) collective-permute-start(bf16[128,384]{1,0:T(8,128)(2,1)S(1)} %slice.87), channel_id=1, source_target_pairs={{0,6},{1,7},{2,0},{3,1},{4,2},{5,3},{6,4},{7,5},{8,14},{9,15},{10,... | collective-permute-start | bytes 294920 | tf_op jit(solution)/shard_map/ppermute | solution.py:23
  113.0 1.2 convolution_convert_fusion.1
  114.3 1.7 %collective-permute-done.24 = bf16[128,384]{1,0:T(8,128)(2,1)S(1)} collective-permute-done((bf16[128,384]{1,0:T(8,128)(2,1)S(1)}, bf16[128,384]{1,0:T(8,128)(2,1)S(1)}, u32[]{:S(2)}, u32[]{:S(2)}) %collective-permute-start.24) | collective-permute-done | bytes 98336 | tf_op jit(solution)/shard_map/ppermute | solution.py:23
  116.0 1.2 convolution_convert_fusion
  117.2 1.2 pad_maximum_fusion
  118.4 9.2 %all-to-all-start.1 = ((bf16[32,16,1280]{2,1,0:T(8,128)(2,1)}), bf16[32,16,1280]{2,1,0:T(8,128)(2,1)S(1)}, u32[]{:S(2)}, u32[]{:S(2)}) async-start(bf16[32,16,1280]{2,1,0:T(8,128)(2,1)} %bitcast.94), calls=%async_computation.1 | async-start | bytes 2621440 | tf_op jit(solution)/shard_map/all_to_all | solution.py:278
  130.9 1.5 copy-done.11
  132.5 1.5 copy-done.12
  134.0 1.5 copy-done.13
  135.6 5.3 %shard_map.95 = (bf16[256,1280]{1,0:T(8,128)(2,1)S(1)}, bf16[256,1280]{1,0:T(8,128)(2,1)S(1)}) custom-call(s32[2]{0:T(128)S(1)} %pad_add_fusion.where_ref, bf16[256,1280]{1,0:T(8,128)(2,1)S(1)} %get-tuple-element.75.refs_0_, bf16[256,1280]{1,0:T(8,128)(2,1)S(1)} %collective-permute-done.1.refs_2_.refs_1_, bf16[256,1280]{1,0:T(8,128)(2,1)S(1)} %copy-done.2, ...), custom_call_target="tpu_custom_call" | custom-call | tf_op jit(solution)/shard_map/pallas_call | solution.py:199
  140.9 4.5 %collective-permute-start.26 = (bf16[256,1280]{1,0:T(8,128)(2,1)S(1)}, bf16[256,1280]{1,0:T(8,128)(2,1)S(1)}, u32[]{:S(2)}, u32[]{:S(2)}) collective-permute-start(bf16[256,1280]{1,0:T(8,128)(2,1)S(1)} %get-tuple-element.84), channel_id=1, source_target_pairs={{0,1},{1,0},{2,3},{3,2},{4,5},{5,4},{6,7},{7,6},{8,9},{9,8},{10,11... | collective-permute-start | bytes 1966088 | tf_op jit(solution)/shard_map/ppermute | solution.py:14
  145.4 1.7 %collective-permute-done.26 = bf16[256,1280]{1,0:T(8,128)(2,1)S(1)} collective-permute-done((bf16[256,1280]{1,0:T(8,128)(2,1)S(1)}, bf16[256,1280]{1,0:T(8,128)(2,1)S(1)}, u32[]{:S(2)}, u32[]{:S(2)}) %collective-permute-start.26) | collective-permute-done | bytes 655392 | tf_op jit(solution)/shard_map/ppermute | solution.py:14
  147.4 3.1 %collective-permute-start.28 = (bf16[64,1280]{1,0:T(8,128)(2,1)S(1)}, bf16[64,1280]{1,0:T(8,128)(2,1)S(1)}, u32[]{:S(2)}, u32[]{:S(2)}) collective-permute-start(bf16[64,1280]{1,0:T(8,128)(2,1)S(1)} %get-tuple-element.90), channel_id=1, source_target_pairs={{0,6},{1,7},{2,0},{3,1},{4,2},{5,3},{6,4},{7,5},{8,14},{9,15},{10,... | collective-permute-start | bytes 491528 | tf_op jit(solution)/shard_map/ppermute | solution.py:23
  150.5 1.1 collective-permute-start.29
  151.9 2.8 %collective-permute-done.27.refs_1_ = bf16[64,1280]{1,0:T(8,128)(2,1)S(1)} collective-permute-done((bf16[64,1280]{1,0:T(8,128)(2,1)S(1)}, bf16[64,1280]{1,0:T(8,128)(2,1)S(1)}, u32[]{:S(2)}, u32[]{:S(2)}) %collective-permute-start.27) | collective-permute-done | bytes 163872 | tf_op jit(solution)/shard_map/ppermute | solution.py:23
  154.7 2.4 %collective-permute-done.28.refs_2_ = bf16[64,1280]{1,0:T(8,128)(2,1)S(1)} collective-permute-done((bf16[64,1280]{1,0:T(8,128)(2,1)S(1)}, bf16[64,1280]{1,0:T(8,128)(2,1)S(1)}, u32[]{:S(2)}, u32[]{:S(2)}) %collective-permute-start.28) | collective-permute-done | bytes 163872 | tf_op jit(solution)/shard_map/ppermute | solution.py:23
  157.1 2.0 %collective-permute-done.29.refs_3_ = bf16[64,1280]{1,0:T(8,128)(2,1)S(1)} collective-permute-done((bf16[64,1280]{1,0:T(8,128)(2,1)S(1)}, bf16[64,1280]{1,0:T(8,128)(2,1)S(1)}, u32[]{:S(2)}, u32[]{:S(2)}) %collective-permute-start.29) | collective-permute-done | bytes 163872 | tf_op jit(solution)/shard_map/ppermute | solution.py:23
  160.2 3.1 %collective-permute-start.30 = (f32[128,640]{1,0:T(8,128)S(1)}, f32[128,640]{1,0:T(8,128)S(1)}, u32[]{:S(2)}, u32[]{:S(2)}) collective-permute-start(f32[128,640]{1,0:T(8,128)S(1)} %get-tuple-element.86), channel_id=1, source_target_pairs={{0,1},{1,0},{2,3},{3,2},{4,5},{5,4},{6,7},{7,6},{8,9},{9,8},{10,11... | collective-permute-start | bytes 983048 | tf_op jit(solution)/shard_map/ppermute | solution.py:14
  163.3 1.3 collective-permute-done.30
  (100 shorter events, 20.6 us)
Async XLA Ops:
  0.0 4.5 %collective-permute-start = (bf16[128,640]{1,0:T(8,128)(2,1)}, bf16[128,640]{1,0:T(8,128)(2,1)S(1)}, u32[]{:S(2)}, u32[]{:S(2)}) collective-permute-start(bf16[128,640]{1,0:T(8,128)(2,1)} %tokens.1), channel_id=1, source_target_pairs={{0,1},{1,0},{2,3},{3,2},{4,5},{5,4},{6,7},{7,6},{8,9},{9,8},{10,11... | collective-permute-start | bytes 491528 | tf_op jit(solution)/shard_map/ppermute | solution.py:14
  7.0 32.0 %collective-permute-start.3 = (bf16[192,5120]{1,0:T(8,128)(2,1)}, bf16[192,5120]{1,0:T(8,128)(2,1)}, u32[]{:S(2)}, u32[]{:S(2)}) collective-permute-start(bf16[192,5120]{1,0:T(8,128)(2,1)} %bitcast.90), channel_id=1, source_target_pairs={{0,1},{1,0},{2,3},{3,2},{4,5},{5,4},{6,7},{7,6},{8,9},{9,8},{10,11... | collective-permute-start | bytes 5898248 | tf_op jit(solution)/shard_map/ppermute | solution.py:14
  7.4 31.7 %collective-permute-start.4 = (bf16[192,5120]{1,0:T(8,128)(2,1)}, bf16[192,5120]{1,0:T(8,128)(2,1)}, u32[]{:S(2)}, u32[]{:S(2)}) collective-permute-start(bf16[192,5120]{1,0:T(8,128)(2,1)} %bitcast.92), channel_id=1, source_target_pairs={{0,1},{1,0},{2,3},{3,2},{4,5},{5,4},{6,7},{7,6},{8,9},{9,8},{10,11... | collective-permute-start | bytes 5898248 | tf_op jit(solution)/shard_map/ppermute | solution.py:14
  7.5 45.4 %all-to-all-start = ((bf16[32,16,1280]{2,1,0:T(8,128)(2,1)}), bf16[32,16,1280]{2,1,0:T(8,128)(2,1)}, u32[]{:S(2)}, u32[]{:S(2)}) async-start(bf16[32,16,1280]{2,1,0:T(8,128)(2,1)} %bitcast.7), calls=%async_computation | async-start | bytes 2621440 | tf_op jit(solution)/shard_map/all_to_all | solution.py:278
  17.1 1.5 copy-start.8
  19.1 17.4 %collective-permute-start.5 = (bf16[256,1280]{1,0:T(8,128)(2,1)S(1)}, bf16[256,1280]{1,0:T(8,128)(2,1)S(1)}, u32[]{:S(2)}, u32[]{:S(2)}) collective-permute-start(bf16[256,1280]{1,0:T(8,128)(2,1)S(1)} %get-tuple-element.58), channel_id=1, source_target_pairs={{0,4},{1,5},{2,6},{3,7},{4,0},{5,1},{6,2},{7,3},{8,12},{9,13},{10,... | collective-permute-start | bytes 1966088 | tf_op jit(solution)/shard_map/ppermute | solution.py:23
  22.0 29.5 %collective-permute-start.1 = (bf16[256,1280]{1,0:T(8,128)(2,1)S(1)}, bf16[256,1280]{1,0:T(8,128)(2,1)S(1)}, u32[]{:S(2)}, u32[]{:S(2)}) collective-permute-start(bf16[256,1280]{1,0:T(8,128)(2,1)S(1)} %get-tuple-element.50), channel_id=1, source_target_pairs={{0,2},{1,3},{2,4},{3,5},{4,6},{5,7},{6,0},{7,1},{8,10},{9,11},{10,... | collective-permute-start | bytes 1966088 | tf_op jit(solution)/shard_map/ppermute | solution.py:23
  22.3 29.1 %collective-permute-start.2 = (bf16[256,1280]{1,0:T(8,128)(2,1)S(1)}, bf16[256,1280]{1,0:T(8,128)(2,1)S(1)}, u32[]{:S(2)}, u32[]{:S(2)}) collective-permute-start(bf16[256,1280]{1,0:T(8,128)(2,1)S(1)} %get-tuple-element.51), channel_id=1, source_target_pairs={{0,6},{1,7},{2,0},{3,1},{4,2},{5,3},{6,4},{7,5},{8,14},{9,15},{10,... | collective-permute-start | bytes 1966088 | tf_op jit(solution)/shard_map/ppermute | solution.py:23
  36.5 15.6 %collective-permute-start.6 = (bf16[256,1280]{1,0:T(8,128)(2,1)S(1)}, bf16[256,1280]{1,0:T(8,128)(2,1)S(1)}, u32[]{:S(2)}, u32[]{:S(2)}) collective-permute-start(bf16[256,1280]{1,0:T(8,128)(2,1)S(1)} %get-tuple-element.75.refs_0_), channel_id=1, source_target_pairs={{0,1},{1,0},{2,3},{3,2},{4,5},{5,4},{6,7},{7,6},{8,9},{9,8},{10,11... | collective-permute-start | bytes 1966088 | tf_op jit(solution)/shard_map/ppermute | solution.py:14
  39.0 13.0 %collective-permute-start.9 = (bf16[256,1280]{1,0:T(8,128)(2,1)S(1)}, bf16[256,1280]{1,0:T(8,128)(2,1)S(1)}, u32[]{:S(2)}, u32[]{:S(2)}) collective-permute-start(bf16[256,1280]{1,0:T(8,128)(2,1)S(1)} %collective-permute-done.5.refs_6_.refs_3_), channel_id=1, source_target_pairs={{0,1},{1,0},{2,3},{3,2},{4,5},{5,4},{6,7},{7,6},{8,9},{9,8},{10,11... | collective-permute-start | bytes 1966088 | tf_op jit(solution)/shard_map/ppermute | solution.py:14
  39.0 1.5 copy-start.9
  40.6 1.5 copy-start.10
  45.3 3.1 %copy-start = (bf16[4,768,1280]{2,1,0:T(8,128)(2,1)}, bf16[4,768,1280]{2,1,0:T(8,128)(2,1)S(1)}, u32[]{:S(2)}) copy-start(bf16[4,768,1280]{2,1,0:T(8,128)(2,1)S(1)} %shard_map.93) | copy-start | bytes 23592964
  51.4 12.9 %copy-start.1 = (bf16[256,1280]{1,0:T(8,128)(2,1)}, bf16[256,1280]{1,0:T(8,128)(2,1)S(1)}, u32[]{:S(2)}) copy-start(bf16[256,1280]{1,0:T(8,128)(2,1)S(1)} %collective-permute-done.2.refs_4_.refs_2_) | copy-start | bytes 1966084
  51.4 2.5 %collective-permute-start.7 = (bf16[256,1280]{1,0:T(8,128)(2,1)S(1)}, bf16[256,1280]{1,0:T(8,128)(2,1)}, u32[]{:S(2)}, u32[]{:S(2)}) collective-permute-start(bf16[256,1280]{1,0:T(8,128)(2,1)S(1)} %collective-permute-done.1.refs_2_.refs_1_), channel_id=1, source_target_pairs={{0,1},{1,0},{2,3},{3,2},{4,5},{5,4},{6,7},{7,6},{8,9},{9,8},{10,11... | collective-permute-start | bytes 1966088 | tf_op jit(solution)/shard_map/ppermute | solution.py:14
  52.1 2.8 %collective-permute-start.8 = (bf16[256,1280]{1,0:T(8,128)(2,1)S(1)}, bf16[256,1280]{1,0:T(8,128)(2,1)}, u32[]{:S(2)}, u32[]{:S(2)}) collective-permute-start(bf16[256,1280]{1,0:T(8,128)(2,1)S(1)} %collective-permute-done.2.refs_4_.refs_2_), channel_id=1, source_target_pairs={{0,1},{1,0},{2,3},{3,2},{4,5},{5,4},{6,7},{7,6},{8,9},{9,8},{10,11... | collective-permute-start | bytes 1966088 | tf_op jit(solution)/shard_map/ppermute | solution.py:14
  52.1 12.2 %copy-start.3 = (bf16[256,1280]{1,0:T(8,128)(2,1)}, bf16[256,1280]{1,0:T(8,128)(2,1)S(1)}, u32[]{:S(2)}) copy-start(bf16[256,1280]{1,0:T(8,128)(2,1)S(1)} %collective-permute-done.6.refs_1_.refs_4_) | copy-start | bytes 1966084
  54.9 11.5 %slice-start = ((s8[7864320]{0:T(1024)(128)(4,1)}), s8[4194304]{0:T(1024)(128)(4,1)S(1)}, s32[]{:S(2)}) async-start(s8[7864320]{0:T(1024)(128)(4,1)} %bitcast.86), calls=%async_computation.2 | async-start | bytes 8388608
  56.4 17.2 %collective-permute-start.10 = (bf16[256,1280]{1,0:T(8,128)(2,1)S(1)}, bf16[256,1280]{1,0:T(8,128)(2,1)S(1)}, u32[]{:S(2)}, u32[]{:S(2)}) collective-permute-start(bf16[256,1280]{1,0:T(8,128)(2,1)S(1)} %get-tuple-element.88), channel_id=1, source_target_pairs={{0,2},{1,3},{2,4},{3,5},{4,6},{5,7},{6,0},{7,1},{8,10},{9,11},{10,... | collective-permute-start | bytes 1966088 | tf_op jit(solution)/shard_map/ppermute | solution.py:23
  57.6 16.0 %collective-permute-start.11 = (bf16[256,1280]{1,0:T(8,128)(2,1)S(1)}, bf16[256,1280]{1,0:T(8,128)(2,1)S(1)}, u32[]{:S(2)}, u32[]{:S(2)}) collective-permute-start(bf16[256,1280]{1,0:T(8,128)(2,1)S(1)} %get-tuple-element.88), channel_id=1, source_target_pairs={{0,6},{1,7},{2,0},{3,1},{4,2},{5,3},{6,4},{7,5},{8,14},{9,15},{10,... | collective-permute-start | bytes 1966088 | tf_op jit(solution)/shard_map/ppermute | solution.py:23
  59.1 5.2 %copy-start.6 = (bf16[256,1280]{1,0:T(8,128)(2,1)S(1)}, bf16[256,1280]{1,0:T(8,128)(2,1)}, u32[]{:S(2)}) copy-start(bf16[256,1280]{1,0:T(8,128)(2,1)} %copy-done.5) | copy-start | bytes 1966084
  59.1 28.5 %collective-permute-start.18 = (bf16[256,1280]{1,0:T(8,128)(2,1)S(1)}, bf16[256,1280]{1,0:T(8,128)(2,1)S(1)}, u32[]{:S(2)}, u32[]{:S(2)}) collective-permute-start(bf16[256,1280]{1,0:T(8,128)(2,1)S(1)} %get-tuple-element.87), channel_id=1, source_target_pairs={{0,2},{1,3},{2,4},{3,5},{4,6},{5,7},{6,0},{7,1},{8,10},{9,11},{10,... | collective-permute-start | bytes 1966088 | tf_op jit(solution)/shard_map/ppermute | solution.py:23
  59.1 28.6 %collective-permute-start.19 = (bf16[256,1280]{1,0:T(8,128)(2,1)S(1)}, bf16[256,1280]{1,0:T(8,128)(2,1)S(1)}, u32[]{:S(2)}, u32[]{:S(2)}) collective-permute-start(bf16[256,1280]{1,0:T(8,128)(2,1)S(1)} %get-tuple-element.87), channel_id=1, source_target_pairs={{0,6},{1,7},{2,0},{3,1},{4,2},{5,3},{6,4},{7,5},{8,14},{9,15},{10,... | collective-permute-start | bytes 1966088 | tf_op jit(solution)/shard_map/ppermute | solution.py:23
  64.3 2.4 %slice-start.1 = ((s8[7864320]{0:T(1024)(128)(4,1)}), s8[3670016]{0:T(1024)(128)(4,1)S(1)}, s32[]{:S(2)}) async-start(s8[7864320]{0:T(1024)(128)(4,1)} %bitcast.86), calls=%async_computation.3 | async-start | bytes 7340032
  73.6 21.0 %collective-permute-start.12 = (bf16[128,1280]{1,0:T(8,128)(2,1)S(1)}, bf16[128,1280]{1,0:T(8,128)(2,1)S(1)}, u32[]{:S(2)}, u32[]{:S(2)}) collective-permute-start(bf16[128,1280]{1,0:T(8,128)(2,1)S(1)} %slice.65), channel_id=1, source_target_pairs={{0,2},{1,3},{2,4},{3,5},{4,6},{5,7},{6,0},{7,1},{8,10},{9,11},{10,... | collective-permute-start | bytes 983048 | tf_op jit(solution)/shard_map/ppermute | solution.py:23
  75.0 20.5 %collective-permute-start.13 = (bf16[128,1280]{1,0:T(8,128)(2,1)S(1)}, bf16[128,1280]{1,0:T(8,128)(2,1)S(1)}, u32[]{:S(2)}, u32[]{:S(2)}) collective-permute-start(bf16[128,1280]{1,0:T(8,128)(2,1)S(1)} %slice.67), channel_id=1, source_target_pairs={{0,6},{1,7},{2,0},{3,1},{4,2},{5,3},{6,4},{7,5},{8,14},{9,15},{10,... | collective-permute-start | bytes 983048 | tf_op jit(solution)/shard_map/ppermute | solution.py:23
  87.7 14.0 %collective-permute-start.20 = (bf16[128,1280]{1,0:T(8,128)(2,1)S(1)}, bf16[128,1280]{1,0:T(8,128)(2,1)S(1)}, u32[]{:S(2)}, u32[]{:S(2)}) collective-permute-start(bf16[128,1280]{1,0:T(8,128)(2,1)S(1)} %slice.82), channel_id=1, source_target_pairs={{0,2},{1,3},{2,4},{3,5},{4,6},{5,7},{6,0},{7,1},{8,10},{9,11},{10,... | collective-permute-start | bytes 983048 | tf_op jit(solution)/shard_map/ppermute | solution.py:23
  87.8 14.7 %collective-permute-start.21 = (bf16[128,1280]{1,0:T(8,128)(2,1)S(1)}, bf16[128,1280]{1,0:T(8,128)(2,1)S(1)}, u32[]{:S(2)}, u32[]{:S(2)}) collective-permute-start(bf16[128,1280]{1,0:T(8,128)(2,1)S(1)} %slice.83), channel_id=1, source_target_pairs={{0,6},{1,7},{2,0},{3,1},{4,2},{5,3},{6,4},{7,5},{8,14},{9,15},{10,... | collective-permute-start | bytes 983048 | tf_op jit(solution)/shard_map/ppermute | solution.py:23
  97.2 9.7 %collective-permute-start.14 = (bf16[256,384]{1,0:T(8,128)(2,1)S(1)}, bf16[256,384]{1,0:T(8,128)(2,1)S(1)}, u32[]{:S(2)}, u32[]{:S(2)}) collective-permute-start(bf16[256,384]{1,0:T(8,128)(2,1)S(1)} %fusion.58), channel_id=1, source_target_pairs={{0,2},{1,3},{2,4},{3,5},{4,6},{5,7},{6,0},{7,1},{8,10},{9,11},{10,... | collective-permute-start | bytes 589832 | tf_op jit(solution)/shard_map/ppermute | solution.py:23
  97.3 9.8 %collective-permute-start.15 = (bf16[256,384]{1,0:T(8,128)(2,1)S(1)}, bf16[256,384]{1,0:T(8,128)(2,1)S(1)}, u32[]{:S(2)}, u32[]{:S(2)}) collective-permute-start(bf16[256,384]{1,0:T(8,128)(2,1)S(1)} %fusion.58), channel_id=1, source_target_pairs={{0,6},{1,7},{2,0},{3,1},{4,2},{5,3},{6,4},{7,5},{8,14},{9,15},{10,... | collective-permute-start | bytes 589832 | tf_op jit(solution)/shard_map/ppermute | solution.py:23
  104.1 5.8 %collective-permute-start.22 = (bf16[256,384]{1,0:T(8,128)(2,1)S(1)}, bf16[256,384]{1,0:T(8,128)(2,1)S(1)}, u32[]{:S(2)}, u32[]{:S(2)}) collective-permute-start(bf16[256,384]{1,0:T(8,128)(2,1)S(1)} %fusion.57), channel_id=1, source_target_pairs={{0,2},{1,3},{2,4},{3,5},{4,6},{5,7},{6,0},{7,1},{8,10},{9,11},{10,... | collective-permute-start | bytes 589832 | tf_op jit(solution)/shard_map/ppermute | solution.py:23
  104.2 5.9 %collective-permute-start.23 = (bf16[256,384]{1,0:T(8,128)(2,1)S(1)}, bf16[256,384]{1,0:T(8,128)(2,1)S(1)}, u32[]{:S(2)}, u32[]{:S(2)}) collective-permute-start(bf16[256,384]{1,0:T(8,128)(2,1)S(1)} %fusion.57), channel_id=1, source_target_pairs={{0,6},{1,7},{2,0},{3,1},{4,2},{5,3},{6,4},{7,5},{8,14},{9,15},{10,... | collective-permute-start | bytes 589832 | tf_op jit(solution)/shard_map/ppermute | solution.py:23
  106.9 6.1 %collective-permute-start.16 = (bf16[128,384]{1,0:T(8,128)(2,1)S(1)}, bf16[128,384]{1,0:T(8,128)(2,1)S(1)}, u32[]{:S(2)}, u32[]{:S(2)}) collective-permute-start(bf16[128,384]{1,0:T(8,128)(2,1)S(1)} %slice.80), channel_id=1, source_target_pairs={{0,2},{1,3},{2,4},{3,5},{4,6},{5,7},{6,0},{7,1},{8,10},{9,11},{10,... | collective-permute-start | bytes 294920 | tf_op jit(solution)/shard_map/ppermute | solution.py:23
  107.0 6.0 %collective-permute-start.17 = (bf16[128,384]{1,0:T(8,128)(2,1)S(1)}, bf16[128,384]{1,0:T(8,128)(2,1)S(1)}, u32[]{:S(2)}, u32[]{:S(2)}) collective-permute-start(bf16[128,384]{1,0:T(8,128)(2,1)S(1)} %slice.81), channel_id=1, source_target_pairs={{0,6},{1,7},{2,0},{3,1},{4,2},{5,3},{6,4},{7,5},{8,14},{9,15},{10,... | collective-permute-start | bytes 294920 | tf_op jit(solution)/shard_map/ppermute | solution.py:23
  110.0 6.0 %collective-permute-start.24 = (bf16[128,384]{1,0:T(8,128)(2,1)S(1)}, bf16[128,384]{1,0:T(8,128)(2,1)S(1)}, u32[]{:S(2)}, u32[]{:S(2)}) collective-permute-start(bf16[128,384]{1,0:T(8,128)(2,1)S(1)} %slice.86), channel_id=1, source_target_pairs={{0,2},{1,3},{2,4},{3,5},{4,6},{5,7},{6,0},{7,1},{8,10},{9,11},{10,... | collective-permute-start | bytes 294920 | tf_op jit(solution)/shard_map/ppermute | solution.py:23
  110.1 5.9 %collective-permute-start.25 = (bf16[128,384]{1,0:T(8,128)(2,1)S(1)}, bf16[128,384]{1,0:T(8,128)(2,1)S(1)}, u32[]{:S(2)}, u32[]{:S(2)}) collective-permute-start(bf16[128,384]{1,0:T(8,128)(2,1)S(1)} %slice.87), channel_id=1, source_target_pairs={{0,6},{1,7},{2,0},{3,1},{4,2},{5,3},{6,4},{7,5},{8,14},{9,15},{10,... | collective-permute-start | bytes 294920 | tf_op jit(solution)/shard_map/ppermute | solution.py:23
  118.4 40.7 %all-to-all-start.1 = ((bf16[32,16,1280]{2,1,0:T(8,128)(2,1)}), bf16[32,16,1280]{2,1,0:T(8,128)(2,1)S(1)}, u32[]{:S(2)}, u32[]{:S(2)}) async-start(bf16[32,16,1280]{2,1,0:T(8,128)(2,1)} %bitcast.94), calls=%async_computation.1 | async-start | bytes 2621440 | tf_op jit(solution)/shard_map/all_to_all | solution.py:278
  127.7 1.1 copy-start.2
  130.9 1.5 copy-start.11
  132.5 1.5 copy-start.12
  134.0 1.5 copy-start.13
  140.9 10.8 %copy-start.15 = (s32[128,6]{0,1:T(8,128)S(1)}, s32[128,6]{0,1:T(8,128)}, u32[]{:S(2)}) copy-start(s32[128,6]{0,1:T(8,128)} %param.10) | copy-start | bytes 9220
  140.9 10.7 %copy-start.16 = (f32[128,6]{0,1:T(8,128)S(1)}, f32[128,6]{0,1:T(8,128)}, u32[]{:S(2)}) copy-start(f32[128,6]{0,1:T(8,128)} %param.11) | copy-start | bytes 9220
  140.9 6.2 %collective-permute-start.26 = (bf16[256,1280]{1,0:T(8,128)(2,1)S(1)}, bf16[256,1280]{1,0:T(8,128)(2,1)S(1)}, u32[]{:S(2)}, u32[]{:S(2)}) collective-permute-start(bf16[256,1280]{1,0:T(8,128)(2,1)S(1)} %get-tuple-element.84), channel_id=1, source_target_pairs={{0,1},{1,0},{2,3},{3,2},{4,5},{5,4},{6,7},{7,6},{8,9},{9,8},{10,11... | collective-permute-start | bytes 1966088 | tf_op jit(solution)/shard_map/ppermute | solution.py:14
  147.3 7.4 %collective-permute-start.27 = (bf16[64,1280]{1,0:T(8,128)(2,1)S(1)}, bf16[64,1280]{1,0:T(8,128)(2,1)S(1)}, u32[]{:S(2)}, u32[]{:S(2)}) collective-permute-start(bf16[64,1280]{1,0:T(8,128)(2,1)S(1)} %get-tuple-element.91), channel_id=1, source_target_pairs={{0,2},{1,3},{2,4},{3,5},{4,6},{5,7},{6,0},{7,1},{8,10},{9,11},{10,... | collective-permute-start | bytes 491528 | tf_op jit(solution)/shard_map/ppermute | solution.py:23
  147.4 9.7 %collective-permute-start.28 = (bf16[64,1280]{1,0:T(8,128)(2,1)S(1)}, bf16[64,1280]{1,0:T(8,128)(2,1)S(1)}, u32[]{:S(2)}, u32[]{:S(2)}) collective-permute-start(bf16[64,1280]{1,0:T(8,128)(2,1)S(1)} %get-tuple-element.90), channel_id=1, source_target_pairs={{0,6},{1,7},{2,0},{3,1},{4,2},{5,3},{6,4},{7,5},{8,14},{9,15},{10,... | collective-permute-start | bytes 491528 | tf_op jit(solution)/shard_map/ppermute | solution.py:23
  150.5 8.5 %collective-permute-start.29 = (bf16[64,1280]{1,0:T(8,128)(2,1)S(1)}, bf16[64,1280]{1,0:T(8,128)(2,1)S(1)}, u32[]{:S(2)}, u32[]{:S(2)}) collective-permute-start(bf16[64,1280]{1,0:T(8,128)(2,1)S(1)} %get-tuple-element.89), channel_id=1, source_target_pairs={{0,4},{1,5},{2,6},{3,7},{4,0},{5,1},{6,2},{7,3},{8,12},{9,13},{10,... | collective-permute-start | bytes 491528 | tf_op jit(solution)/shard_map/ppermute | solution.py:23
  160.2 4.4 %collective-permute-start.30 = (f32[128,640]{1,0:T(8,128)S(1)}, f32[128,640]{1,0:T(8,128)S(1)}, u32[]{:S(2)}, u32[]{:S(2)}) collective-permute-start(f32[128,640]{1,0:T(8,128)S(1)} %get-tuple-element.86), channel_id=1, source_target_pairs={{0,1},{1,0},{2,3},{3,2},{4,5},{5,4},{6,7},{7,6},{8,9},{9,8},{10,11... | collective-permute-start | bytes 983048 | tf_op jit(solution)/shard_map/ppermute | solution.py:14
  (4 other events, 4.0 us)

commit v5 on v4

--- a/solution.py
+++ b/solution.py
@@ -144,6 +144,26 @@
         out_specs=pl.BlockSpec((2 * CHIPS * unit, tile), lambda n: (0, n)),
         compiler_params=pltpu.CompilerParams(vmem_limit_bytes=24 << 20),
     )(*[part for pair in zip(own, other) for part in pair])
+
+
+def split_kernel(rows, *outs):
+    low = 0
+    for out in outs:
+        out[...] = rows[low : low + out.shape[0], :]
+        low += out.shape[0]
+
+
+def split_rows(rows):
+    count, width = rows.shape
+    tile = width // 2
+    return pl.pallas_call(
+        split_kernel,
+        out_shape=[jax.ShapeDtypeStruct((count // 2, width), BF16)] * 2,
+        grid=(2,),
+        in_specs=[pl.BlockSpec((count, tile), lambda n: (0, n))],
+        out_specs=[pl.BlockSpec((count // 2, tile), lambda n: (0, n))] * 2,
+        compiler_params=pltpu.CompilerParams(vmem_limit_bytes=24 << 20),
+    )(rows)
 
 
 def act_of(gate, up):
@@ -294,8 +314,7 @@
     )
     down_all = join_down(down_mine.shape[0], own_pack, other_pack)
 
-    cut = rows.shape[0] // 2
-    pieces = [rows[:cut], rows[cut:]]
+    pieces = split_rows(rows)
     sides = [(shift_chips(piece, 1), shift_chips(piece, -1)) for piece in pieces]
     acts = [project_rows(piece, weights[0]) for piece in pieces]
     sides[0], acts, down_all = lax.optimization_barrier((sides[0], acts, down_all))

time: 166 us -> 165 us (level)
    unnamed x38 -> x36, local copies, waits for them, and re-layouts: 17.8 us -> 18.8 us
  transfers between devices with their start and end apart: 33 -> 33, of which waited for: 16 -> 16; matrix products, arithmetic and copies ran while one was open for 8% -> 7% of each run, Pallas kernels for 7% -> 7%
where the time goes in v5:
time: 165 us; the launch traced here: 164 us
  starting transfers between devices  66.6 us (40%)
  waiting for transfers between devices  49 us (30%)
  local copies, waits for them, and re-layouts  19 us (12%)
  Pallas kernels  14.2 us (9%)
  matrix products  11.6 us (7%)
  other arithmetic  3.51 us (2%)
    ppermute x22, waiting for transfers between devices, shift_chips(): return lax.ppermute(value, 'loop', pairs)  44.6 us
    ppermute x22, starting transfers between devices, shift_chips(): return lax.ppermute(value, 'loop', pairs)  32.2 us
    unnamed x36, local copies, waits for them, and re-layouts  18.8 us
    all_to_all x2, starting transfers between devices, exchange(): lax.all_to_all(value, 'expert', split_axis=0, concat_axis=0, tiled=True)  18.7 us
    ppermute x9, starting transfers between devices, swap_cores(): return lax.ppermute(value, 'loop', [(i, i ^ 1) for i in range(2 * CHIPS)])  15.7 us
    dot_general x10, matrix products, project_rows(): lax.dot_general(rows, weight, (((1,), (1,)), ((), ())), preferred_element...  9.03 us
    pallas_call x1, Pallas kernels, shared_terms(): pl.pallas_call(shared_kernel, out_shape=[jax.ShapeDtypeStruct(shape, BF16...  5.43 us
    ppermute x9, waiting for transfers between devices, swap_cores(): return lax.ppermute(value, 'loop', [(i, i ^ 1) for i in range(2 * CHIPS)])  4.4 us
  transfers between devices with their start and end apart: 33, of which 16 were waited for; matrix products, arithmetic and copies ran while one was open for 7% of the time, Pallas kernels for 7%

profile of v5, /device:TPU:1, one launch (start us, length us, event | category | flops | bytes accessed | tf_op | source)
XLA Modules:
  0.0 164.4 jit_solution(9506679673155470450)
XLA Ops:
  0.0 3.2 %collective-permute-start = (bf16[128,640]{1,0:T(8,128)(2,1)}, bf16[128,640]{1,0:T(8,128)(2,1)S(1)}, u32[]{:S(2)}, u32[]{:S(2)}) collective-permute-start(bf16[128,640]{1,0:T(8,128)(2,1)} %tokens.1), channel_id=1, source_target_pairs={{0,1},{1,0},{2,3},{3,2},{4,5},{5,4},{6,7},{7,6},{8,9},{9,8},{10,11... | collective-permute-start | bytes 491528 | tf_op jit(solution)/shard_map/ppermute | solution.py:14
  5.4 1.6 shard_map.91
  7.5 9.5 %all-to-all-start = ((bf16[32,16,1280]{2,1,0:T(8,128)(2,1)}), bf16[32,16,1280]{2,1,0:T(8,128)(2,1)S(1)}, u32[]{:S(2)}, u32[]{:S(2)}) async-start(bf16[32,16,1280]{2,1,0:T(8,128)(2,1)} %bitcast.7), calls=%async_computation | async-start | bytes 2621440 | tf_op jit(solution)/shard_map/all_to_all | solution.py:298
  17.0 1.5 copy-done.7
  19.0 2.8 %collective-permute-start.5 = (bf16[256,1280]{1,0:T(8,128)(2,1)S(1)}, bf16[256,1280]{1,0:T(8,128)(2,1)S(1)}, u32[]{:S(2)}, u32[]{:S(2)}) collective-permute-start(bf16[256,1280]{1,0:T(8,128)(2,1)S(1)} %get-tuple-element.60), channel_id=1, source_target_pairs={{0,4},{1,5},{2,6},{3,7},{4,0},{5,1},{6,2},{7,3},{8,12},{9,13},{10,... | collective-permute-start | bytes 1966088 | tf_op jit(solution)/shard_map/ppermute | solution.py:23
  22.2 2.4 %collective-permute-start.2 = (bf16[256,1280]{1,0:T(8,128)(2,1)S(1)}, bf16[256,1280]{1,0:T(8,128)(2,1)}, u32[]{:S(2)}, u32[]{:S(2)}) collective-permute-start(bf16[256,1280]{1,0:T(8,128)(2,1)S(1)} %get-tuple-element.53), channel_id=1, source_target_pairs={{0,6},{1,7},{2,0},{3,1},{4,2},{5,3},{6,4},{7,5},{8,14},{9,15},{10,... | collective-permute-start | bytes 1966088 | tf_op jit(solution)/shard_map/ppermute | solution.py:23
  24.5 11.8 %collective-permute-done.5.refs_6_.refs_3_ = bf16[256,1280]{1,0:T(8,128)(2,1)S(1)} collective-permute-done((bf16[256,1280]{1,0:T(8,128)(2,1)S(1)}, bf16[256,1280]{1,0:T(8,128)(2,1)S(1)}, u32[]{:S(2)}, u32[]{:S(2)}) %collective-permute-start.5) | collective-permute-done | bytes 655392 | tf_op jit(solution)/shard_map/ppermute | solution.py:23
  36.3 2.6 %collective-permute-start.6 = (bf16[256,1280]{1,0:T(8,128)(2,1)S(1)}, bf16[256,1280]{1,0:T(8,128)(2,1)S(1)}, u32[]{:S(2)}, u32[]{:S(2)}) collective-permute-start(bf16[256,1280]{1,0:T(8,128)(2,1)S(1)} %get-tuple-element.79.refs_0_), channel_id=1, source_target_pairs={{0,1},{1,0},{2,3},{3,2},{4,5},{5,4},{6,7},{7,6},{8,9},{9,8},{10,11... | collective-permute-start | bytes 1966088 | tf_op jit(solution)/shard_map/ppermute | solution.py:14
  39.0 1.5 copy-done.8
  40.5 1.5 copy-done.9
  42.0 3.2 %shard_map.93 = bf16[4,768,1280]{2,1,0:T(8,128)(2,1)S(1)} custom-call(s32[1]{0:T(128)} %bitcast.chip_ref, bf16[192,5120]{1,0:T(8,128)(2,1)S(1)} %bitcast.94, bf16[192,5120]{1,0:T(8,128)(2,1)} %collective-permute-done.3.refs_1_, bf16[192,5120]{1,0:T(8,128)(2,1)S(1)} %bitcast.96, bf16[192,5120]{1,0:T(8,128)(2,1)} %collective-permute-done.4.refs_3_), custom_call_target="tpu_custom_call" | custom-call | tf_op jit(solution)/shard_map/pallas_call | solution.py:82
  45.2 3.1 %copy-done = bf16[4,768,1280]{2,1,0:T(8,128)(2,1)} copy-done((bf16[4,768,1280]{2,1,0:T(8,128)(2,1)}, bf16[4,768,1280]{2,1,0:T(8,128)(2,1)S(1)}, u32[]{:S(2)}) %copy-start) | copy-done | bytes 7864344
  48.3 3.0 %collective-permute-done.1.refs_2_.refs_1_ = bf16[256,1280]{1,0:T(8,128)(2,1)S(1)} collective-permute-done((bf16[256,1280]{1,0:T(8,128)(2,1)S(1)}, bf16[256,1280]{1,0:T(8,128)(2,1)S(1)}, u32[]{:S(2)}, u32[]{:S(2)}) %collective-permute-start.1) | collective-permute-done | bytes 655392 | tf_op jit(solution)/shard_map/ppermute | solution.py:23
  55.5 1.2 collective-permute-start.10
  56.6 1.6 collective-permute-start.11
  58.2 2.7 %collective-permute-start.19 = (bf16[256,1280]{1,0:T(8,128)(2,1)S(1)}, bf16[256,1280]{1,0:T(8,128)(2,1)S(1)}, u32[]{:S(2)}, u32[]{:S(2)}) collective-permute-start(bf16[256,1280]{1,0:T(8,128)(2,1)S(1)} %get-tuple-element.64), channel_id=1, source_target_pairs={{0,6},{1,7},{2,0},{3,1},{4,2},{5,3},{6,4},{7,5},{8,14},{9,15},{10,... | collective-permute-start | bytes 1966088 | tf_op jit(solution)/shard_map/ppermute | solution.py:23
  60.9 2.3 %fusion.16 = f32[256,768]{1,0:T(8,128)S(1)} fusion(bf16[256,1280]{1,0:T(8,128)(2,1)S(1)} %get-tuple-element.64, bf16[4,768,1280]{2,1,0:T(8,128)(2,1)} %copy-done), kind=kOutput, calls=%fused_computation.18 | convolution fusion | flops 503316480 | bytes 3407872 | tf_op jit(solution)/shard_map/dot_general | solution.py:31
  64.3 2.1 %shard_map.95 = bf16[1536,1280]{1,0:T(8,128)(2,1)S(1)} custom-call(bf16[256,1280]{1,0:T(8,128)(2,1)S(1)} %get-tuple-element.79.refs_0_, bf16[256,1280]{1,0:T(8,128)(2,1)S(1)} %copy-done.2, bf16[256,1280]{1,0:T(8,128)(2,1)S(1)} %collective-permute-done.1.refs_2_.refs_1_, bf16[256,1280]{1,0:T(8,128)(2,1)} %collective-permute-done.7.refs_3_.refs_5_, ...), custom_call_target="tpu_custom_call" | custom-call | tf_op jit(solution)/shard_map/pallas_call | solution.py:139
  67.6 5.1 %collective-permute-done.10 = bf16[256,1280]{1,0:T(8,128)(2,1)S(1)} collective-permute-done((bf16[256,1280]{1,0:T(8,128)(2,1)S(1)}, bf16[256,1280]{1,0:T(8,128)(2,1)S(1)}, u32[]{:S(2)}, u32[]{:S(2)}) %collective-permute-start.10) | collective-permute-done | bytes 655392 | tf_op jit(solution)/shard_map/ppermute | solution.py:23
  74.1 2.2 %collective-permute-start.13 = (bf16[128,1280]{1,0:T(8,128)(2,1)S(1)}, bf16[128,1280]{1,0:T(8,128)(2,1)S(1)}, u32[]{:S(2)}, u32[]{:S(2)}) collective-permute-start(bf16[128,1280]{1,0:T(8,128)(2,1)S(1)} %slice.59), channel_id=1, source_target_pairs={{0,6},{1,7},{2,0},{3,1},{4,2},{5,3},{6,4},{7,5},{8,14},{9,15},{10,... | collective-permute-start | bytes 983048 | tf_op jit(solution)/shard_map/ppermute | solution.py:23
  76.3 10.4 %collective-permute-done.18 = bf16[256,1280]{1,0:T(8,128)(2,1)S(1)} collective-permute-done((bf16[256,1280]{1,0:T(8,128)(2,1)S(1)}, bf16[256,1280]{1,0:T(8,128)(2,1)S(1)}, u32[]{:S(2)}, u32[]{:S(2)}) %collective-permute-start.18) | collective-permute-done | bytes 655392 | tf_op jit(solution)/shard_map/ppermute | solution.py:23
  86.9 2.7 %collective-permute-start.21 = (bf16[128,1280]{1,0:T(8,128)(2,1)S(1)}, bf16[128,1280]{1,0:T(8,128)(2,1)S(1)}, u32[]{:S(2)}, u32[]{:S(2)}) collective-permute-start(bf16[128,1280]{1,0:T(8,128)(2,1)S(1)} %slice.75), channel_id=1, source_target_pairs={{0,6},{1,7},{2,0},{3,1},{4,2},{5,3},{6,4},{7,5},{8,14},{9,15},{10,... | collective-permute-start | bytes 983048 | tf_op jit(solution)/shard_map/ppermute | solution.py:23
  90.3 3.4 %collective-permute-done.12 = bf16[128,1280]{1,0:T(8,128)(2,1)S(1)} collective-permute-done((bf16[128,1280]{1,0:T(8,128)(2,1)S(1)}, bf16[128,1280]{1,0:T(8,128)(2,1)S(1)}, u32[]{:S(2)}, u32[]{:S(2)}) %collective-permute-start.12) | collective-permute-done | bytes 327712 | tf_op jit(solution)/shard_map/ppermute | solution.py:23
  96.3 2.7 %collective-permute-start.15 = (bf16[256,384]{1,0:T(8,128)(2,1)S(1)}, bf16[256,384]{1,0:T(8,128)(2,1)S(1)}, u32[]{:S(2)}, u32[]{:S(2)}) collective-permute-start(bf16[256,384]{1,0:T(8,128)(2,1)S(1)} %fusion.58), channel_id=1, source_target_pairs={{0,6},{1,7},{2,0},{3,1},{4,2},{5,3},{6,4},{7,5},{8,14},{9,15},{10,... | collective-permute-start | bytes 589832 | tf_op jit(solution)/shard_map/ppermute | solution.py:23
  99.0 1.8 %collective-permute-done.20 = bf16[128,1280]{1,0:T(8,128)(2,1)S(1)} collective-permute-done((bf16[128,1280]{1,0:T(8,128)(2,1)S(1)}, bf16[128,1280]{1,0:T(8,128)(2,1)S(1)}, u32[]{:S(2)}, u32[]{:S(2)}) %collective-permute-start.20) | collective-permute-done | bytes 327712 | tf_op jit(solution)/shard_map/ppermute | solution.py:23
  103.3 2.7 %collective-permute-start.23 = (bf16[256,384]{1,0:T(8,128)(2,1)S(1)}, bf16[256,384]{1,0:T(8,128)(2,1)S(1)}, u32[]{:S(2)}, u32[]{:S(2)}) collective-permute-start(bf16[256,384]{1,0:T(8,128)(2,1)S(1)} %fusion.57), channel_id=1, source_target_pairs={{0,6},{1,7},{2,0},{3,1},{4,2},{5,3},{6,4},{7,5},{8,14},{9,15},{10,... | collective-permute-start | bytes 589832 | tf_op jit(solution)/shard_map/ppermute | solution.py:23
  106.1 2.9 %collective-permute-start.17 = (bf16[128,384]{1,0:T(8,128)(2,1)S(1)}, bf16[128,384]{1,0:T(8,128)(2,1)S(1)}, u32[]{:S(2)}, u32[]{:S(2)}) collective-permute-start(bf16[128,384]{1,0:T(8,128)(2,1)S(1)} %slice.73), channel_id=1, source_target_pairs={{0,6},{1,7},{2,0},{3,1},{4,2},{5,3},{6,4},{7,5},{8,14},{9,15},{10,... | collective-permute-start | bytes 294920 | tf_op jit(solution)/shard_map/ppermute | solution.py:23
  109.2 2.7 %collective-permute-start.25 = (bf16[128,384]{1,0:T(8,128)(2,1)S(1)}, bf16[128,384]{1,0:T(8,128)(2,1)S(1)}, u32[]{:S(2)}, u32[]{:S(2)}) collective-permute-start(bf16[128,384]{1,0:T(8,128)(2,1)S(1)} %slice.79), channel_id=1, source_target_pairs={{0,6},{1,7},{2,0},{3,1},{4,2},{5,3},{6,4},{7,5},{8,14},{9,15},{10,... | collective-permute-start | bytes 294920 | tf_op jit(solution)/shard_map/ppermute | solution.py:23
  112.1 1.2 convolution_convert_fusion.1
  113.3 1.8 %collective-permute-done.24 = bf16[128,384]{1,0:T(8,128)(2,1)S(1)} collective-permute-done((bf16[128,384]{1,0:T(8,128)(2,1)S(1)}, bf16[128,384]{1,0:T(8,128)(2,1)S(1)}, u32[]{:S(2)}, u32[]{:S(2)}) %collective-permute-start.24) | collective-permute-done | bytes 98336 | tf_op jit(solution)/shard_map/ppermute | solution.py:23
  115.1 1.2 convolution_convert_fusion
  116.3 1.2 pad_maximum_fusion
  117.5 9.2 %all-to-all-start.1 = ((bf16[32,16,1280]{2,1,0:T(8,128)(2,1)}), bf16[32,16,1280]{2,1,0:T(8,128)(2,1)S(1)}, u32[]{:S(2)}, u32[]{:S(2)}) async-start(bf16[32,16,1280]{2,1,0:T(8,128)(2,1)} %bitcast.97), calls=%async_computation.1 | async-start | bytes 2621440 | tf_op jit(solution)/shard_map/all_to_all | solution.py:298
  126.8 1.1 copy-done.3
  127.9 1.1 copy-done.6
  129.0 1.5 copy-done.10
  130.5 1.5 copy-done.11
  132.1 1.5 copy-done.12
  133.6 5.4 %shard_map.96 = (bf16[256,1280]{1,0:T(8,128)(2,1)S(1)}, bf16[256,1280]{1,0:T(8,128)(2,1)S(1)}) custom-call(s32[2]{0:T(128)S(1)} %pad_add_fusion.where_ref, bf16[256,1280]{1,0:T(8,128)(2,1)S(1)} %get-tuple-element.79.refs_0_, bf16[256,1280]{1,0:T(8,128)(2,1)S(1)} %collective-permute-done.1.refs_2_.refs_1_, ...), custom_call_target="tpu_custom_call" | custom-call | tf_op jit(solution)/shard_map/pallas_call | solution.py:219
  139.1 4.5 %collective-permute-start.26 = (bf16[256,1280]{1,0:T(8,128)(2,1)S(1)}, bf16[256,1280]{1,0:T(8,128)(2,1)S(1)}, u32[]{:S(2)}, u32[]{:S(2)}) collective-permute-start(bf16[256,1280]{1,0:T(8,128)(2,1)S(1)} %get-tuple-element.88), channel_id=1, source_target_pairs={{0,1},{1,0},{2,3},{3,2},{4,5},{5,4},{6,7},{7,6},{8,9},{9,8},{10,11... | collective-permute-start | bytes 1966088 | tf_op jit(solution)/shard_map/ppermute | solution.py:14
  143.6 1.7 %collective-permute-done.26 = bf16[256,1280]{1,0:T(8,128)(2,1)S(1)} collective-permute-done((bf16[256,1280]{1,0:T(8,128)(2,1)S(1)}, bf16[256,1280]{1,0:T(8,128)(2,1)S(1)}, u32[]{:S(2)}, u32[]{:S(2)}) %collective-permute-start.26) | collective-permute-done | bytes 655392 | tf_op jit(solution)/shard_map/ppermute | solution.py:14
  145.6 3.1 %collective-permute-start.28 = (bf16[64,1280]{1,0:T(8,128)(2,1)S(1)}, bf16[64,1280]{1,0:T(8,128)(2,1)S(1)}, u32[]{:S(2)}, u32[]{:S(2)}) collective-permute-start(bf16[64,1280]{1,0:T(8,128)(2,1)S(1)} %get-tuple-element.92), channel_id=1, source_target_pairs={{0,6},{1,7},{2,0},{3,1},{4,2},{5,3},{6,4},{7,5},{8,14},{9,15},{10,... | collective-permute-start | bytes 491528 | tf_op jit(solution)/shard_map/ppermute | solution.py:23
  148.7 1.1 collective-permute-start.29
  150.1 2.8 %collective-permute-done.27.refs_1_ = bf16[64,1280]{1,0:T(8,128)(2,1)S(1)} collective-permute-done((bf16[64,1280]{1,0:T(8,128)(2,1)S(1)}, bf16[64,1280]{1,0:T(8,128)(2,1)S(1)}, u32[]{:S(2)}, u32[]{:S(2)}) %collective-permute-start.27) | collective-permute-done | bytes 163872 | tf_op jit(solution)/shard_map/ppermute | solution.py:23
  152.9 2.4 %collective-permute-done.28.refs_2_ = bf16[64,1280]{1,0:T(8,128)(2,1)S(1)} collective-permute-done((bf16[64,1280]{1,0:T(8,128)(2,1)S(1)}, bf16[64,1280]{1,0:T(8,128)(2,1)S(1)}, u32[]{:S(2)}, u32[]{:S(2)}) %collective-permute-start.28) | collective-permute-done | bytes 163872 | tf_op jit(solution)/shard_map/ppermute | solution.py:23
  155.3 2.0 %collective-permute-done.29.refs_3_ = bf16[64,1280]{1,0:T(8,128)(2,1)S(1)} collective-permute-done((bf16[64,1280]{1,0:T(8,128)(2,1)S(1)}, bf16[64,1280]{1,0:T(8,128)(2,1)S(1)}, u32[]{:S(2)}, u32[]{:S(2)}) %collective-permute-start.29) | collective-permute-done | bytes 163872 | tf_op jit(solution)/shard_map/ppermute | solution.py:23
  158.3 4.1 %collective-permute-start.30 = (f32[128,640]{1,0:T(8,128)S(1)}, f32[128,640]{1,0:T(8,128)S(1)}, u32[]{:S(2)}, u32[]{:S(2)}) collective-permute-start(f32[128,640]{1,0:T(8,128)S(1)} %get-tuple-element.90), channel_id=1, source_target_pairs={{0,1},{1,0},{2,3},{3,2},{4,5},{5,4},{6,7},{7,6},{8,9},{9,8},{10,11... | collective-permute-start | bytes 983048 | tf_op jit(solution)/shard_map/ppermute | solution.py:14
  162.4 1.3 collective-permute-done.30
  (98 shorter events, 19.9 us)
Async XLA Ops:
  0.0 4.5 %collective-permute-start = (bf16[128,640]{1,0:T(8,128)(2,1)}, bf16[128,640]{1,0:T(8,128)(2,1)S(1)}, u32[]{:S(2)}, u32[]{:S(2)}) collective-permute-start(bf16[128,640]{1,0:T(8,128)(2,1)} %tokens.1), channel_id=1, source_target_pairs={{0,1},{1,0},{2,3},{3,2},{4,5},{5,4},{6,7},{7,6},{8,9},{9,8},{10,11... | collective-permute-start | bytes 491528 | tf_op jit(solution)/shard_map/ppermute | solution.py:14
  7.0 31.9 %collective-permute-start.3 = (bf16[192,5120]{1,0:T(8,128)(2,1)}, bf16[192,5120]{1,0:T(8,128)(2,1)}, u32[]{:S(2)}, u32[]{:S(2)}) collective-permute-start(bf16[192,5120]{1,0:T(8,128)(2,1)} %bitcast.93), channel_id=1, source_target_pairs={{0,1},{1,0},{2,3},{3,2},{4,5},{5,4},{6,7},{7,6},{8,9},{9,8},{10,11... | collective-permute-start | bytes 5898248 | tf_op jit(solution)/shard_map/ppermute | solution.py:14
  7.4 31.6 %collective-permute-start.4 = (bf16[192,5120]{1,0:T(8,128)(2,1)}, bf16[192,5120]{1,0:T(8,128)(2,1)}, u32[]{:S(2)}, u32[]{:S(2)}) collective-permute-start(bf16[192,5120]{1,0:T(8,128)(2,1)} %bitcast.95), channel_id=1, source_target_pairs={{0,1},{1,0},{2,3},{3,2},{4,5},{5,4},{6,7},{7,6},{8,9},{9,8},{10,11... | collective-permute-start | bytes 5898248 | tf_op jit(solution)/shard_map/ppermute | solution.py:14
  7.5 46.3 %all-to-all-start = ((bf16[32,16,1280]{2,1,0:T(8,128)(2,1)}), bf16[32,16,1280]{2,1,0:T(8,128)(2,1)S(1)}, u32[]{:S(2)}, u32[]{:S(2)}) async-start(bf16[32,16,1280]{2,1,0:T(8,128)(2,1)} %bitcast.7), calls=%async_computation | async-start | bytes 2621440 | tf_op jit(solution)/shard_map/all_to_all | solution.py:298
  17.0 1.5 copy-start.7
  19.0 17.3 %collective-permute-start.5 = (bf16[256,1280]{1,0:T(8,128)(2,1)S(1)}, bf16[256,1280]{1,0:T(8,128)(2,1)S(1)}, u32[]{:S(2)}, u32[]{:S(2)}) collective-permute-start(bf16[256,1280]{1,0:T(8,128)(2,1)S(1)} %get-tuple-element.60), channel_id=1, source_target_pairs={{0,4},{1,5},{2,6},{3,7},{4,0},{5,1},{6,2},{7,3},{8,12},{9,13},{10,... | collective-permute-start | bytes 1966088 | tf_op jit(solution)/shard_map/ppermute | solution.py:23
  21.9 29.5 %collective-permute-start.1 = (bf16[256,1280]{1,0:T(8,128)(2,1)S(1)}, bf16[256,1280]{1,0:T(8,128)(2,1)S(1)}, u32[]{:S(2)}, u32[]{:S(2)}) collective-permute-start(bf16[256,1280]{1,0:T(8,128)(2,1)S(1)} %get-tuple-element.52), channel_id=1, source_target_pairs={{0,2},{1,3},{2,4},{3,5},{4,6},{5,7},{6,0},{7,1},{8,10},{9,11},{10,... | collective-permute-start | bytes 1966088 | tf_op jit(solution)/shard_map/ppermute | solution.py:23
  22.2 29.1 %collective-permute-start.2 = (bf16[256,1280]{1,0:T(8,128)(2,1)S(1)}, bf16[256,1280]{1,0:T(8,128)(2,1)}, u32[]{:S(2)}, u32[]{:S(2)}) collective-permute-start(bf16[256,1280]{1,0:T(8,128)(2,1)S(1)} %get-tuple-element.53), channel_id=1, source_target_pairs={{0,6},{1,7},{2,0},{3,1},{4,2},{5,3},{6,4},{7,5},{8,14},{9,15},{10,... | collective-permute-start | bytes 1966088 | tf_op jit(solution)/shard_map/ppermute | solution.py:23
  36.3 15.8 %collective-permute-start.6 = (bf16[256,1280]{1,0:T(8,128)(2,1)S(1)}, bf16[256,1280]{1,0:T(8,128)(2,1)S(1)}, u32[]{:S(2)}, u32[]{:S(2)}) collective-permute-start(bf16[256,1280]{1,0:T(8,128)(2,1)S(1)} %get-tuple-element.79.refs_0_), channel_id=1, source_target_pairs={{0,1},{1,0},{2,3},{3,2},{4,5},{5,4},{6,7},{7,6},{8,9},{9,8},{10,11... | collective-permute-start | bytes 1966088 | tf_op jit(solution)/shard_map/ppermute | solution.py:14
  38.9 14.0 %collective-permute-start.9 = (bf16[256,1280]{1,0:T(8,128)(2,1)S(1)}, bf16[256,1280]{1,0:T(8,128)(2,1)S(1)}, u32[]{:S(2)}, u32[]{:S(2)}) collective-permute-start(bf16[256,1280]{1,0:T(8,128)(2,1)S(1)} %collective-permute-done.5.refs_6_.refs_3_), channel_id=1, source_target_pairs={{0,1},{1,0},{2,3},{3,2},{4,5},{5,4},{6,7},{7,6},{8,9},{9,8},{10,11... | collective-permute-start | bytes 1966088 | tf_op jit(solution)/shard_map/ppermute | solution.py:14
  38.9 1.5 copy-start.8
  40.5 1.5 copy-start.9
  45.2 3.1 %copy-start = (bf16[4,768,1280]{2,1,0:T(8,128)(2,1)}, bf16[4,768,1280]{2,1,0:T(8,128)(2,1)S(1)}, u32[]{:S(2)}) copy-start(bf16[4,768,1280]{2,1,0:T(8,128)(2,1)S(1)} %shard_map.93) | copy-start | bytes 23592964
  51.3 3.5 %collective-permute-start.7 = (bf16[256,1280]{1,0:T(8,128)(2,1)S(1)}, bf16[256,1280]{1,0:T(8,128)(2,1)}, u32[]{:S(2)}, u32[]{:S(2)}) collective-permute-start(bf16[256,1280]{1,0:T(8,128)(2,1)S(1)} %collective-permute-done.1.refs_2_.refs_1_), channel_id=1, source_target_pairs={{0,1},{1,0},{2,3},{3,2},{4,5},{5,4},{6,7},{7,6},{8,9},{9,8},{10,11... | collective-permute-start | bytes 1966088 | tf_op jit(solution)/shard_map/ppermute | solution.py:14
  52.1 3.0 %collective-permute-start.8 = (bf16[256,1280]{1,0:T(8,128)(2,1)}, bf16[256,1280]{1,0:T(8,128)(2,1)}, u32[]{:S(2)}, u32[]{:S(2)}) collective-permute-start(bf16[256,1280]{1,0:T(8,128)(2,1)} %collective-permute-done.2.refs_4_.refs_2_), channel_id=1, source_target_pairs={{0,1},{1,0},{2,3},{3,2},{4,5},{5,4},{6,7},{7,6},{8,9},{9,8},{10,11... | collective-permute-start | bytes 1966088 | tf_op jit(solution)/shard_map/ppermute | solution.py:14
  55.1 11.3 %slice-start = ((s8[7864320]{0:T(1024)(128)(4,1)}), s8[4194304]{0:T(1024)(128)(4,1)S(1)}, s32[]{:S(2)}) async-start(s8[7864320]{0:T(1024)(128)(4,1)} %bitcast.88), calls=%async_computation.2 | async-start | bytes 8388608
  55.5 17.2 %collective-permute-start.10 = (bf16[256,1280]{1,0:T(8,128)(2,1)S(1)}, bf16[256,1280]{1,0:T(8,128)(2,1)S(1)}, u32[]{:S(2)}, u32[]{:S(2)}) collective-permute-start(bf16[256,1280]{1,0:T(8,128)(2,1)S(1)} %get-tuple-element.62), channel_id=1, source_target_pairs={{0,2},{1,3},{2,4},{3,5},{4,6},{5,7},{6,0},{7,1},{8,10},{9,11},{10,... | collective-permute-start | bytes 1966088 | tf_op jit(solution)/shard_map/ppermute | solution.py:23
  56.6 16.1 %collective-permute-start.11 = (bf16[256,1280]{1,0:T(8,128)(2,1)S(1)}, bf16[256,1280]{1,0:T(8,128)(2,1)S(1)}, u32[]{:S(2)}, u32[]{:S(2)}) collective-permute-start(bf16[256,1280]{1,0:T(8,128)(2,1)S(1)} %get-tuple-element.62), channel_id=1, source_target_pairs={{0,6},{1,7},{2,0},{3,1},{4,2},{5,3},{6,4},{7,5},{8,14},{9,15},{10,... | collective-permute-start | bytes 1966088 | tf_op jit(solution)/shard_map/ppermute | solution.py:23
  58.2 5.0 %copy-start.2 = (bf16[256,1280]{1,0:T(8,128)(2,1)S(1)}, bf16[256,1280]{1,0:T(8,128)(2,1)}, u32[]{:S(2)}) copy-start(bf16[256,1280]{1,0:T(8,128)(2,1)} %copy-done.1) | copy-start | bytes 1966084
  58.2 28.5 %collective-permute-start.18 = (bf16[256,1280]{1,0:T(8,128)(2,1)S(1)}, bf16[256,1280]{1,0:T(8,128)(2,1)S(1)}, u32[]{:S(2)}, u32[]{:S(2)}) collective-permute-start(bf16[256,1280]{1,0:T(8,128)(2,1)S(1)} %get-tuple-element.64), channel_id=1, source_target_pairs={{0,2},{1,3},{2,4},{3,5},{4,6},{5,7},{6,0},{7,1},{8,10},{9,11},{10,... | collective-permute-start | bytes 1966088 | tf_op jit(solution)/shard_map/ppermute | solution.py:23
  58.2 28.6 %collective-permute-start.19 = (bf16[256,1280]{1,0:T(8,128)(2,1)S(1)}, bf16[256,1280]{1,0:T(8,128)(2,1)S(1)}, u32[]{:S(2)}, u32[]{:S(2)}) collective-permute-start(bf16[256,1280]{1,0:T(8,128)(2,1)S(1)} %get-tuple-element.64), channel_id=1, source_target_pairs={{0,6},{1,7},{2,0},{3,1},{4,2},{5,3},{6,4},{7,5},{8,14},{9,15},{10,... | collective-permute-start | bytes 1966088 | tf_op jit(solution)/shard_map/ppermute | solution.py:23
  63.2 1.1 copy-start.5
  64.3 2.6 %slice-start.1 = ((s8[7864320]{0:T(1024)(128)(4,1)}), s8[3670016]{0:T(1024)(128)(4,1)S(1)}, s32[]{:S(2)}) async-start(s8[7864320]{0:T(1024)(128)(4,1)} %bitcast.88), calls=%async_computation.3 | async-start | bytes 7340032
  72.7 21.0 %collective-permute-start.12 = (bf16[128,1280]{1,0:T(8,128)(2,1)S(1)}, bf16[128,1280]{1,0:T(8,128)(2,1)S(1)}, u32[]{:S(2)}, u32[]{:S(2)}) collective-permute-start(bf16[128,1280]{1,0:T(8,128)(2,1)S(1)} %slice.57), channel_id=1, source_target_pairs={{0,2},{1,3},{2,4},{3,5},{4,6},{5,7},{6,0},{7,1},{8,10},{9,11},{10,... | collective-permute-start | bytes 983048 | tf_op jit(solution)/shard_map/ppermute | solution.py:23
  74.1 20.5 %collective-permute-start.13 = (bf16[128,1280]{1,0:T(8,128)(2,1)S(1)}, bf16[128,1280]{1,0:T(8,128)(2,1)S(1)}, u32[]{:S(2)}, u32[]{:S(2)}) collective-permute-start(bf16[128,1280]{1,0:T(8,128)(2,1)S(1)} %slice.59), channel_id=1, source_target_pairs={{0,6},{1,7},{2,0},{3,1},{4,2},{5,3},{6,4},{7,5},{8,14},{9,15},{10,... | collective-permute-start | bytes 983048 | tf_op jit(solution)/shard_map/ppermute | solution.py:23
  86.8 14.0 %collective-permute-start.20 = (bf16[128,1280]{1,0:T(8,128)(2,1)S(1)}, bf16[128,1280]{1,0:T(8,128)(2,1)S(1)}, u32[]{:S(2)}, u32[]{:S(2)}) collective-permute-start(bf16[128,1280]{1,0:T(8,128)(2,1)S(1)} %slice.74), channel_id=1, source_target_pairs={{0,2},{1,3},{2,4},{3,5},{4,6},{5,7},{6,0},{7,1},{8,10},{9,11},{10,... | collective-permute-start | bytes 983048 | tf_op jit(solution)/shard_map/ppermute | solution.py:23
  86.9 14.7 %collective-permute-start.21 = (bf16[128,1280]{1,0:T(8,128)(2,1)S(1)}, bf16[128,1280]{1,0:T(8,128)(2,1)S(1)}, u32[]{:S(2)}, u32[]{:S(2)}) collective-permute-start(bf16[128,1280]{1,0:T(8,128)(2,1)S(1)} %slice.75), channel_id=1, source_target_pairs={{0,6},{1,7},{2,0},{3,1},{4,2},{5,3},{6,4},{7,5},{8,14},{9,15},{10,... | collective-permute-start | bytes 983048 | tf_op jit(solution)/shard_map/ppermute | solution.py:23
  96.2 9.8 %collective-permute-start.14 = (bf16[256,384]{1,0:T(8,128)(2,1)S(1)}, bf16[256,384]{1,0:T(8,128)(2,1)S(1)}, u32[]{:S(2)}, u32[]{:S(2)}) collective-permute-start(bf16[256,384]{1,0:T(8,128)(2,1)S(1)} %fusion.58), channel_id=1, source_target_pairs={{0,2},{1,3},{2,4},{3,5},{4,6},{5,7},{6,0},{7,1},{8,10},{9,11},{10,... | collective-permute-start | bytes 589832 | tf_op jit(solution)/shard_map/ppermute | solution.py:23
  96.3 9.8 %collective-permute-start.15 = (bf16[256,384]{1,0:T(8,128)(2,1)S(1)}, bf16[256,384]{1,0:T(8,128)(2,1)S(1)}, u32[]{:S(2)}, u32[]{:S(2)}) collective-permute-start(bf16[256,384]{1,0:T(8,128)(2,1)S(1)} %fusion.58), channel_id=1, source_target_pairs={{0,6},{1,7},{2,0},{3,1},{4,2},{5,3},{6,4},{7,5},{8,14},{9,15},{10,... | collective-permute-start | bytes 589832 | tf_op jit(solution)/shard_map/ppermute | solution.py:23
  103.2 5.8 %collective-permute-start.22 = (bf16[256,384]{1,0:T(8,128)(2,1)S(1)}, bf16[256,384]{1,0:T(8,128)(2,1)S(1)}, u32[]{:S(2)}, u32[]{:S(2)}) collective-permute-start(bf16[256,384]{1,0:T(8,128)(2,1)S(1)} %fusion.57), channel_id=1, source_target_pairs={{0,2},{1,3},{2,4},{3,5},{4,6},{5,7},{6,0},{7,1},{8,10},{9,11},{10,... | collective-permute-start | bytes 589832 | tf_op jit(solution)/shard_map/ppermute | solution.py:23
  103.3 5.9 %collective-permute-start.23 = (bf16[256,384]{1,0:T(8,128)(2,1)S(1)}, bf16[256,384]{1,0:T(8,128)(2,1)S(1)}, u32[]{:S(2)}, u32[]{:S(2)}) collective-permute-start(bf16[256,384]{1,0:T(8,128)(2,1)S(1)} %fusion.57), channel_id=1, source_target_pairs={{0,6},{1,7},{2,0},{3,1},{4,2},{5,3},{6,4},{7,5},{8,14},{9,15},{10,... | collective-permute-start | bytes 589832 | tf_op jit(solution)/shard_map/ppermute | solution.py:23
  106.0 6.1 %collective-permute-start.16 = (bf16[128,384]{1,0:T(8,128)(2,1)S(1)}, bf16[128,384]{1,0:T(8,128)(2,1)S(1)}, u32[]{:S(2)}, u32[]{:S(2)}) collective-permute-start(bf16[128,384]{1,0:T(8,128)(2,1)S(1)} %slice.72), channel_id=1, source_target_pairs={{0,2},{1,3},{2,4},{3,5},{4,6},{5,7},{6,0},{7,1},{8,10},{9,11},{10,... | collective-permute-start | bytes 294920 | tf_op jit(solution)/shard_map/ppermute | solution.py:23
  106.1 6.0 %collective-permute-start.17 = (bf16[128,384]{1,0:T(8,128)(2,1)S(1)}, bf16[128,384]{1,0:T(8,128)(2,1)S(1)}, u32[]{:S(2)}, u32[]{:S(2)}) collective-permute-start(bf16[128,384]{1,0:T(8,128)(2,1)S(1)} %slice.73), channel_id=1, source_target_pairs={{0,6},{1,7},{2,0},{3,1},{4,2},{5,3},{6,4},{7,5},{8,14},{9,15},{10,... | collective-permute-start | bytes 294920 | tf_op jit(solution)/shard_map/ppermute | solution.py:23
  109.1 6.0 %collective-permute-start.24 = (bf16[128,384]{1,0:T(8,128)(2,1)S(1)}, bf16[128,384]{1,0:T(8,128)(2,1)S(1)}, u32[]{:S(2)}, u32[]{:S(2)}) collective-permute-start(bf16[128,384]{1,0:T(8,128)(2,1)S(1)} %slice.78), channel_id=1, source_target_pairs={{0,2},{1,3},{2,4},{3,5},{4,6},{5,7},{6,0},{7,1},{8,10},{9,11},{10,... | collective-permute-start | bytes 294920 | tf_op jit(solution)/shard_map/ppermute | solution.py:23
  109.2 5.9 %collective-permute-start.25 = (bf16[128,384]{1,0:T(8,128)(2,1)S(1)}, bf16[128,384]{1,0:T(8,128)(2,1)S(1)}, u32[]{:S(2)}, u32[]{:S(2)}) collective-permute-start(bf16[128,384]{1,0:T(8,128)(2,1)S(1)} %slice.79), channel_id=1, source_target_pairs={{0,6},{1,7},{2,0},{3,1},{4,2},{5,3},{6,4},{7,5},{8,14},{9,15},{10,... | collective-permute-start | bytes 294920 | tf_op jit(solution)/shard_map/ppermute | solution.py:23
  117.5 39.8 %all-to-all-start.1 = ((bf16[32,16,1280]{2,1,0:T(8,128)(2,1)}), bf16[32,16,1280]{2,1,0:T(8,128)(2,1)S(1)}, u32[]{:S(2)}, u32[]{:S(2)}) async-start(bf16[32,16,1280]{2,1,0:T(8,128)(2,1)} %bitcast.97), calls=%async_computation.1 | async-start | bytes 2621440 | tf_op jit(solution)/shard_map/all_to_all | solution.py:298
  126.8 1.1 copy-start.3
  127.9 1.1 copy-start.6
  129.0 1.5 copy-start.10
  130.5 1.5 copy-start.11
  132.1 1.5 copy-start.12
  139.0 10.8 %copy-start.14 = (s32[128,6]{0,1:T(8,128)S(1)}, s32[128,6]{0,1:T(8,128)}, u32[]{:S(2)}) copy-start(s32[128,6]{0,1:T(8,128)} %param.10) | copy-start | bytes 9220
  139.1 10.7 %copy-start.15 = (f32[128,6]{0,1:T(8,128)S(1)}, f32[128,6]{0,1:T(8,128)}, u32[]{:S(2)}) copy-start(f32[128,6]{0,1:T(8,128)} %param.11) | copy-start | bytes 9220
  139.1 6.2 %collective-permute-start.26 = (bf16[256,1280]{1,0:T(8,128)(2,1)S(1)}, bf16[256,1280]{1,0:T(8,128)(2,1)S(1)}, u32[]{:S(2)}, u32[]{:S(2)}) collective-permute-start(bf16[256,1280]{1,0:T(8,128)(2,1)S(1)} %get-tuple-element.88), channel_id=1, source_target_pairs={{0,1},{1,0},{2,3},{3,2},{4,5},{5,4},{6,7},{7,6},{8,9},{9,8},{10,11... | collective-permute-start | bytes 1966088 | tf_op jit(solution)/shard_map/ppermute | solution.py:14
  145.5 7.4 %collective-permute-start.27 = (bf16[64,1280]{1,0:T(8,128)(2,1)S(1)}, bf16[64,1280]{1,0:T(8,128)(2,1)S(1)}, u32[]{:S(2)}, u32[]{:S(2)}) collective-permute-start(bf16[64,1280]{1,0:T(8,128)(2,1)S(1)} %get-tuple-element.93), channel_id=1, source_target_pairs={{0,2},{1,3},{2,4},{3,5},{4,6},{5,7},{6,0},{7,1},{8,10},{9,11},{10,... | collective-permute-start | bytes 491528 | tf_op jit(solution)/shard_map/ppermute | solution.py:23
  145.6 9.7 %collective-permute-start.28 = (bf16[64,1280]{1,0:T(8,128)(2,1)S(1)}, bf16[64,1280]{1,0:T(8,128)(2,1)S(1)}, u32[]{:S(2)}, u32[]{:S(2)}) collective-permute-start(bf16[64,1280]{1,0:T(8,128)(2,1)S(1)} %get-tuple-element.92), channel_id=1, source_target_pairs={{0,6},{1,7},{2,0},{3,1},{4,2},{5,3},{6,4},{7,5},{8,14},{9,15},{10,... | collective-permute-start | bytes 491528 | tf_op jit(solution)/shard_map/ppermute | solution.py:23
  148.7 8.5 %collective-permute-start.29 = (bf16[64,1280]{1,0:T(8,128)(2,1)S(1)}, bf16[64,1280]{1,0:T(8,128)(2,1)S(1)}, u32[]{:S(2)}, u32[]{:S(2)}) collective-permute-start(bf16[64,1280]{1,0:T(8,128)(2,1)S(1)} %get-tuple-element.91), channel_id=1, source_target_pairs={{0,4},{1,5},{2,6},{3,7},{4,0},{5,1},{6,2},{7,3},{8,12},{9,13},{10,... | collective-permute-start | bytes 491528 | tf_op jit(solution)/shard_map/ppermute | solution.py:23
  158.3 5.3 %collective-permute-start.30 = (f32[128,640]{1,0:T(8,128)S(1)}, f32[128,640]{1,0:T(8,128)S(1)}, u32[]{:S(2)}, u32[]{:S(2)}) collective-permute-start(f32[128,640]{1,0:T(8,128)S(1)} %get-tuple-element.90), channel_id=1, source_target_pairs={{0,1},{1,0},{2,3},{3,2},{4,5},{5,4},{6,7},{7,6},{8,9},{9,8},{10,11... | collective-permute-start | bytes 983048 | tf_op jit(solution)/shard_map/ppermute | solution.py:14
  (3 other events, 2.6 us)
